TPU v7x, 32 devices: a whole 2x2x4 slice. The times are simulated.
32 devices in a mesh: dp: 8 (over y, x, core), ctx: 4 (over z).
Axes of the slice: x: 2, y: 2, z: 4, core: 2. Of those that a mesh axis runs over, the one named last changes fastest.
Arguments:
- layer_input_rows: bfloat16 [8, 512, 1536], P('dp', 'ctx'), may hold values from -6 to 6
- routes: int32 [8, 512, 8], P('dp', 'ctx'), may hold values from 0 to 19, all different within a row; in each aligned block of 128 rows (0 to 127, 128 to 255, ..., all dimensions but the last counted through in order) at most 76 rows name the same one
- prefix: int32 [8], P('dp'), may hold values from 1 to 512
- sequence_adapter_index: int32 [8], P('dp'), may hold values from 0 to 7
- attention_norm_gain: float32 [1536], replicated, may hold values from 0.1 to 1.9
- expert_norm_gain: float32 [1536], replicated, may hold values from 0.1 to 1.9
- query_weight: bfloat16 [1536, 1536], replicated, may hold values from -0.15625 to 0.15625
- key_value_weight: bfloat16 [1536, 1024], replicated, may hold values from -0.15625 to 0.15625
- projection_weight: bfloat16 [1536, 1536], replicated, may hold values from -1 to 1
- router_weight: bfloat16 [1536, 20], replicated, may hold values from -0.078125 to 0.078125
- gate_up_weight: bfloat16 [20, 1536, 1024], P('ctx'), may hold values from -0.15625 to 0.15625
- down_weight: bfloat16 [20, 512, 1536], P('ctx'), may hold values from -1 to 1
- adapter_query_key_value_input: bfloat16 [8, 1536, 48], replicated, may hold values from -0.15625 to 0.15625
- adapter_query_output: bfloat16 [8, 16, 1536], replicated, may hold values from -0.25 to 0.25
- adapter_key_value_output: bfloat16 [8, 2, 16, 512], replicated, may hold values from -0.25 to 0.25
- adapter_projection_input: bfloat16 [8, 1536, 16], replicated, may hold values from -0.15625 to 0.15625
- adapter_projection_output: bfloat16 [8, 16, 1536], replicated, may hold values from -0.25 to 0.25
- adapter_gate_up_input: bfloat16 [8, 20, 1536, 32], P(None, 'ctx'), may hold values from -0.15625 to 0.15625
- adapter_gate_up_output: bfloat16 [8, 20, 2, 16, 512], P(None, 'ctx'), may hold values from -0.25 to 0.25
- adapter_down_input: bfloat16 [8, 20, 512, 16], P(None, 'ctx'), may hold values from -0.25 to 0.25
- adapter_down_output: bfloat16 [8, 20, 16, 1536], P(None, 'ctx'), may hold values from -0.25 to 0.25
- cotangent: bfloat16 [8, 512, 1536], P('dp', 'ctx'), may hold values from -6 to 6
Outputs:
- grad_x: float32 [8, 512, 1536], P('dp', 'ctx')
- grad_qkv_a: float32 [8, 1536, 48], P(None, 'dp')
- grad_query_b: float32 [8, 16, 1536], P(None, None, 'dp')
- grad_kv_b: float32 [8, 2, 16, 512], P(None, None, None, 'dp')
- grad_out_a: float32 [8, 1536, 16], P(None, 'dp')
- grad_out_b: float32 [8, 16, 1536], P(None, None, 'dp')
- grad_gateup_a: float32 [8, 20, 1536, 32], P(None, 'ctx', 'dp')
- grad_gateup_b: float32 [8, 20, 2, 16, 512], P(None, 'ctx', None, None, 'dp')
- grad_down_a: float32 [8, 20, 512, 16], P(None, 'ctx', 'dp')
- grad_down_b: float32 [8, 20, 16, 1536], P(None, 'ctx', None, 'dp')
Inputs may be any that keep to these rules, and one draw needn't show every extreme that they name: `routes`: each token names 8 different experts. Among the 128 tokens of one device (aligned blocks of 128 positions of a sequence) no expert is named more than 76 times, and in every draw some expert is named exactly 76 times by the tokens of some device.
All inputs are finite; a program needn't handle non-finite values.
Results may differ from a plain program's by a relative error of at most 0.024.
Values may be sent and summed in bfloat16 or wider, within the bound.
No kernel may reach another device: no remote copies, remote signals or barrier semaphores. Data moves between devices by JAX's collectives and lax.ppermute only.
A program may use at most 256 MiB of HBM per device.

v0:
```python
import functools

import jax
import jax.numpy as jnp
from jax import lax
from jax.experimental import pallas as pl
from jax.experimental.pallas import tpu as pltpu
from jax.sharding import PartitionSpec as P

MODEL_WIDTH = 1536
QUERY_HEADS = 24
KEY_HEADS = 8
HEAD_SIZE = 64
EXPERT_HIDDEN = 512
TOPK = 8
ADAPTER_RANK = 16
ADAPTER_CHOICES = 8
QUERY_FEATURES = 1536
KEY_FEATURES = 512
LANES = 128
PAIRS = KEY_HEADS // 2
PAIR_QUERY = QUERY_FEATURES // PAIRS
COLUMNS = 512

EPS = 1e-05
ADAPTER_SCALE = 2.0
ROPE_BASE = 10000.0
MASKED = -1e30
SCALING = HEAD_SIZE ** (-0.5)
F32 = jnp.float32
BF16 = jnp.bfloat16
MIB = 1024 * 1024


def mm(left, right):
    return jnp.dot(left, right, preferred_element_type=F32)


def mm_nt(left, right):
    return lax.dot_general(left, right, (((1,), (1,)), ((), ())), preferred_element_type=F32)


def mm_tn(left, right):
    return lax.dot_general(left, right, (((0,), (0,)), ((), ())), preferred_element_type=F32)


def rotation(size, by):
    return [(i, (i + by) % size) for i in range(size)]


def ring_gather(block, size):
    blocks = [block]
    for _ in range(size - 1):
        blocks.append(lax.ppermute(blocks[-1], "ctx", rotation(size, 1)))
    return blocks[1:] + blocks[:1]


def low_lanes(shape):
    return lax.broadcasted_iota(jnp.int32, shape, 1) % LANES < HEAD_SIZE


def swapped(tile):
    return jnp.concatenate([tile[:, HEAD_SIZE:], tile[:, :HEAD_SIZE]], axis=1)


def turned(tile, cosine, sine):
    half = HEAD_SIZE // 2
    lane = lax.broadcasted_iota(jnp.int32, tile.shape, 1)
    other = jnp.where(
        lane % HEAD_SIZE < half, pltpu.roll(tile, LANES - half, 1), pltpu.roll(tile, half, 1)
    )
    return tile * cosine + other * sine


def placed_heads(tiles):
    return [
        tiles[0],
        swapped(tiles[0]),
        tiles[1],
        tiles[1],
        swapped(tiles[2]),
        tiles[2],
    ]


def lane_tiles(block):
    return [block[:, t * LANES : (t + 1) * LANES] for t in range(block.shape[1] // LANES)]


def call(kernel, scalars, grid, ins, outs, scratch, flops, vmem=48):
    bytes_accessed = sum(a.size * a.dtype.itemsize for a, _, _ in ins)
    return pl.pallas_call(
        kernel,
        grid_spec=pltpu.PrefetchScalarGridSpec(
            num_scalar_prefetch=1,
            grid=(grid,),
            in_specs=[pl.BlockSpec(b, m) for _, b, m in ins],
            out_specs=[pl.BlockSpec(b, m) for _, _, b, m in outs],
            scratch_shapes=scratch,
        ),
        out_shape=[jax.ShapeDtypeStruct(s, d) for s, d, _, _ in outs],
        compiler_params=pltpu.CompilerParams(
            vmem_limit_bytes=vmem * MIB, dimension_semantics=("arbitrary",)
        ),
        cost_estimate=pl.CostEstimate(
            flops=flops, bytes_accessed=bytes_accessed, transcendentals=0
        ),
    )(scalars, *[a for a, _, _ in ins])


def whole(array):
    return (array, array.shape, lambda i, s, n=array.ndim: (0,) * n)


def whole_out(shape, dtype):
    return (shape, dtype, shape, lambda i, s, n=len(shape): (0,) * n)


def chosen_whole(table):
    rest = table.shape[1:]
    return (table, (1,) + rest, lambda i, s, n=len(rest): (s[0],) + (0,) * n)


def qkv_kernel(blocks, scalars, *refs):
    xs, refs = refs[:blocks], refs[blocks:]
    gain, down, query_w, kv_w, query_out, kv_out, cosine, sine = refs[:8]
    q_ref, k_ref, v_ref, normed_ref, lora_ref = refs[8:]
    step = pl.program_id(0)
    q_steps = QUERY_FEATURES // COLUMNS

    @pl.when(step == 0)
    def _():
        rows = xs[0].shape[0]
        for b, x_ref in enumerate(xs):
            x = x_ref[...].astype(F32)
            inv = lax.rsqrt(jnp.mean(x * x, axis=-1, keepdims=True) + EPS)
            normed_ref[b * rows : (b + 1) * rows] = (x * inv * gain[...]).astype(BF16)
        lora_ref[...] = mm_nt(normed_ref[...], down[0]).astype(BF16)

    def rope_to(out_ref, pre, scale):
        cos, sin = cosine[...] * scale, sine[...] * scale
        for t, tile in enumerate(lane_tiles(pre)):
            out_ref[:, t * LANES : (t + 1) * LANES] = turned(tile, cos, sin).astype(BF16)

    r = ADAPTER_RANK

    @pl.when(step < q_steps)
    def _():
        pre = mm(normed_ref[...], query_w[...])
        pre = pre + mm(lora_ref[:, :r] * ADAPTER_SCALE, query_out[0])
        rope_to(q_ref, pre, SCALING)

    @pl.when(step == q_steps)
    def _():
        pre = mm(normed_ref[...], kv_w[...])
        pre = pre + mm(lora_ref[:, r : 2 * r] * ADAPTER_SCALE, kv_out[0, 0])
        rope_to(k_ref, pre, 1.0)

    @pl.when(step == q_steps + 1)
    def _():
        pre = mm(normed_ref[...], kv_w[...])
        v_ref[...] = (pre + mm(lora_ref[:, 2 * r :] * ADAPTER_SCALE, kv_out[0, 1])).astype(BF16)


def qkv(scalars, xs, gain, down, query_w, kv_w, query_out, kv_out, cosine, sine):
    rows = sum(x.shape[0] for x in xs)
    q_steps = QUERY_FEATURES // COLUMNS
    last = q_steps - 1
    return call(
        functools.partial(qkv_kernel, len(xs)),
        scalars,
        q_steps + 2,
        [whole(x) for x in xs]
        + [
            whole(gain),
            chosen_whole(down),
            (query_w, (MODEL_WIDTH, COLUMNS), lambda i, s: (0, jnp.minimum(i, last))),
            (kv_w, (MODEL_WIDTH, COLUMNS), lambda i, s: (0, jnp.maximum(i - q_steps, 0))),
            (query_out, (1, ADAPTER_RANK, COLUMNS), lambda i, s: (s[0], 0, jnp.minimum(i, last))),
            chosen_whole(kv_out),
            whole(cosine),
            whole(sine),
        ],
        [
            (
                (rows, QUERY_FEATURES),
                BF16,
                (rows, COLUMNS),
                lambda i, s: (0, jnp.minimum(i, last)),
            ),
            whole_out((rows, KEY_FEATURES), BF16),
            whole_out((rows, KEY_FEATURES), BF16),
            whole_out((rows, MODEL_WIDTH), BF16),
            whole_out((rows, 3 * ADAPTER_RANK), BF16),
        ],
        [],
        2 * rows * MODEL_WIDTH * (QUERY_FEATURES + 2 * KEY_FEATURES),
    )


def attend_kernel(blocks, with_own, scalars, *refs):
    xs, refs = refs[:blocks], refs[blocks:]
    q_ref, k_ref, v_ref, bias, proj_w, proj_in, proj_out, gain, router, named = refs[:10]
    outs = refs[10:]
    if with_own:
        normed_ref, gates_ref, att_ref, lora_ref, middle_ref, inv_ref, total, rank_total = outs
    else:
        normed_ref, gates_ref, total, rank_total = outs
    step = pl.program_id(0)
    own = xs[0].shape[0]

    keys, values = k_ref[...], v_ref[...]
    low = low_lanes(keys.shape)
    zero, one = jnp.zeros_like(keys), jnp.ones_like(values)
    key_of = [jnp.where(low, keys, zero), jnp.where(low, zero, keys)]
    value_of = [jnp.where(low, values, one), jnp.where(low, one, values)]
    heads = []
    for h, query in enumerate(placed_heads(lane_tiles(q_ref[...]))):
        scores = mm_nt(query, key_of[h // 3]) + bias[...]
        shifted = jnp.exp(scores - jnp.max(scores, axis=-1, keepdims=True)).astype(BF16)
        sums = mm(shifted, value_of[h // 3])
        heads.append(sums / pltpu.roll(sums, HEAD_SIZE, 1))
    low_q = low_lanes(heads[0].shape)
    attended = jnp.concatenate(
        [
            jnp.where(low_q, heads[0], pltpu.roll(heads[1], HEAD_SIZE, 1)),
            jnp.where(low_q, heads[2], heads[3]),
            jnp.where(low_q, pltpu.roll(heads[4], HEAD_SIZE, 1), heads[5]),
        ],
        axis=1,
    ).astype(BF16)
    if with_own:
        att_ref[...] = attended[-own:]
    part = mm(attended, proj_w[...])
    rank_part = mm_nt(attended, proj_in[0])

    @pl.when(step == 0)
    def _():
        total[...] = part
        rank_total[...] = rank_part

    @pl.when(step > 0)
    def _():
        total[...] += part
        rank_total[...] += rank_part

    @pl.when(step == PAIRS - 1)
    def _():
        lora_out = rank_total[...].astype(BF16)
        branch = total[...] + mm(lora_out * ADAPTER_SCALE, proj_out[0])
        for b, x_ref in enumerate(xs):
            middle = x_ref[...].astype(F32) + branch[b * own : (b + 1) * own]
            inv = lax.rsqrt(jnp.mean(middle * middle, axis=-1, keepdims=True) + EPS)
            normed_ref[b * own : (b + 1) * own] = (middle * inv * gain[...]).astype(BF16)
            if with_own and b == blocks - 1:
                middle_ref[...] = middle
                inv_ref[...] = inv
                lora_ref[...] = lora_out[b * own : (b + 1) * own]
        logits = mm_nt(normed_ref[...], router[...])
        mask = named[...] > 0.0
        chosen = jnp.where(mask, logits, MASKED)
        shifted = jnp.exp(chosen - jnp.max(chosen, axis=-1, keepdims=True))
        shifted = jnp.where(mask, shifted, 0.0)
        gates_ref[...] = shifted / jnp.sum(shifted, axis=-1, keepdims=True)


def attend(scalars, part, with_own, xs, q, k, v, bias, proj_w, proj_in, proj_out, gain, router, named):
    own = xs[0].shape[0]
    rows = own * len(xs)
    span = k.shape[0]
    experts = router.shape[0]
    outs = [
        whole_out((rows, MODEL_WIDTH), BF16),
        whole_out((rows, experts), F32),
    ]
    if with_own:
        outs += [
            ((own, QUERY_FEATURES), BF16, (own, PAIR_QUERY), lambda i, s: (0, i)),
            whole_out((own, ADAPTER_RANK), BF16),
            whole_out((own, MODEL_WIDTH), F32),
            whole_out((own, 1), F32),
        ]
    return call(
        functools.partial(attend_kernel, len(xs), with_own),
        scalars,
        PAIRS,
        [whole(x) for x in xs]
        + [
            (q, (rows, PAIR_QUERY), lambda i, s: (part, i)),
            (k, (span, LANES), lambda i, s: (0, i)),
            (v, (span, LANES), lambda i, s: (0, i)),
            (bias, (rows, span), lambda i, s: (part, 0)),
            (proj_w, (PAIR_QUERY, MODEL_WIDTH), lambda i, s: (i, 0)),
            (proj_in, (1, ADAPTER_RANK, PAIR_QUERY), lambda i, s: (s[0], 0, i)),
            chosen_whole(proj_out),
            whole(gain),
            whole(router),
            (named, (rows, experts), lambda i, s: (part, 0)),
        ],
        outs,
        [pltpu.VMEM((rows, MODEL_WIDTH), F32), pltpu.VMEM((rows, ADAPTER_RANK), F32)],
        4 * rows * span * QUERY_FEATURES + 2 * rows * MODEL_WIDTH * QUERY_FEATURES,
    )


def expert_kernel(blocks, parts, first, scalars, *refs):
    cots, refs = refs[:blocks], refs[blocks:]
    x_ref, gates, up_w, down_w, up_in, up_out, down_in, down_out = refs[:8]
    refs = refs[8:]
    if first:
        rows_ref, gg_ref, wide_ref, narrow_ref, cot_all, total, gg_all = refs
    else:
        wide_old, narrow_old, rows_ref, gg_ref, send_ref, cot_all, total, gg_all = refs
    step = pl.program_id(0)
    here = pl.num_programs(0)
    own = cots[0].shape[0]
    r = ADAPTER_RANK

    @pl.when(step == 0)
    def _():
        for b, cot in enumerate(cots):
            cot_all[b * own : (b + 1) * own] = cot[...]
        total[...] = jnp.zeros_like(total)
        gg_all[...] = jnp.zeros_like(gg_all)

    x, cot = x_ref[...], cot_all[...]
    lane = lax.broadcasted_iota(jnp.int32, gates.shape, 1)
    gate_of = jnp.sum(
        jnp.where(lane == scalars[2] * here + step, gates[...], 0.0), axis=1, keepdims=True
    )
    rank_in = mm_nt(x, up_in[0, 0]).astype(BF16)
    rank_in2 = rank_in * ADAPTER_SCALE
    gate_pre = mm(x, up_w[0, :, :EXPERT_HIDDEN]) + mm(rank_in2[:, :r], up_out[0, 0, 0])
    up_pre = mm(x, up_w[0, :, EXPERT_HIDDEN:]) + mm(rank_in2[:, r:], up_out[0, 0, 1])
    sig = 1.0 / (1.0 + jnp.exp(-gate_pre))
    silu = gate_pre * sig
    hidden = (silu * up_pre).astype(BF16)
    rank_mid = mm_nt(hidden, down_in[0, 0]).astype(BF16)
    cot_mid = ADAPTER_SCALE * mm_nt(cot, down_out[0, 0])
    cot_hidden = mm_nt(cot, down_w[0])
    gate_grad = jnp.sum(hidden.astype(F32) * cot_hidden, axis=1, keepdims=True) + jnp.sum(
        rank_mid.astype(F32) * cot_mid, axis=1, keepdims=True
    )
    gg_lane = lax.broadcasted_iota(jnp.int32, gg_all.shape, 1)
    gg_all[...] += jnp.where(gg_lane == step, gate_grad, 0.0)
    grad_rank_mid = (gate_of * cot_mid).astype(BF16)
    grad_hidden = gate_of * cot_hidden + mm(grad_rank_mid, down_in[0, 0])
    grad_up = (grad_hidden * silu).astype(BF16)
    grad_gate = (grad_hidden * up_pre * sig * (1.0 + gate_pre * (1.0 - sig))).astype(BF16)
    grad_rank_in = jnp.concatenate(
        [mm_nt(grad_gate, up_out[0, 0, 0]), mm_nt(grad_up, up_out[0, 0, 1])], axis=1
    )
    grad_rank_in = (ADAPTER_SCALE * grad_rank_in).astype(BF16)
    total[...] += (
        mm_nt(grad_gate, up_w[0, :, :EXPERT_HIDDEN])
        + mm_nt(grad_up, up_w[0, :, EXPERT_HIDDEN:])
        + mm(grad_rank_in, up_in[0, 0])
    )
    gated_mid = (ADAPTER_SCALE * gate_of * rank_mid.astype(F32)).astype(BF16)
    wide = jnp.concatenate([mm_tn(grad_rank_in, x), mm_tn(gated_mid, cot)], axis=0)
    narrow = jnp.concatenate(
        [
            mm_tn(rank_in2[:, :r], grad_gate),
            mm_tn(rank_in2[:, r:], grad_up),
            mm_tn(grad_rank_mid, hidden),
        ],
        axis=0,
    )
    if first:
        wide_ref[0] = wide
        narrow_ref[0] = narrow
    else:
        wide = (wide + wide_old[0]).astype(BF16)
        narrow = (narrow + narrow_old[0]).astype(BF16)
        at = pl.ds(pl.multiple_of(step * (3 * r), 16), 3 * r)
        w, v = MODEL_WIDTH // parts, EXPERT_HIDDEN // parts
        for p in range(parts):
            send_ref[p, at, :w] = wide[:, p * w : (p + 1) * w]
            send_ref[p, at, w:] = narrow[:, p * v : (p + 1) * v]

        @pl.when(step == 0)
        def _():
            tail = send_ref.shape[1] - here * 3 * r
            chosen = jnp.full((tail, w + v), scalars[0], jnp.int32).astype(F32).astype(BF16)
            for p in range(parts):
                send_ref[p, here * 3 * r :] = chosen

    @pl.when(step == here - 1)
    def _():
        rows_ref[...] = total[...].astype(BF16)
        gg_ref[...] = gg_all[...].T[: gg_ref.shape[0]]


def experts(scalars, parts, cots, x, gates, tables, before):
    up_w, down_w, up_in, up_out, down_in, down_out = tables
    own = cots[0].shape[0]
    rows = own * len(cots)
    here = up_w.shape[0]
    r = ADAPTER_RANK
    per_expert = lambda i, s: (i, 0, 0)
    ins = [whole(c) for c in cots] + [
        whole(x),
        whole(gates),
        (up_w, (1,) + up_w.shape[1:], per_expert),
        (down_w, (1,) + down_w.shape[1:], per_expert),
        (up_in, (1, 1) + up_in.shape[2:], lambda i, s: (s[0], i, 0, 0)),
        (up_out, (1, 1) + up_out.shape[2:], lambda i, s: (s[0], i, 0, 0, 0)),
        (down_in, (1, 1) + down_in.shape[2:], lambda i, s: (s[0], i, 0, 0)),
        (down_out, (1, 1) + down_out.shape[2:], lambda i, s: (s[0], i, 0, 0)),
    ]
    outs = [whole_out((rows, MODEL_WIDTH), BF16), whole_out((8, rows), F32)]
    if before is None:
        for width in (MODEL_WIDTH, EXPERT_HIDDEN):
            outs.append(((here, 3 * r, width), F32, (1, 3 * r, width), per_expert))
    else:
        ins += [(b, (1,) + b.shape[1:], per_expert) for b in before]
        width = (MODEL_WIDTH + EXPERT_HIDDEN) // parts
        outs.append(whole_out((parts, here * 3 * r + 16, width), BF16))
    return call(
        functools.partial(expert_kernel, len(cots), parts, before is None),
        scalars,
        here,
        ins,
        outs,
        [
            pltpu.VMEM((rows, MODEL_WIDTH), BF16),
            pltpu.VMEM((rows, MODEL_WIDTH), F32),
            pltpu.VMEM((rows, LANES), F32),
        ],
        here * 2 * rows * MODEL_WIDTH * EXPERT_HIDDEN * 5,
    )


def middle_kernel(blocks, scalars, *refs):
    parts, refs = refs[:blocks], refs[blocks:]
    gate_grads, gates, router, middle_ref, inv_ref, gain, cot = refs[:7]
    proj_w, proj_in, proj_out, q_ref, k_ref, v_ref, bias, cosine, sine = refs[7:16]
    grad_middle, branch_ref, lora_ref, gq_ref, gk_ref, gv_ref, grad_att = refs[16:]
    step = pl.program_id(0)

    @pl.when(step == 0)
    def _():
        gates_own = gates[...]
        gg = gate_grads[...]
        chosen = gates_own * (gg - jnp.sum(gates_own * gg, axis=-1, keepdims=True))
        grad = mm(chosen.astype(BF16), router[...])
        for part in parts:
            grad = grad + part[...].astype(F32)
        scaled = grad * gain[...]
        middle, inv = middle_ref[...], inv_ref[...]
        grad = (
            cot[...].astype(F32)
            + inv * scaled
            - middle * (inv * inv * inv) * jnp.mean(scaled * middle, axis=-1, keepdims=True)
        )
        grad_middle[...] = grad
        branch = grad.astype(BF16)
        branch_ref[...] = branch
        lora = (ADAPTER_SCALE * mm_nt(branch, proj_out[0])).astype(BF16)
        lora_ref[...] = lora
        attended = (mm_nt(branch, proj_w[...]) + mm(lora, proj_in[0])).astype(BF16)
        for i in range(PAIRS):
            grad_att[i] = attended[:, i * PAIR_QUERY : (i + 1) * PAIR_QUERY]

    keys, values = k_ref[...], v_ref[...]
    low = low_lanes(keys.shape)
    zero = jnp.zeros_like(keys)
    key_of = [jnp.where(low, keys, zero), jnp.where(low, zero, keys)]
    value_of = [jnp.where(low, values, zero), jnp.where(low, zero, values)]
    queries = placed_heads(lane_tiles(q_ref[...]))
    grads = placed_heads(lane_tiles(grad_att[step]))
    low_q = low_lanes(queries[0].shape)
    zero_q = jnp.zeros_like(queries[0])
    probs_all, scores_all, queries_all, grads_all = [], [], [], []
    for h in range(6):
        j = h // 3
        scores = mm_nt(key_of[j], queries[h]) + bias[...]
        shifted = jnp.exp(scores - jnp.max(scores, axis=0, keepdims=True))
        probs = shifted / jnp.sum(shifted, axis=0, keepdims=True)
        grad_probs = mm_nt(value_of[j], grads[h])
        grad_scores = probs * (grad_probs - jnp.sum(probs * grad_probs, axis=0, keepdims=True))
        probs_all.append(probs.astype(BF16))
        scores_all.append(grad_scores.astype(BF16))
        inside = low_q if j == 0 else jnp.logical_not(low_q)
        queries_all.append(jnp.where(inside, queries[h], zero_q))
        grads_all.append(jnp.where(inside, grads[h], zero_q))
    scores_six = jnp.concatenate(scores_all, axis=1)
    grad_key = mm(scores_six, jnp.concatenate(queries_all, axis=0))
    gk_ref[...] = turned(grad_key, cosine[...], -sine[...]).astype(BF16)
    gv_ref[...] = mm(
        jnp.concatenate(probs_all, axis=1), jnp.concatenate(grads_all, axis=0)
    ).astype(BF16)
    own = q_ref.shape[0]
    key_t = [key_of[0].astype(F32).T.astype(BF16), key_of[1].astype(F32).T.astype(BF16)]
    halves = [key_t[0][:HEAD_SIZE], key_t[1][HEAD_SIZE:]]
    cos, sin = cosine[-own:], -sine[-own:]
    for t in range(3):
        pair = [mm(halves[h // 3], scores_all[h]) for h in (2 * t, 2 * t + 1)]
        tile = SCALING * jnp.concatenate(pair, axis=0).T
        gq_ref[:, t * LANES : (t + 1) * LANES] = turned(tile, cos, sin).astype(BF16)


def middle_backward(
    scalars, parts, gate_grads, gates, router, middle, inv, gain, cot, proj_w, proj_in, proj_out,
    q, k, v, bias_t, cosine, sine,
):
    own = cot.shape[0]
    span = k.shape[0]
    last = span // own - 1
    experts_all = router.shape[0]
    gates_last = gates.shape[0] // own - 1
    return call(
        functools.partial(middle_kernel, len(parts)),
        scalars,
        PAIRS,
        [(a, (own, MODEL_WIDTH), lambda i, s, b=b: (b, 0)) for a, b in parts]
        + [
            whole(gate_grads),
            (gates, (own, experts_all), lambda i, s: (gates_last, 0)),
            whole(router),
            whole(middle),
            whole(inv),
            whole(gain),
            whole(cot),
            whole(proj_w),
            chosen_whole(proj_in),
            chosen_whole(proj_out),
            (q, (own, PAIR_QUERY), lambda i, s: (last, i)),
            (k, (span, LANES), lambda i, s: (0, i)),
            (v, (span, LANES), lambda i, s: (0, i)),
            whole(bias_t),
            whole(cosine),
            whole(sine),
        ],
        [
            whole_out((own, MODEL_WIDTH), F32),
            whole_out((own, MODEL_WIDTH), BF16),
            whole_out((own, ADAPTER_RANK), BF16),
            ((own, QUERY_FEATURES), BF16, (own, PAIR_QUERY), lambda i, s: (0, i)),
            ((span, KEY_FEATURES), BF16, (span, LANES), lambda i, s: (0, i)),
            ((span, KEY_FEATURES), BF16, (span, LANES), lambda i, s: (0, i)),
        ],
        [pltpu.VMEM((PAIRS, own, PAIR_QUERY), BF16)],
        10 * own * span * QUERY_FEATURES + 2 * own * MODEL_WIDTH * QUERY_FEATURES,
    )


def adapter_kernel(parts, scalars, *refs):
    gq, gk, gv, query_out, kv_out, normed, lora_in, attended, lora_out, branch, grad_lora = refs[:11]
    query_w, send_ref, first_ref = refs[11:]
    own = gq.shape[0]
    r = ADAPTER_RANK
    lora_q = (ADAPTER_SCALE * mm_nt(gq[...], query_out[0])).astype(BF16)
    lora_k = (ADAPTER_SCALE * mm_nt(gk[...], kv_out[0, 0])).astype(BF16)
    lora_v = (ADAPTER_SCALE * mm_nt(gv[...], kv_out[0, 1])).astype(BF16)
    low2 = lora_in[...] * ADAPTER_SCALE
    wide = [
        mm_tn(lora_q, normed[-own:]),
        mm_tn(lora_k, normed[...]),
        mm_tn(lora_v, normed[...]),
        mm_tn(low2[-own:, :r], gq[...]),
        mm_tn(grad_lora[...], attended[...]),
        mm_tn(lora_out[...] * ADAPTER_SCALE, branch[...]),
    ]
    narrow = [mm_tn(low2[:, r : 2 * r], gk[...]), mm_tn(low2[:, 2 * r :], gv[...])]
    w, v = MODEL_WIDTH // parts, KEY_FEATURES // parts
    for n, rows in enumerate(wide):
        rows = rows.astype(BF16)
        for p in range(parts):
            send_ref[p, n * r : (n + 1) * r, :w] = rows[:, p * w : (p + 1) * w]
    for n in range(len(wide)):
        for p in range(parts):
            if n < len(narrow):
                rows = narrow[n][:, p * v : (p + 1) * v].astype(BF16)
            else:
                rows = jnp.zeros((r, v), BF16)
            send_ref[p, n * r : (n + 1) * r, w:] = rows
    first_ref[...] = mm_nt(gq[...], query_w[...])


def adapters(scalars, parts, gq, gk, gv, query_out, kv_out, normed, lora_in, attended, lora_out,
             branch, grad_lora, query_w):
    own = gq.shape[0]
    return call(
        functools.partial(adapter_kernel, parts),
        scalars,
        1,
        [
            whole(gq),
            whole(gk),
            whole(gv),
            chosen_whole(query_out),
            chosen_whole(kv_out),
            whole(normed),
            whole(lora_in),
            whole(attended),
            whole(lora_out),
            whole(branch),
            whole(grad_lora),
            whole(query_w),
        ],
        [
            whole_out((parts, 6 * ADAPTER_RANK, (MODEL_WIDTH + KEY_FEATURES) // parts), BF16),
            whole_out((own, MODEL_WIDTH), F32),
        ],
        [],
        2 * own * MODEL_WIDTH * QUERY_FEATURES * 2,
    )


def input_kernel(blocks, scalars, *refs):
    gks, gvs, refs = refs[:blocks], refs[blocks : 2 * blocks], refs[2 * blocks :]
    gq, first, kv_w, query_out, kv_out, down, x_ref, gain, grad_middle, out_ref = refs
    grad_k, grad_v = [
        functools.reduce(lambda a, b: a + b, [g[...].astype(F32) for g in gs]).astype(BF16)
        for gs in (gks, gvs)
    ]
    lora = jnp.concatenate(
        [
            mm_nt(gq[...], query_out[0]),
            mm_nt(grad_k, kv_out[0, 0]),
            mm_nt(grad_v, kv_out[0, 1]),
        ],
        axis=1,
    )
    lora = (ADAPTER_SCALE * lora).astype(BF16)
    grad = (
        first[...]
        + mm_nt(grad_k, kv_w[:, :KEY_FEATURES])
        + mm_nt(grad_v, kv_w[:, KEY_FEATURES:])
        + mm(lora, down[0])
    )
    x = x_ref[...].astype(F32)
    inv = lax.rsqrt(jnp.mean(x * x, axis=-1, keepdims=True) + EPS)
    scaled = grad * gain[...]
    out_ref[...] = (
        grad_middle[...]
        + inv * scaled
        - x * (inv * inv * inv) * jnp.mean(scaled * x, axis=-1, keepdims=True)
    )


def input_backward(scalars, gks, gvs, gq, first, kv_w, query_out, kv_out, down, x, gain, grad_middle):
    own = x.shape[0]
    blocked = [(a, (own, KEY_FEATURES), lambda i, s, b=b: (b, 0)) for a, b in gks + gvs]
    return call(
        functools.partial(input_kernel, len(gks)),
        scalars,
        1,
        blocked
        + [
            whole(gq),
            whole(first),
            whole(kv_w),
            chosen_whole(query_out),
            chosen_whole(kv_out),
            chosen_whole(down),
            whole(x),
            whole(gain),
            whole(grad_middle),
        ],
        [whole_out((own, MODEL_WIDTH), F32)],
        [],
        4 * own * MODEL_WIDTH * KEY_FEATURES,
    )[0]


def by_adapter(received, selector):
    return jnp.einsum("as,srw->arw", selector, received.astype(F32), precision="highest")


def shards(
    layer_input_rows,
    routes,
    prefix,
    sequence_adapter_index,
    attention_norm_gain,
    expert_norm_gain,
    query_weight,
    key_value_weight,
    projection_weight,
    router_weight,
    gate_up_weight,
    down_weight,
    adapter_query_key_value_input,
    adapter_query_output,
    adapter_key_value_output,
    adapter_projection_input,
    adapter_projection_output,
    adapter_gate_up_input,
    adapter_gate_up_output,
    adapter_down_input,
    adapter_down_output,
    cotangent,
):
    ctx_size = lax.axis_size("ctx")
    dp_size = lax.axis_size("dp")
    rank = lax.axis_index("ctx")
    own = layer_input_rows.shape[1]
    span = own * ctx_size
    experts_here = gate_up_weight.shape[0]
    experts_all = experts_here * ctx_size
    half = ctx_size // 2
    scalars = jnp.stack([sequence_adapter_index[0], prefix[0], rank]).astype(jnp.int32)
    gain_attn = attention_norm_gain[None]
    gain_ffn = expert_norm_gain[None]

    order = (rank - 1 - jnp.arange(ctx_size, dtype=jnp.int32)) % ctx_size
    positions = (order[:, None] * own + jnp.arange(own, dtype=jnp.int32)[None, :]).reshape(-1)
    inputs = ring_gather(layer_input_rows[0], ctx_size)
    route_blocks = ring_gather(routes[0], ctx_size)
    cot_own, inputs[-2] = lax.optimization_barrier((cotangent[0], inputs[-2]))
    cots = ring_gather(cot_own, ctx_size)

    size = HEAD_SIZE // 2
    frequency = ROPE_BASE ** (-jnp.arange(size, dtype=F32) / size)
    angles = positions.astype(F32)[:, None] * frequency[None, :]
    cosine, sine = jnp.cos(angles), jnp.sin(angles)
    cosine = jnp.concatenate([cosine] * 4, axis=1)
    sine = jnp.concatenate([-sine, sine] * 2, axis=1)
    allowed = (positions[None, :] <= positions[:, None]) | (positions[None, :] < prefix[0])
    bias = jnp.where(allowed, 0.0, MASKED).astype(F32)
    bias_t = bias[-own:].T
    expert_ids = jnp.arange(experts_all, dtype=jnp.int32)
    routes_all = jnp.concatenate(route_blocks, axis=0)
    named = jnp.any(routes_all[:, :, None] == expert_ids[None, None, :], axis=1).astype(F32)

    qkv_in_t = adapter_query_key_value_input.transpose(0, 2, 1)
    proj_in_t = adapter_projection_input.transpose(0, 2, 1)
    router_t = router_weight.T
    q, k, v, normed, lora_in = qkv(
        scalars, inputs, gain_attn, qkv_in_t, query_weight, key_value_weight,
        adapter_query_output, adapter_key_value_output, cosine, sine,
    )
    tables = (
        gate_up_weight,
        down_weight,
        adapter_gate_up_input.transpose(0, 1, 3, 2),
        adapter_gate_up_output,
        adapter_down_input.transpose(0, 1, 3, 2),
        adapter_down_output,
    )

    def attend_half(part, with_own):
        return attend(
            scalars, part, with_own, inputs[part * half : (part + 1) * half], q, k, v, bias,
            projection_weight, proj_in_t, adapter_projection_output, gain_ffn, router_t, named,
        )

    normed_first, gates_first = attend_half(0, False)
    rows_first, gg_first, wide, narrow = experts(
        scalars, dp_size, cots[:half], normed_first, gates_first, tables, None
    )
    normed_last, gates_last, attended, lora_out, middle, inv = attend_half(1, True)
    rows_last, gg_last, send = experts(
        scalars, dp_size, cots[half:], normed_last, gates_last, tables, (wide, narrow)
    )

    def back(first, last, axis):
        got = []
        for j in range(ctx_size - 1):
            source, at = (first, j) if j < half else (last, j - half)
            block = lax.slice_in_dim(source, at * own, (at + 1) * own, axis=axis)
            got.append((lax.ppermute(block, "ctx", rotation(ctx_size, -1 - j)), 0))
        return got

    gg_blocks = [b[:experts_here] for b, _ in back(gg_first, gg_last, 1)]
    got = back(rows_first, rows_last, 0)
    got.append((rows_last, half - 1))
    gg_blocks.append(gg_last[:experts_here, -own:])
    gate_grads = jnp.concatenate(gg_blocks, axis=0)
    shift = (jnp.arange(experts_all, dtype=jnp.int32) - (rank + 1) * experts_here) % experts_all
    gate_grads = jnp.take(gate_grads, shift, axis=0).T
    expert_got = lax.all_to_all(send, "dp", 0, 0, tiled=True)

    grad_middle, branch, grad_lora, gq, gk, gv = middle_backward(
        scalars, got, gate_grads, gates_last, router_t, middle, inv, gain_ffn, cot_own,
        projection_weight, proj_in_t, adapter_projection_output, q, k, v, bias_t, cosine, sine,
    )

    def scatter(array):
        blocks = []
        for j in range(ctx_size - 1):
            block = array[j * own : (j + 1) * own]
            blocks.append((lax.ppermute(block, "ctx", rotation(ctx_size, -1 - j)), 0))
        return blocks + [(array, ctx_size - 1)]

    gks, gvs = scatter(gk), scatter(gv)
    attention_rows, first = adapters(
        scalars, dp_size, gq, gk, gv, adapter_query_output, adapter_key_value_output, normed,
        lora_in, attended, lora_out, branch, grad_lora, query_weight,
    )
    grad_inputs = input_backward(
        scalars, gks, gvs, gq, first, key_value_weight, adapter_query_output,
        adapter_key_value_output, qkv_in_t, layer_input_rows[0], gain_attn, grad_middle,
    )

    rows_count = 6 * ADAPTER_RANK // ctx_size
    pieces = attention_rows.reshape(dp_size, ctx_size, rows_count, -1)

    def piece(j):
        return lax.dynamic_index_in_dim(pieces, (rank + j) % ctx_size, 1, keepdims=False)

    choices = expert_got[:, experts_here * 3 * ADAPTER_RANK, 0].astype(F32)
    selector = (jnp.arange(ADAPTER_CHOICES, dtype=F32)[:, None] == choices[None, :]).astype(F32)
    share = piece(0).astype(F32)
    for j in range(1, ctx_size):
        share = share + lax.ppermute(piece(j), "ctx", rotation(ctx_size, j)).astype(F32)
    share = lax.all_to_all(share.astype(BF16), "dp", 0, 0, tiled=True)
    share = by_adapter(share, selector).astype(BF16)
    attention_sum = [share]
    for j in range(1, ctx_size):
        attention_sum.append(lax.ppermute(share, "ctx", rotation(ctx_size, j)))
    attention_sum = jnp.stack(attention_sum, axis=1)
    back_order = (rank - jnp.arange(ctx_size, dtype=jnp.int32)) % ctx_size
    attention_sum = jnp.take(attention_sum, back_order, axis=1)
    attention_sum = attention_sum.reshape(ADAPTER_CHOICES, 6 * ADAPTER_RANK, -1).astype(F32)
    expert_sum = by_adapter(expert_got[:, : experts_here * 3 * ADAPTER_RANK], selector)

    wide_width = MODEL_WIDTH // dp_size
    r = ADAPTER_RANK
    attn_wide, attn_narrow = attention_sum[..., :wide_width], attention_sum[..., wide_width:]
    by_expert = expert_sum.reshape(ADAPTER_CHOICES, experts_here, 3 * r, -1)
    exp_wide, exp_narrow = by_expert[..., :wide_width], by_expert[..., wide_width:]
    return (
        grad_inputs[None],
        attn_wide[:, : 3 * r].transpose(0, 2, 1),
        attn_wide[:, 3 * r : 4 * r],
        attn_narrow[:, : 2 * r].reshape(ADAPTER_CHOICES, 2, r, -1),
        attn_wide[:, 4 * r : 5 * r].transpose(0, 2, 1),
        attn_wide[:, 5 * r :],
        exp_wide[:, :, : 2 * r].transpose(0, 1, 3, 2),
        exp_narrow[:, :, : 2 * r].reshape(ADAPTER_CHOICES, experts_here, 2, r, -1),
        exp_narrow[:, :, 2 * r :].transpose(0, 1, 3, 2),
        exp_wide[:, :, 2 * r :],
    )


def solution(mesh):
    placed = (
        P("dp", "ctx", None),
        P("dp", "ctx", None),
        P("dp"),
        P("dp"),
        P(),
        P(),
        P(),
        P(),
        P(),
        P(),
        P("ctx", None, None),
        P("ctx", None, None),
        P(),
        P(),
        P(),
        P(),
        P(),
        P(None, "ctx", None, None),
        P(None, "ctx", None, None, None),
        P(None, "ctx", None, None),
        P(None, "ctx", None, None),
        P("dp", "ctx", None),
    )
    return jax.shard_map(
        shards,
        mesh=mesh,
        in_specs=placed,
        out_specs=(
            P("dp", "ctx", None),
            P(None, "dp", None),
            P(None, None, "dp"),
            P(None, None, None, "dp"),
            P(None, "dp", None),
            P(None, None, "dp"),
            P(None, "ctx", "dp", None),
            P(None, "ctx", None, None, "dp"),
            P(None, "ctx", "dp", None),
            P(None, "ctx", None, "dp"),
        ),
        check_vma=False,
    )
```

profile of v0, /device:TPU:0, one launch (start us, length us, event | category | flops | bytes accessed | tf_op | source)
XLA Modules:
  0.0 288.1 jit_solution(13698872028937571004)
XLA Ops:
  0.7 3.1 %collective-permute-start.5 = (s32[128,8]{0,1:T(8,128)}, s32[128,8]{0,1:T(8,128)S(1)}, u32[]{:S(2)}, u32[]{:S(2)}) collective-permute-start(s32[128,8]{0,1:T(8,128)} %bitcast.98), channel_id=1, source_target_pairs={{0,1},{1,2},{2,3},{3,0},{4,5},{5,6},{6,7},{7,4},{8,9},{9,10},{10,1... | collective-permute-start | bytes 12296 | tf_op jit(solution)/shard_map/ppermute | solution.py:54
  3.7 1.6 collective-permute-start
  7.2 9.2 %collective-permute-done.refs_0_ = bf16[128,1536]{1,0:T(8,128)(2,1)S(1)} collective-permute-done((bf16[128,1536]{1,0:T(8,128)(2,1)}, bf16[128,1536]{1,0:T(8,128)(2,1)S(1)}, u32[]{:S(2)}, u32[]{:S(2)}) %collective-permute-start) | collective-permute-done | bytes 393248 | tf_op jit(solution)/shard_map/ppermute | solution.py:54
  18.4 9.4 %collective-permute-done.1.refs_1_ = bf16[128,1536]{1,0:T(8,128)(2,1)S(1)} collective-permute-done((bf16[128,1536]{1,0:T(8,128)(2,1)S(1)}, bf16[128,1536]{1,0:T(8,128)(2,1)S(1)}, u32[]{:S(2)}, u32[]{:S(2)}) %collective-permute-start.1) | collective-permute-done | bytes 393248 | tf_op jit(solution)/shard_map/ppermute | solution.py:54
  29.2 9.2 %collective-permute-done.2.refs_2_.refs_0_ = bf16[128,1536]{1,0:T(8,128)(2,1)S(1)} collective-permute-done((bf16[128,1536]{1,0:T(8,128)(2,1)S(1)}, bf16[128,1536]{1,0:T(8,128)(2,1)S(1)}, u32[]{:S(2)}, u32[]{:S(2)}) %collective-permute-start.2) | collective-permute-done | bytes 393248 | tf_op jit(solution)/shard_map/ppermute | solution.py:54
  42.1 6.7 %collective-permute-done.7 = s32[128,8]{0,1:T(8,128)S(1)} collective-permute-done((s32[128,8]{0,1:T(8,128)S(1)}, s32[128,8]{0,1:T(8,128)S(1)}, u32[]{:S(2)}, u32[]{:S(2)}) %collective-permute-start.7) | collective-permute-done | bytes 4128 | tf_op jit(solution)/shard_map/ppermute | solution.py:54
  55.7 12.5 %shard_map.285 = (bf16[512,1536]{1,0:T(8,128)(2,1)}, bf16[512,512]{1,0:T(8,128)(2,1)S(1)}, bf16[512,512]{1,0:T(8,128)(2,1)S(1)}, bf16[512,1536]{1,0:T(8,128)(2,1)}, bf16[512,48]{1,0:T(8,128)(2,1)S(1)}) custom-call(s32[3]{0:T(128)S(1)} %pad_add_fusion.1.scalars, bf16[128,1536]{1,0:T(8,128)(2,1)S(1)} %copy-done.24, bf16[128,1536]{1,0:T(8,128)(2,1)S(1)} %copy-done.27, ...), custom_call_target="tpu_custom_call" | custom-call | flops 4026531840 | bytes 11802624 | tf_op jit(solution)/shard_map/pallas_call | solution.py:92
  68.9 14.6 %shard_map.288 = (bf16[256,1536]{1,0:T(8,128)(2,1)S(1)}, f32[256,20]{1,0:T(8,128)S(1)}, bf16[128,1536]{1,0:T(8,128)(2,1)S(1)}, bf16[128,16]{1,0:T(8,128)(2,1)S(1...) custom-call(s32[3]{0:T(128)S(1)} %copy-done.39, bf16[128,1536]{1,0:T(8,128)(2,1)S(1)} %copy-done.31, ...), custom_call_target="tpu_custom_call" | custom-call | flops 2013265920 | bytes 10070016 | tf_op jit(solution)/shard_map/pallas_call | solution.py:92
  84.5 14.7 %shard_map.286 = (bf16[256,1536]{1,0:T(8,128)(2,1)S(1)}, f32[256,20]{1,0:T(8,128)S(1)}) custom-call(s32[3]{0:T(128)S(1)} %copy-done.39, bf16[128,1536]{1,0:T(8,128)(2,1)S(1)} %copy-done.25, bf16[128,1536]{1,0:T(8,128)(2,1)S(1)} %copy-done.28, bf16[512,1536]{1,0:T(8,128)(2,1)} %get-tuple-element.42.refs_2_.refs_14_, ...), custom_call_target="tpu_custom_call" | custom-call | flops 2013265920 | bytes 10070016 | tf_op jit(solution)/shard_map/pallas_call | solution.py:92
  99.3 26.3 %shard_map.287 = (bf16[256,1536]{1,0:T(8,128)(2,1)S(1)}, f32[8,256]{1,0:T(8,128)S(1)}, f32[5,48,1536]{2,1,0:T(8,128)}, f32[5,48,512]{2,1,0:T(8,128)S(1)}) custom-call(s32[3]{0:T(128)S(1)} %copy-done.40, bf16[128,1536]{1,0:T(8,128)(2,1)} %collective-permute-done.3.refs_0_, bf16[128,1536]{1,0:T(8,128)(2,1)S(1)} %collective-permute-done.4.refs_1_, ...), custom_call_target="tpu_custom_call" | custom-call | flops 10066329600 | bytes 33050624 | tf_op jit(solution)/shard_map/pallas_call | solution.py:92
  126.1 3.8 %collective-permute-start.12 = (f32[8,128]{1,0:T(8,128)S(1)}, f32[8,128]{1,0:T(8,128)}, u32[]{:S(2)}, u32[]{:S(2)}) collective-permute-start(f32[8,128]{1,0:T(8,128)S(1)} %get-tuple-element.84), channel_id=1, source_target_pairs={{0,3},{1,0},{2,1},{3,2},{4,7},{5,4},{6,5},{7,6},{8,11},{9,8},{10,9... | collective-permute-start | bytes 12296 | tf_op jit(solution)/shard_map/ppermute | solution.py:764
  131.4 2.4 collective-permute-start.9
  133.8 2.9 %collective-permute-start.8 = (bf16[128,1536]{1,0:T(8,128)(2,1)}, bf16[128,1536]{1,0:T(8,128)(2,1)}, u32[]{:S(2)}, u32[]{:S(2)}) collective-permute-start(bf16[128,1536]{1,0:T(8,128)(2,1)} %get-tuple-element.74), channel_id=1, source_target_pairs={{0,3},{1,0},{2,1},{3,2},{4,7},{5,4},{6,5},{7,6},{8,11},{9,8},{10,9... | collective-permute-start | bytes 1179656 | tf_op jit(solution)/shard_map/ppermute | solution.py:764
  136.7 7.1 %collective-permute-done.10.refs_0_ = bf16[128,1536]{1,0:T(8,128)(2,1)S(1)} collective-permute-done((bf16[128,1536]{1,0:T(8,128)(2,1)S(1)}, bf16[128,1536]{1,0:T(8,128)(2,1)S(1)}, u32[]{:S(2)}, u32[]{:S(2)}) %collective-permute-start.10) | collective-permute-done | bytes 393248 | tf_op jit(solution)/shard_map/ppermute | solution.py:54
  143.8 23.9 %shard_map.289 = (bf16[256,1536]{1,0:T(8,128)(2,1)S(1)}, f32[8,256]{1,0:T(8,128)S(1)}, bf16[8,256,256]{2,1,0:T(8,128)(2,1)S(1)}) custom-call(s32[3]{0:T(128)S(1)} %copy-done.40, bf16[128,1536]{1,0:T(8,128)(2,1)S(1)} %collective-permute-done.10.refs_0_, bf16[128,1536]{1,0:T(8,128)(2,1)S(1)} %bitcast.78, bf16[256,1536]{1,0:T(8,128)(2,1)S(1)} %get-tuple-element.48.refs_2_, ...), custom_call_target="tpu_custom_call" | custom-call | flops 10066329600 | bytes 35016704 | tf_op jit(solution)/shard_map/pallas_call | solution.py:92
  169.9 13.6 %collective-permute-start.14 = (f32[8,128]{1,0:T(8,128)}, f32[8,128]{1,0:T(8,128)}, u32[]{:S(2)}, u32[]{:S(2)}) collective-permute-start(f32[8,128]{1,0:T(8,128)} %slice.104), channel_id=1, source_target_pairs={{0,1},{1,2},{2,3},{3,0},{4,5},{5,6},{6,7},{7,4},{8,9},{9,10},{10,1... | collective-permute-start | bytes 12296 | tf_op jit(solution)/shard_map/ppermute | solution.py:764
  184.3 2.5 collective-permute-start.11
  191.1 4.5 %all-to-all-start = ((bf16[8,256,256]{2,1,0:T(8,128)(2,1)}), bf16[8,256,256]{2,1,0:T(8,128)(2,1)}, u32[]{:S(2)}, u32[]{:S(2)}) async-start(bf16[8,256,256]{2,1,0:T(8,128)(2,1)} %copy-done.13), calls=%async_computation | async-start | bytes 2097152 | tf_op jit(solution)/shard_map/all_to_all | solution.py:774
  196.9 2.0 gather_fusion
  204.8 15.1 %shard_map.290 = (f32[128,1536]{1,0:T(8,128)}, bf16[128,1536]{1,0:T(8,128)(2,1)S(1)}, bf16[128,16]{1,0:T(8,128)(2,1)S(1)}, bf16[128,1536]{1,0:T(8,128)(2,1)S(1)}...) custom-call(s32[3]{0:T(128)S(1)} %copy-done.41, bf16[128,1536]{1,0:T(8,128)(2,1)} %collective-permute-done.8.refs_0_, ...), custom_call_target="tpu_custom_call" | custom-call | flops 1610612736 | bytes 12157440 | tf_op jit(solution)/shard_map/pallas_call | solution.py:92
  219.9 5.7 %shard_map.291 = (bf16[8,96,256]{2,1,0:T(8,128)(2,1)S(1)}, f32[128,1536]{1,0:T(8,128)S(1)}) custom-call(s32[3]{0:T(128)S(1)} %copy-done.42, bf16[128,1536]{1,0:T(8,128)(2,1)S(1)} %get-tuple-element.59.refs_0_.refs_8_, bf16[512,512]{1,0:T(8,128)(2,1)S(1)} %get-tuple-element.57.refs_1_.refs_3_, bf16[512,512]{1,0:T(8,128)(2,1)S(1)} %get-tuple-element.58.refs_2_.refs_7_, ...), custom_call_target="tpu_custom_call" | custom-call | flops 1207959552 | bytes 9232384 | tf_op jit(solution)/shard_map/pallas_call | solution.py:92
  225.8 3.8 %collective-permute-start.23 = (bf16[8,24,256]{2,1,0:T(8,128)(2,1)S(1)}, bf16[8,24,256]{2,1,0:T(8,128)(2,1)S(1)}, u32[]{:S(2)}, u32[]{:S(2)}) collective-permute-start(bf16[8,24,256]{2,1,0:T(8,128)(2,1)S(1)} %get-tuple-element.82), channel_id=1, source_target_pairs={{0,3},{1,0},{2,1},{3,2},{4,7},{5,4},{6,5},{7,6},{8,11},{9,8},{10,9... | collective-permute-start | bytes 294920 | tf_op jit(solution)/shard_map/ppermute | solution.py:808
  230.2 2.4 collective-permute-start.16
  233.2 2.4 collective-permute-start.15
  235.6 8.2 %collective-permute-done.22 = bf16[8,24,256]{2,1,0:T(8,128)(2,1)S(1)} collective-permute-done((bf16[8,24,256]{2,1,0:T(8,128)(2,1)S(1)}, bf16[8,24,256]{2,1,0:T(8,128)(2,1)S(1)}, u32[]{:S(2)}, u32[]{:S(2)}) %collective-permute-start.22) | collective-permute-done | bytes 98336 | tf_op jit(solution)/shard_map/ppermute | solution.py:808
  244.6 7.6 %collective-permute-done.16.refs_1_ = bf16[128,512]{1,0:T(8,128)(2,1)S(1)} collective-permute-done((bf16[128,512]{1,0:T(8,128)(2,1)S(1)}, bf16[128,512]{1,0:T(8,128)(2,1)S(1)}, u32[]{:S(2)}, u32[]{:S(2)}) %collective-permute-start.16) | collective-permute-done | bytes 131104 | tf_op jit(solution)/shard_map/ppermute | solution.py:785
  252.2 5.6 %collective-permute-done.19.refs_5_ = bf16[128,512]{1,0:T(8,128)(2,1)S(1)} collective-permute-done((bf16[128,512]{1,0:T(8,128)(2,1)S(1)}, bf16[128,512]{1,0:T(8,128)(2,1)S(1)}, u32[]{:S(2)}, u32[]{:S(2)}) %collective-permute-start.19) | collective-permute-done | bytes 131104 | tf_op jit(solution)/shard_map/ppermute | solution.py:785
  257.9 5.0 %shard_map.292 = f32[128,1536]{1,0:T(8,128)} custom-call(s32[3]{0:T(128)S(1)} %copy-done.42, bf16[128,512]{1,0:T(8,128)(2,1)S(1)} %collective-permute-done.15.refs_0_, bf16[128,512]{1,0:T(8,128)(2,1)S(1)} %collective-permute-done.16.refs_1_, bf16[128,512]{1,0:T(8,128)(2,1)S(1)} %collective-permute-done.17.refs_2_, ...), custom_call_target="tpu_custom_call" | custom-call | flops 402653184 | bytes 9181184 | tf_op jit(solution)/shard_map/pallas_call | solution.py:92
  262.9 3.9 %all-to-all-start.1 = ((bf16[8,24,256]{2,1,0:T(8,128)(2,1)}), bf16[8,24,256]{2,1,0:T(8,128)(2,1)S(1)}, u32[]{:S(2)}, u32[]{:S(2)}) async-start(bf16[8,24,256]{2,1,0:T(8,128)(2,1)} %fusion.6), calls=%async_computation.1 | async-start | bytes 196608 | tf_op jit(solution)/shard_map/all_to_all | solution.py:809
  267.7 4.3 %all-to-all-done.1 = bf16[8,24,256]{2,1,0:T(8,128)(2,1)S(1)} async-done(((bf16[8,24,256]{2,1,0:T(8,128)(2,1)}), bf16[8,24,256]{2,1,0:T(8,128)(2,1)S(1)}, u32[]{:S(2)}, u32[]{:S(2)}) %all-to-all-start.1) | async-done | bytes 98336 | tf_op jit(solution)/shard_map/all_to_all | solution.py:809
  272.2 3.8 %collective-permute-start.26 = (bf16[8,24,256]{2,0,1:T(8,128)(2,1)S(1)}, bf16[8,24,256]{2,0,1:T(8,128)(2,1)S(1)}, u32[]{:S(2)}, u32[]{:S(2)}) collective-permute-start(bf16[8,24,256]{2,0,1:T(8,128)(2,1)S(1)} %convolution_convert_fusion), channel_id=1, source_target_pairs={{0,3},{1,0},{2,1},{3,2},{4,7},{5,4},{6,5},{7,6},{8,11},{9,8},{10,9... | collective-permute-start | bytes 294920 | tf_op jit(solution)/shard_map/ppermute | solution.py:813
  283.2 1.7 collective-permute-done.25
  (191 shorter events, 45.9 us)
Async XLA Ops:
  0.6 38.5 %copy-start.18 = (bf16[1,128,1536]{2,1,0:T(8,128)(2,1)S(1)}, bf16[1,128,1536]{2,1,0:T(8,128)(2,1)}, u32[]{:S(2)}) copy-start(bf16[1,128,1536]{2,1,0:T(8,128)(2,1)} %param.43) | copy-start | bytes 1179652
  0.7 28.6 %collective-permute-start.5 = (s32[128,8]{0,1:T(8,128)}, s32[128,8]{0,1:T(8,128)S(1)}, u32[]{:S(2)}, u32[]{:S(2)}) collective-permute-start(s32[128,8]{0,1:T(8,128)} %bitcast.98), channel_id=1, source_target_pairs={{0,1},{1,2},{2,3},{3,0},{4,5},{5,6},{6,7},{7,4},{8,9},{9,10},{10,1... | collective-permute-start | bytes 12296 | tf_op jit(solution)/shard_map/ppermute | solution.py:54
  3.7 12.6 %collective-permute-start = (bf16[128,1536]{1,0:T(8,128)(2,1)}, bf16[128,1536]{1,0:T(8,128)(2,1)S(1)}, u32[]{:S(2)}, u32[]{:S(2)}) collective-permute-start(bf16[128,1536]{1,0:T(8,128)(2,1)} %bitcast.68), channel_id=1, source_target_pairs={{0,1},{1,2},{2,3},{3,0},{4,5},{5,6},{6,7},{7,4},{8,9},{9,10},{10,1... | collective-permute-start | bytes 1179656 | tf_op jit(solution)/shard_map/ppermute | solution.py:54
  16.3 11.5 %collective-permute-start.1 = (bf16[128,1536]{1,0:T(8,128)(2,1)S(1)}, bf16[128,1536]{1,0:T(8,128)(2,1)S(1)}, u32[]{:S(2)}, u32[]{:S(2)}) collective-permute-start(bf16[128,1536]{1,0:T(8,128)(2,1)S(1)} %collective-permute-done.refs_0_), channel_id=1, source_target_pairs={{0,1},{1,2},{2,3},{3,0},{4,5},{5,6},{6,7},{7,4},{8,9},{9,10},{10,1... | collective-permute-start | bytes 1179656 | tf_op jit(solution)/shard_map/ppermute | solution.py:54
  27.8 10.6 %collective-permute-start.2 = (bf16[128,1536]{1,0:T(8,128)(2,1)S(1)}, bf16[128,1536]{1,0:T(8,128)(2,1)S(1)}, u32[]{:S(2)}, u32[]{:S(2)}) collective-permute-start(bf16[128,1536]{1,0:T(8,128)(2,1)S(1)} %collective-permute-done.1.refs_1_), channel_id=1, source_target_pairs={{0,1},{1,2},{2,3},{3,0},{4,5},{5,6},{6,7},{7,4},{8,9},{9,10},{10,1... | collective-permute-start | bytes 1179656 | tf_op jit(solution)/shard_map/ppermute | solution.py:54
  29.2 11.1 %collective-permute-start.6 = (s32[128,8]{0,1:T(8,128)S(1)}, s32[128,8]{0,1:T(8,128)S(1)}, u32[]{:S(2)}, u32[]{:S(2)}) collective-permute-start(s32[128,8]{0,1:T(8,128)S(1)} %collective-permute-done.5), channel_id=1, source_target_pairs={{0,1},{1,2},{2,3},{3,0},{4,5},{5,6},{6,7},{7,4},{8,9},{9,10},{10,1... | collective-permute-start | bytes 12296 | tf_op jit(solution)/shard_map/ppermute | solution.py:54
  39.1 10.1 %collective-permute-start.3 = (bf16[128,1536]{1,0:T(8,128)(2,1)S(1)}, bf16[128,1536]{1,0:T(8,128)(2,1)}, u32[]{:S(2)}, u32[]{:S(2)}) collective-permute-start(bf16[128,1536]{1,0:T(8,128)(2,1)S(1)} %bitcast.77), channel_id=1, source_target_pairs={{0,1},{1,2},{2,3},{3,0},{4,5},{5,6},{6,7},{7,4},{8,9},{9,10},{10,1... | collective-permute-start | bytes 1179656 | tf_op jit(solution)/shard_map/ppermute | solution.py:54
  40.3 8.5 %collective-permute-start.7 = (s32[128,8]{0,1:T(8,128)S(1)}, s32[128,8]{0,1:T(8,128)S(1)}, u32[]{:S(2)}, u32[]{:S(2)}) collective-permute-start(s32[128,8]{0,1:T(8,128)S(1)} %collective-permute-done.6), channel_id=1, source_target_pairs={{0,1},{1,2},{2,3},{3,0},{4,5},{5,6},{6,7},{7,4},{8,9},{9,10},{10,1... | collective-permute-start | bytes 12296 | tf_op jit(solution)/shard_map/ppermute | solution.py:54
  49.2 50.0 %collective-permute-start.4 = (bf16[128,1536]{1,0:T(8,128)(2,1)}, bf16[128,1536]{1,0:T(8,128)(2,1)S(1)}, u32[]{:S(2)}, u32[]{:S(2)}) collective-permute-start(bf16[128,1536]{1,0:T(8,128)(2,1)} %collective-permute-done.3.refs_0_), channel_id=1, source_target_pairs={{0,1},{1,2},{2,3},{3,0},{4,5},{5,6},{6,7},{7,4},{8,9},{9,10},{10,1... | collective-permute-start | bytes 1179656 | tf_op jit(solution)/shard_map/ppermute | solution.py:54
  84.4 59.4 %copy-start.32 = (f32[256,20]{1,0:T(8,128)}, f32[256,20]{1,0:T(8,128)S(1)}, u32[]{:S(2)}) copy-start(f32[256,20]{1,0:T(8,128)S(1)} %get-tuple-element.49.refs_3_.refs_5_) | copy-start | bytes 61444
  99.3 44.6 %copy-start.19 = (bf16[1,128,1536]{2,1,0:T(8,128)(2,1)S(1)}, bf16[1,128,1536]{2,1,0:T(8,128)(2,1)}, u32[]{:S(2)}) copy-start(bf16[1,128,1536]{2,1,0:T(8,128)(2,1)} %param.43) | copy-start | bytes 1179652
  126.1 58.1 %collective-permute-start.12 = (f32[8,128]{1,0:T(8,128)S(1)}, f32[8,128]{1,0:T(8,128)}, u32[]{:S(2)}, u32[]{:S(2)}) collective-permute-start(f32[8,128]{1,0:T(8,128)S(1)} %get-tuple-element.84), channel_id=1, source_target_pairs={{0,3},{1,0},{2,1},{3,2},{4,7},{5,4},{6,5},{7,6},{8,11},{9,8},{10,9... | collective-permute-start | bytes 12296 | tf_op jit(solution)/shard_map/ppermute | solution.py:764
  129.9 65.7 %collective-permute-start.13 = (f32[8,128]{1,0:T(8,128)}, f32[8,128]{1,0:T(8,128)}, u32[]{:S(2)}, u32[]{:S(2)}) collective-permute-start(f32[8,128]{1,0:T(8,128)} %get-tuple-element.85), channel_id=1, source_target_pairs={{0,2},{1,3},{2,0},{3,1},{4,6},{5,7},{6,4},{7,5},{8,10},{9,11},{10,... | collective-permute-start | bytes 12296 | tf_op jit(solution)/shard_map/ppermute | solution.py:764
  129.9 13.9 %collective-permute-start.10 = (bf16[128,1536]{1,0:T(8,128)(2,1)S(1)}, bf16[128,1536]{1,0:T(8,128)(2,1)S(1)}, u32[]{:S(2)}, u32[]{:S(2)}) collective-permute-start(bf16[128,1536]{1,0:T(8,128)(2,1)S(1)} %collective-permute-done.4.refs_1_), channel_id=1, source_target_pairs={{0,1},{1,2},{2,3},{3,0},{4,5},{5,6},{6,7},{7,4},{8,9},{9,10},{10,1... | collective-permute-start | bytes 1179656 | tf_op jit(solution)/shard_map/ppermute | solution.py:54
  131.4 69.8 %collective-permute-start.9 = (bf16[128,1536]{1,0:T(8,128)(2,1)}, bf16[128,1536]{1,0:T(8,128)(2,1)}, u32[]{:S(2)}, u32[]{:S(2)}) collective-permute-start(bf16[128,1536]{1,0:T(8,128)(2,1)} %get-tuple-element.73), channel_id=1, source_target_pairs={{0,2},{1,3},{2,0},{3,1},{4,6},{5,7},{6,4},{7,5},{8,10},{9,11},{10,... | collective-permute-start | bytes 1179656 | tf_op jit(solution)/shard_map/ppermute | solution.py:764
  133.8 67.4 %collective-permute-start.8 = (bf16[128,1536]{1,0:T(8,128)(2,1)}, bf16[128,1536]{1,0:T(8,128)(2,1)}, u32[]{:S(2)}, u32[]{:S(2)}) collective-permute-start(bf16[128,1536]{1,0:T(8,128)(2,1)} %get-tuple-element.74), channel_id=1, source_target_pairs={{0,3},{1,0},{2,1},{3,2},{4,7},{5,4},{6,5},{7,6},{8,11},{9,8},{10,9... | collective-permute-start | bytes 1179656 | tf_op jit(solution)/shard_map/ppermute | solution.py:764
  169.9 25.7 %collective-permute-start.14 = (f32[8,128]{1,0:T(8,128)}, f32[8,128]{1,0:T(8,128)}, u32[]{:S(2)}, u32[]{:S(2)}) collective-permute-start(f32[8,128]{1,0:T(8,128)} %slice.104), channel_id=1, source_target_pairs={{0,1},{1,2},{2,3},{3,0},{4,5},{5,6},{6,7},{7,4},{8,9},{9,10},{10,1... | collective-permute-start | bytes 12296 | tf_op jit(solution)/shard_map/ppermute | solution.py:764
  184.3 17.0 %collective-permute-start.11 = (bf16[128,1536]{1,0:T(8,128)(2,1)}, bf16[128,1536]{1,0:T(8,128)(2,1)}, u32[]{:S(2)}, u32[]{:S(2)}) collective-permute-start(bf16[128,1536]{1,0:T(8,128)(2,1)} %slice.99), channel_id=1, source_target_pairs={{0,1},{1,2},{2,3},{3,0},{4,5},{5,6},{6,7},{7,4},{8,9},{9,10},{10,1... | collective-permute-start | bytes 1179656 | tf_op jit(solution)/shard_map/ppermute | solution.py:764
  191.1 71.8 %all-to-all-start = ((bf16[8,256,256]{2,1,0:T(8,128)(2,1)}), bf16[8,256,256]{2,1,0:T(8,128)(2,1)}, u32[]{:S(2)}, u32[]{:S(2)}) async-start(bf16[8,256,256]{2,1,0:T(8,128)(2,1)} %copy-done.13), calls=%async_computation | async-start | bytes 2097152 | tf_op jit(solution)/shard_map/all_to_all | solution.py:774
  225.7 7.5 %collective-permute-start.21 = (bf16[8,24,256]{2,1,0:T(8,128)(2,1)S(1)}, bf16[8,24,256]{2,1,0:T(8,128)(2,1)S(1)}, u32[]{:S(2)}, u32[]{:S(2)}) collective-permute-start(bf16[8,24,256]{2,1,0:T(8,128)(2,1)S(1)} %get-tuple-element.81), channel_id=1, source_target_pairs={{0,1},{1,2},{2,3},{3,0},{4,5},{5,6},{6,7},{7,4},{8,9},{9,10},{10,1... | collective-permute-start | bytes 294920 | tf_op jit(solution)/shard_map/ppermute | solution.py:808
  225.8 9.8 %collective-permute-start.23 = (bf16[8,24,256]{2,1,0:T(8,128)(2,1)S(1)}, bf16[8,24,256]{2,1,0:T(8,128)(2,1)S(1)}, u32[]{:S(2)}, u32[]{:S(2)}) collective-permute-start(bf16[8,24,256]{2,1,0:T(8,128)(2,1)S(1)} %get-tuple-element.82), channel_id=1, source_target_pairs={{0,3},{1,0},{2,1},{3,2},{4,7},{5,4},{6,5},{7,6},{8,11},{9,8},{10,9... | collective-permute-start | bytes 294920 | tf_op jit(solution)/shard_map/ppermute | solution.py:808
  229.6 14.3 %collective-permute-start.22 = (bf16[8,24,256]{2,1,0:T(8,128)(2,1)S(1)}, bf16[8,24,256]{2,1,0:T(8,128)(2,1)S(1)}, u32[]{:S(2)}, u32[]{:S(2)}) collective-permute-start(bf16[8,24,256]{2,1,0:T(8,128)(2,1)S(1)} %get-tuple-element.83), channel_id=1, source_target_pairs={{0,2},{1,3},{2,0},{3,1},{4,6},{5,7},{6,4},{7,5},{8,10},{9,11},{10,... | collective-permute-start | bytes 294920 | tf_op jit(solution)/shard_map/ppermute | solution.py:808
  229.6 14.2 %collective-permute-start.17 = (bf16[128,512]{1,0:T(8,128)(2,1)S(1)}, bf16[128,512]{1,0:T(8,128)(2,1)S(1)}, u32[]{:S(2)}, u32[]{:S(2)}) collective-permute-start(bf16[128,512]{1,0:T(8,128)(2,1)S(1)} %get-tuple-element.78), channel_id=1, source_target_pairs={{0,1},{1,2},{2,3},{3,0},{4,5},{5,6},{6,7},{7,4},{8,9},{9,10},{10,1... | collective-permute-start | bytes 393224 | tf_op jit(solution)/shard_map/ppermute | solution.py:785
  230.2 22.0 %collective-permute-start.16 = (bf16[128,512]{1,0:T(8,128)(2,1)S(1)}, bf16[128,512]{1,0:T(8,128)(2,1)S(1)}, u32[]{:S(2)}, u32[]{:S(2)}) collective-permute-start(bf16[128,512]{1,0:T(8,128)(2,1)S(1)} %get-tuple-element.79), channel_id=1, source_target_pairs={{0,2},{1,3},{2,0},{3,1},{4,6},{5,7},{6,4},{7,5},{8,10},{9,11},{10,... | collective-permute-start | bytes 393224 | tf_op jit(solution)/shard_map/ppermute | solution.py:785
  233.2 19.0 %collective-permute-start.15 = (bf16[128,512]{1,0:T(8,128)(2,1)S(1)}, bf16[128,512]{1,0:T(8,128)(2,1)S(1)}, u32[]{:S(2)}, u32[]{:S(2)}) collective-permute-start(bf16[128,512]{1,0:T(8,128)(2,1)S(1)} %get-tuple-element.80), channel_id=1, source_target_pairs={{0,3},{1,0},{2,1},{3,2},{4,7},{5,4},{6,5},{7,6},{8,11},{9,8},{10,9... | collective-permute-start | bytes 393224 | tf_op jit(solution)/shard_map/ppermute | solution.py:785
  235.6 16.6 %collective-permute-start.20 = (bf16[128,512]{1,0:T(8,128)(2,1)S(1)}, bf16[128,512]{1,0:T(8,128)(2,1)S(1)}, u32[]{:S(2)}, u32[]{:S(2)}) collective-permute-start(bf16[128,512]{1,0:T(8,128)(2,1)S(1)} %get-tuple-element.75), channel_id=1, source_target_pairs={{0,1},{1,2},{2,3},{3,0},{4,5},{5,6},{6,7},{7,4},{8,9},{9,10},{10,1... | collective-permute-start | bytes 393224 | tf_op jit(solution)/shard_map/ppermute | solution.py:785
  243.8 14.0 %collective-permute-start.19 = (bf16[128,512]{1,0:T(8,128)(2,1)S(1)}, bf16[128,512]{1,0:T(8,128)(2,1)S(1)}, u32[]{:S(2)}, u32[]{:S(2)}) collective-permute-start(bf16[128,512]{1,0:T(8,128)(2,1)S(1)} %get-tuple-element.76), channel_id=1, source_target_pairs={{0,2},{1,3},{2,0},{3,1},{4,6},{5,7},{6,4},{7,5},{8,10},{9,11},{10,... | collective-permute-start | bytes 393224 | tf_op jit(solution)/shard_map/ppermute | solution.py:785
  243.8 14.0 %collective-permute-start.18 = (bf16[128,512]{1,0:T(8,128)(2,1)S(1)}, bf16[128,512]{1,0:T(8,128)(2,1)S(1)}, u32[]{:S(2)}, u32[]{:S(2)}) collective-permute-start(bf16[128,512]{1,0:T(8,128)(2,1)S(1)} %get-tuple-element.77), channel_id=1, source_target_pairs={{0,3},{1,0},{2,1},{3,2},{4,7},{5,4},{6,5},{7,6},{8,11},{9,8},{10,9... | collective-permute-start | bytes 393224 | tf_op jit(solution)/shard_map/ppermute | solution.py:785
  262.9 9.1 %all-to-all-start.1 = ((bf16[8,24,256]{2,1,0:T(8,128)(2,1)}), bf16[8,24,256]{2,1,0:T(8,128)(2,1)S(1)}, u32[]{:S(2)}, u32[]{:S(2)}) async-start(bf16[8,24,256]{2,1,0:T(8,128)(2,1)} %fusion.6), calls=%async_computation.1 | async-start | bytes 196608 | tf_op jit(solution)/shard_map/all_to_all | solution.py:809
  272.2 11.0 %collective-permute-start.26 = (bf16[8,24,256]{2,0,1:T(8,128)(2,1)S(1)}, bf16[8,24,256]{2,0,1:T(8,128)(2,1)S(1)}, u32[]{:S(2)}, u32[]{:S(2)}) collective-permute-start(bf16[8,24,256]{2,0,1:T(8,128)(2,1)S(1)} %convolution_convert_fusion), channel_id=1, source_target_pairs={{0,3},{1,0},{2,1},{3,2},{4,7},{5,4},{6,5},{7,6},{8,11},{9,8},{10,9... | collective-permute-start | bytes 294920 | tf_op jit(solution)/shard_map/ppermute | solution.py:813
  276.0 8.9 %collective-permute-start.25 = (bf16[8,24,256]{2,0,1:T(8,128)(2,1)S(1)}, bf16[8,24,256]{2,0,1:T(8,128)(2,1)S(1)}, u32[]{:S(2)}, u32[]{:S(2)}) collective-permute-start(bf16[8,24,256]{2,0,1:T(8,128)(2,1)S(1)} %convolution_convert_fusion), channel_id=1, source_target_pairs={{0,2},{1,3},{2,0},{3,1},{4,6},{5,7},{6,4},{7,5},{8,10},{9,11},{10,... | collective-permute-start | bytes 294920 | tf_op jit(solution)/shard_map/ppermute | solution.py:813
  276.0 8.9 %collective-permute-start.24 = (bf16[8,24,256]{2,0,1:T(8,128)(2,1)S(1)}, bf16[8,24,256]{2,0,1:T(8,128)(2,1)S(1)}, u32[]{:S(2)}, u32[]{:S(2)}) collective-permute-start(bf16[8,24,256]{2,0,1:T(8,128)(2,1)S(1)} %convolution_convert_fusion), channel_id=1, source_target_pairs={{0,1},{1,2},{2,3},{3,0},{4,5},{5,6},{6,7},{7,4},{8,9},{9,10},{10,1... | collective-permute-start | bytes 294920 | tf_op jit(solution)/shard_map/ppermute | solution.py:813
  (48 other events, 689.2 us)
where the time goes:
time: 289 us; the launch traced here: 288 us
  Pallas kernels  118 us (41%)
  waiting for transfers between devices  69.6 us (24%)
  starting transfers between devices  52.9 us (18%)
  local copies, waits for them, and re-layouts  35.5 us (12%)
  other arithmetic  9.05 us (3%)
    pallas_call x8, Pallas kernels, call(): pl.pallas_call(kernel, grid_spec=pltpu.PrefetchScalarGridSpec(num_scalar_...  118 us
    ppermute x9, waiting for transfers between devices, ring_gather(): blocks.append(lax.ppermute(blocks[-1], 'ctx', rotation(size, 1)))  41.6 us
    ppermute x6, starting transfers between devices, back(): got.append((lax.ppermute(block, 'ctx', rotation(ctx_size, -1 - j)), 0))  25.1 us
    unnamed x105, local copies, waits for them, and re-layouts  17 us
    ppermute x6, waiting for transfers between devices, scatter(): blocks.append((lax.ppermute(block, 'ctx', rotation(ctx_size, -1 - j)), 0))  13.3 us
    ppermute x3, waiting for transfers between devices, shards(): lax.ppermute(piece(j), 'ctx', rotation(ctx_size, j)).astype(F32)  8.77 us
  transfers between devices with their start and end apart: 29, of which 11 were waited for; matrix products, arithmetic and copies ran while one was open for 10% of the time, Pallas kernels for 32%

commit v1 on v0

--- a/solution.py
+++ b/solution.py
@@ -20,6 +20,8 @@
 LANES = 128
 PAIRS = KEY_HEADS // 2
 PAIR_QUERY = QUERY_FEATURES // PAIRS
+GATE_LANES = 8
+SENT = MODEL_WIDTH + LANES
 COLUMNS = 512
 
 EPS = 1e-05
@@ -48,11 +50,18 @@
     return [(i, (i + by) % size) for i in range(size)]
 
 
-def ring_gather(block, size):
-    blocks = [block]
-    for _ in range(size - 1):
-        blocks.append(lax.ppermute(blocks[-1], "ctx", rotation(size, 1)))
-    return blocks[1:] + blocks[:1]
+def after(value, *others):
+    return lax.optimization_barrier((value, *others))[0]
+
+
+def rotations(block, size):
+    return [lax.ppermute(block, "ctx", rotation(size, j)) for j in range(1, size)] + [block]
+
+
+def send_back(blocks, size, first):
+    return [
+        lax.ppermute(b, "ctx", rotation(size, -1 - j)) for j, b in enumerate(blocks, first)
+    ]
 
 
 def low_lanes(shape):
@@ -87,9 +96,8 @@
     return [block[:, t * LANES : (t + 1) * LANES] for t in range(block.shape[1] // LANES)]
 
 
-def call(kernel, scalars, grid, ins, outs, scratch, flops, vmem=48):
-    bytes_accessed = sum(a.size * a.dtype.itemsize for a, _, _ in ins)
-    return pl.pallas_call(
+def call(kernel, scalars, grid, ins, outs, scratch, flops, vmem=62):
+    return list(pl.pallas_call(
         kernel,
         grid_spec=pltpu.PrefetchScalarGridSpec(
             num_scalar_prefetch=1,
@@ -103,9 +111,9 @@
             vmem_limit_bytes=vmem * MIB, dimension_semantics=("arbitrary",)
         ),
         cost_estimate=pl.CostEstimate(
-            flops=flops, bytes_accessed=bytes_accessed, transcendentals=0
+            flops=0, bytes_accessed=0, transcendentals=0
         ),
-    )(scalars, *[a for a, _, _ in ins])
+    )(scalars, *[a for a, _, _ in ins]))
 
 
 def whole(array):
@@ -268,10 +276,9 @@
     own = xs[0].shape[0]
     rows = own * len(xs)
     span = k.shape[0]
-    experts = router.shape[0]
     outs = [
         whole_out((rows, MODEL_WIDTH), BF16),
-        whole_out((rows, experts), F32),
+        whole_out((rows, LANES), F32),
     ]
     if with_own:
         outs += [
@@ -295,7 +302,7 @@
             chosen_whole(proj_out),
             whole(gain),
             whole(router),
-            (named, (rows, experts), lambda i, s: (part, 0)),
+            (named, (rows, LANES), lambda i, s: (part, 0)),
         ],
         outs,
         [pltpu.VMEM((rows, MODEL_WIDTH), F32), pltpu.VMEM((rows, ADAPTER_RANK), F32)],
@@ -307,88 +314,119 @@
     cots, refs = refs[:blocks], refs[blocks:]
     x_ref, gates, up_w, down_w, up_in, up_out, down_in, down_out = refs[:8]
     refs = refs[8:]
+    if not first:
+        (wide_old, narrow_old), refs = refs[:2], refs[2:]
+    rows_refs, refs = refs[:blocks], refs[blocks:]
     if first:
-        rows_ref, gg_ref, wide_ref, narrow_ref, cot_all, total, gg_all = refs
+        (wide_ref, narrow_ref), refs = refs[:2], refs[2:]
     else:
-        wide_old, narrow_old, rows_ref, gg_ref, send_ref, cot_all, total, gg_all = refs
+        send_ref, refs = refs[0], refs[1:]
+    cot_all, total, gg_all, rank_in_all, cot_mid_all, grad_rank_all, gated_all = refs
     step = pl.program_id(0)
-    here = pl.num_programs(0)
+    here = up_in.shape[1]
     own = cots[0].shape[0]
     r = ADAPTER_RANK
+    up_in_rows = up_in[0].reshape(here * 2 * r, MODEL_WIDTH)
+    x = x_ref[...]
 
     @pl.when(step == 0)
     def _():
         for b, cot in enumerate(cots):
             cot_all[b * own : (b + 1) * own] = cot[...]
-        total[...] = jnp.zeros_like(total)
         gg_all[...] = jnp.zeros_like(gg_all)
-
-    x, cot = x_ref[...], cot_all[...]
+        rank_in = mm_nt(x, up_in_rows).astype(BF16) * ADAPTER_SCALE
+        down_out_rows = down_out[0].reshape(here * r, MODEL_WIDTH)
+        cot_mid = ADAPTER_SCALE * mm_nt(cot_all[...], down_out_rows)
+        for e in range(here):
+            rank_in_all[e] = rank_in[:, e * 2 * r : (e + 1) * 2 * r]
+            cot_mid_all[e] = cot_mid[:, e * r : (e + 1) * r]
+
+    cot = cot_all[...]
     lane = lax.broadcasted_iota(jnp.int32, gates.shape, 1)
     gate_of = jnp.sum(
         jnp.where(lane == scalars[2] * here + step, gates[...], 0.0), axis=1, keepdims=True
     )
-    rank_in = mm_nt(x, up_in[0, 0]).astype(BF16)
-    rank_in2 = rank_in * ADAPTER_SCALE
-    gate_pre = mm(x, up_w[0, :, :EXPERT_HIDDEN]) + mm(rank_in2[:, :r], up_out[0, 0, 0])
-    up_pre = mm(x, up_w[0, :, EXPERT_HIDDEN:]) + mm(rank_in2[:, r:], up_out[0, 0, 1])
-    sig = 1.0 / (1.0 + jnp.exp(-gate_pre))
+    rank_in2 = rank_in_all[step]
+    none = jnp.zeros((r, EXPERT_HIDDEN), BF16)
+    out_map = jnp.concatenate(
+        [
+            jnp.concatenate([up_out[0, 0, 0], none], axis=1),
+            jnp.concatenate([none, up_out[0, 0, 1]], axis=1),
+        ],
+        axis=0,
+    )
+    pre = mm(x, up_w[0]) + mm(rank_in2, out_map)
+    gate_pre, up_pre = pre[:, :EXPERT_HIDDEN], pre[:, EXPERT_HIDDEN:]
+    cot_hidden = mm_nt(cot, down_w[0])
+    sig = 0.5 * jnp.tanh(0.5 * gate_pre) + 0.5
     silu = gate_pre * sig
-    hidden = (silu * up_pre).astype(BF16)
-    rank_mid = mm_nt(hidden, down_in[0, 0]).astype(BF16)
-    cot_mid = ADAPTER_SCALE * mm_nt(cot, down_out[0, 0])
-    cot_hidden = mm_nt(cot, down_w[0])
+    hidden_wide = silu * up_pre
+    hidden = hidden_wide.astype(BF16)
+    rank_mid = mm_nt(hidden, down_in[0, 0]).astype(BF16).astype(F32)
+    cot_mid = cot_mid_all[step]
     gate_grad = jnp.sum(hidden.astype(F32) * cot_hidden, axis=1, keepdims=True) + jnp.sum(
-        rank_mid.astype(F32) * cot_mid, axis=1, keepdims=True
+        rank_mid * cot_mid, axis=1, keepdims=True
     )
     gg_lane = lax.broadcasted_iota(jnp.int32, gg_all.shape, 1)
     gg_all[...] += jnp.where(gg_lane == step, gate_grad, 0.0)
     grad_rank_mid = (gate_of * cot_mid).astype(BF16)
     grad_hidden = gate_of * cot_hidden + mm(grad_rank_mid, down_in[0, 0])
+    grad_gate = (grad_hidden * up_pre * (sig + silu * (1.0 - sig))).astype(BF16)
     grad_up = (grad_hidden * silu).astype(BF16)
-    grad_gate = (grad_hidden * up_pre * sig * (1.0 + gate_pre * (1.0 - sig))).astype(BF16)
-    grad_rank_in = jnp.concatenate(
-        [mm_nt(grad_gate, up_out[0, 0, 0]), mm_nt(grad_up, up_out[0, 0, 1])], axis=1
-    )
-    grad_rank_in = (ADAPTER_SCALE * grad_rank_in).astype(BF16)
-    total[...] += (
-        mm_nt(grad_gate, up_w[0, :, :EXPERT_HIDDEN])
-        + mm_nt(grad_up, up_w[0, :, EXPERT_HIDDEN:])
-        + mm(grad_rank_in, up_in[0, 0])
-    )
-    gated_mid = (ADAPTER_SCALE * gate_of * rank_mid.astype(F32)).astype(BF16)
-    wide = jnp.concatenate([mm_tn(grad_rank_in, x), mm_tn(gated_mid, cot)], axis=0)
+    grad_both = jnp.concatenate([grad_gate, grad_up], axis=1)
+    grad_rank_all[step] = (ADAPTER_SCALE * mm_nt(grad_both, out_map)).astype(BF16)
+    gated_all[step] = (ADAPTER_SCALE * gate_of * rank_mid).astype(BF16)
+    part = mm_nt(grad_both, up_w[0])
+
+    @pl.when(step == 0)
+    def _():
+        total[...] = part
+
+    @pl.when(step > 0)
+    def _():
+        total[...] += part
+
+    both = mm_tn(
+        jnp.concatenate([rank_in2, grad_rank_mid], axis=1),
+        jnp.concatenate([grad_both, hidden], axis=1),
+    )
     narrow = jnp.concatenate(
         [
-            mm_tn(rank_in2[:, :r], grad_gate),
-            mm_tn(rank_in2[:, r:], grad_up),
-            mm_tn(grad_rank_mid, hidden),
+            both[i * r : (i + 1) * r, i * EXPERT_HIDDEN : (i + 1) * EXPERT_HIDDEN]
+            for i in range(3)
         ],
         axis=0,
     )
+    w, v = MODEL_WIDTH // parts, EXPERT_HIDDEN // parts
     if first:
-        wide_ref[0] = wide
         narrow_ref[0] = narrow
     else:
-        wide = (wide + wide_old[0]).astype(BF16)
         narrow = (narrow + narrow_old[0]).astype(BF16)
         at = pl.ds(pl.multiple_of(step * (3 * r), 16), 3 * r)
-        w, v = MODEL_WIDTH // parts, EXPERT_HIDDEN // parts
         for p in range(parts):
-            send_ref[p, at, :w] = wide[:, p * w : (p + 1) * w]
             send_ref[p, at, w:] = narrow[:, p * v : (p + 1) * v]
 
-        @pl.when(step == 0)
-        def _():
-            tail = send_ref.shape[1] - here * 3 * r
-            chosen = jnp.full((tail, w + v), scalars[0], jnp.int32).astype(F32).astype(BF16)
+    @pl.when(step == here - 1)
+    def _():
+        grad_rank = jnp.concatenate([grad_rank_all[e] for e in range(here)], axis=1)
+        gated = jnp.concatenate([gated_all[e] for e in range(here)], axis=1)
+        rows = total[...] + mm(grad_rank, up_in_rows)
+        high = gg_all[...].astype(BF16).astype(F32)
+        both = high + pltpu.roll(gg_all[...] - high, GATE_LANES, 1)
+        for b, rows_ref in enumerate(rows_refs):
+            at = slice(b * own, (b + 1) * own)
+            rows_ref[:, :MODEL_WIDTH] = rows[at].astype(BF16)
+            rows_ref[:, MODEL_WIDTH:] = both[at].astype(BF16)
+        wide = jnp.concatenate([mm_tn(grad_rank, x), mm_tn(gated, cot)], axis=0)
+        if first:
+            wide_ref[...] = wide
+        else:
+            wide = (wide + wide_old[...]).astype(BF16)
+            rows = here * 3 * r
+            chosen = jnp.full((16, w + v), scalars[0], jnp.int32).astype(F32).astype(BF16)
             for p in range(parts):
-                send_ref[p, here * 3 * r :] = chosen
-
-    @pl.when(step == here - 1)
-    def _():
-        rows_ref[...] = total[...].astype(BF16)
-        gg_ref[...] = gg_all[...].T[: gg_ref.shape[0]]
+                send_ref[p, :rows, :w] = wide[:, p * w : (p + 1) * w]
+                send_ref[p, rows:] = chosen
 
 
 def experts(scalars, parts, cots, x, gates, tables, before):
@@ -403,17 +441,18 @@
         whole(gates),
         (up_w, (1,) + up_w.shape[1:], per_expert),
         (down_w, (1,) + down_w.shape[1:], per_expert),
-        (up_in, (1, 1) + up_in.shape[2:], lambda i, s: (s[0], i, 0, 0)),
+        chosen_whole(up_in),
         (up_out, (1, 1) + up_out.shape[2:], lambda i, s: (s[0], i, 0, 0, 0)),
         (down_in, (1, 1) + down_in.shape[2:], lambda i, s: (s[0], i, 0, 0)),
-        (down_out, (1, 1) + down_out.shape[2:], lambda i, s: (s[0], i, 0, 0)),
+        chosen_whole(down_out),
     ]
-    outs = [whole_out((rows, MODEL_WIDTH), BF16), whole_out((8, rows), F32)]
+    outs = [whole_out((own, SENT), BF16) for _ in cots]
     if before is None:
-        for width in (MODEL_WIDTH, EXPERT_HIDDEN):
-            outs.append(((here, 3 * r, width), F32, (1, 3 * r, width), per_expert))
+        outs.append(whole_out((here * 3 * r, MODEL_WIDTH), F32))
+        outs.append(((here, 3 * r, EXPERT_HIDDEN), F32, (1, 3 * r, EXPERT_HIDDEN), per_expert))
     else:
-        ins += [(b, (1,) + b.shape[1:], per_expert) for b in before]
+        wide, narrow = before
+        ins += [whole(wide), (narrow, (1,) + narrow.shape[1:], per_expert)]
         width = (MODEL_WIDTH + EXPERT_HIDDEN) // parts
         outs.append(whole_out((parts, here * 3 * r + 16, width), BF16))
     return call(
@@ -426,26 +465,38 @@
             pltpu.VMEM((rows, MODEL_WIDTH), BF16),
             pltpu.VMEM((rows, MODEL_WIDTH), F32),
             pltpu.VMEM((rows, LANES), F32),
+            pltpu.VMEM((here, rows, 2 * r), BF16),
+            pltpu.VMEM((here, rows, r), F32),
+            pltpu.VMEM((here, rows, 2 * r), BF16),
+            pltpu.VMEM((here, rows, r), BF16),
         ],
         here * 2 * rows * MODEL_WIDTH * EXPERT_HIDDEN * 5,
     )
 
 
-def middle_kernel(blocks, scalars, *refs):
+def middle_kernel(blocks, here, scalars, *refs):
     parts, refs = refs[:blocks], refs[blocks:]
-    gate_grads, gates, router, middle_ref, inv_ref, gain, cot = refs[:7]
-    proj_w, proj_in, proj_out, q_ref, k_ref, v_ref, bias, cosine, sine = refs[7:16]
-    grad_middle, branch_ref, lora_ref, gq_ref, gk_ref, gv_ref, grad_att = refs[16:]
+    gates, router, middle_ref, inv_ref, gain, cot = refs[:6]
+    proj_w, proj_in, proj_out, q_ref, k_ref, v_ref, bias, cosine, sine = refs[6:15]
+    grad_middle, branch_ref, lora_ref, gq_ref = refs[15:19]
+    gkv_refs, grad_att = refs[19:-1], refs[-1]
     step = pl.program_id(0)
+    own = q_ref.shape[0]
 
     @pl.when(step == 0)
     def _():
         gates_own = gates[...]
-        gg = gate_grads[...]
+        lane = lax.broadcasted_iota(jnp.int32, gates_own.shape, 1)
+        gg = jnp.zeros_like(gates_own)
+        for j, part in enumerate(parts):
+            both = part[:, MODEL_WIDTH:].astype(F32)
+            both = both + pltpu.roll(both, LANES - GATE_LANES, 1)
+            both = jnp.where(lane < here, both, 0.0)
+            gg = gg + pltpu.roll(both, lax.rem(scalars[2] + 1 + j, blocks) * here, 1)
         chosen = gates_own * (gg - jnp.sum(gates_own * gg, axis=-1, keepdims=True))
         grad = mm(chosen.astype(BF16), router[...])
         for part in parts:
-            grad = grad + part[...].astype(F32)
+            grad = grad + part[:, :MODEL_WIDTH].astype(F32)
         scaled = grad * gain[...]
         middle, inv = middle_ref[...], inv_ref[...]
         grad = (
@@ -486,11 +537,13 @@
         grads_all.append(jnp.where(inside, grads[h], zero_q))
     scores_six = jnp.concatenate(scores_all, axis=1)
     grad_key = mm(scores_six, jnp.concatenate(queries_all, axis=0))
-    gk_ref[...] = turned(grad_key, cosine[...], -sine[...]).astype(BF16)
-    gv_ref[...] = mm(
+    grad_key = turned(grad_key, cosine[...], -sine[...]).astype(BF16)
+    grad_value = mm(
         jnp.concatenate(probs_all, axis=1), jnp.concatenate(grads_all, axis=0)
     ).astype(BF16)
-    own = q_ref.shape[0]
+    for b, gkv_ref in enumerate(gkv_refs):
+        gkv_ref[:, :LANES] = grad_key[b * own : (b + 1) * own]
+        gkv_ref[:, LANES:] = grad_value[b * own : (b + 1) * own]
     key_t = [key_of[0].astype(F32).T.astype(BF16), key_of[1].astype(F32).T.astype(BF16)]
     halves = [key_t[0][:HEAD_SIZE], key_t[1][HEAD_SIZE:]]
     cos, sin = cosine[-own:], -sine[-own:]
@@ -501,22 +554,20 @@
 
 
 def middle_backward(
-    scalars, parts, gate_grads, gates, router, middle, inv, gain, cot, proj_w, proj_in, proj_out,
+    scalars, parts, here, gates, router, middle, inv, gain, cot, proj_w, proj_in, proj_out,
     q, k, v, bias_t, cosine, sine,
 ):
     own = cot.shape[0]
     span = k.shape[0]
     last = span // own - 1
-    experts_all = router.shape[0]
     gates_last = gates.shape[0] // own - 1
     return call(
-        functools.partial(middle_kernel, len(parts)),
+        functools.partial(middle_kernel, len(parts), here),
         scalars,
         PAIRS,
-        [(a, (own, MODEL_WIDTH), lambda i, s, b=b: (b, 0)) for a, b in parts]
+        [whole(part) for part in parts]
         + [
-            whole(gate_grads),
-            (gates, (own, experts_all), lambda i, s: (gates_last, 0)),
+            (gates, (own, LANES), lambda i, s: (gates_last, 0)),
             whole(router),
             whole(middle),
             whole(inv),
@@ -537,22 +588,31 @@
             whole_out((own, MODEL_WIDTH), BF16),
             whole_out((own, ADAPTER_RANK), BF16),
             ((own, QUERY_FEATURES), BF16, (own, PAIR_QUERY), lambda i, s: (0, i)),
-            ((span, KEY_FEATURES), BF16, (span, LANES), lambda i, s: (0, i)),
-            ((span, KEY_FEATURES), BF16, (span, LANES), lambda i, s: (0, i)),
+        ]
+        + [
+            ((own, 2 * KEY_FEATURES), BF16, (own, 2 * LANES), lambda i, s: (0, i))
+            for _ in range(span // own)
         ],
         [pltpu.VMEM((PAIRS, own, PAIR_QUERY), BF16)],
         10 * own * span * QUERY_FEATURES + 2 * own * MODEL_WIDTH * QUERY_FEATURES,
     )
 
 
-def adapter_kernel(parts, scalars, *refs):
-    gq, gk, gv, query_out, kv_out, normed, lora_in, attended, lora_out, branch, grad_lora = refs[:11]
-    query_w, send_ref, first_ref = refs[11:]
+def key_and_value(columns):
+    return jnp.concatenate(columns[0::2], axis=1), jnp.concatenate(columns[1::2], axis=1)
+
+
+def adapter_kernel(parts, blocks, scalars, *refs):
+    gkvs, refs = refs[:blocks], refs[blocks:]
+    gq, query_out, kv_out, normed, lora_in, attended, lora_out, branch, grad_lora = refs[:9]
+    send_refs, table = refs[9:-1], refs[-1]
     own = gq.shape[0]
     r = ADAPTER_RANK
+    gkv = jnp.concatenate([g[...] for g in gkvs], axis=0)
+    gk, gv = key_and_value(lane_tiles(gkv))
     lora_q = (ADAPTER_SCALE * mm_nt(gq[...], query_out[0])).astype(BF16)
-    lora_k = (ADAPTER_SCALE * mm_nt(gk[...], kv_out[0, 0])).astype(BF16)
-    lora_v = (ADAPTER_SCALE * mm_nt(gv[...], kv_out[0, 1])).astype(BF16)
+    lora_k = (ADAPTER_SCALE * mm_nt(gk, kv_out[0, 0])).astype(BF16)
+    lora_v = (ADAPTER_SCALE * mm_nt(gv, kv_out[0, 1])).astype(BF16)
     low2 = lora_in[...] * ADAPTER_SCALE
     wide = [
         mm_tn(lora_q, normed[-own:]),
@@ -562,33 +622,34 @@
         mm_tn(grad_lora[...], attended[...]),
         mm_tn(lora_out[...] * ADAPTER_SCALE, branch[...]),
     ]
-    narrow = [mm_tn(low2[:, r : 2 * r], gk[...]), mm_tn(low2[:, 2 * r :], gv[...])]
+    narrow = [mm_tn(low2[:, r : 2 * r], gk), mm_tn(low2[:, 2 * r :], gv)]
+    wide, narrow = jnp.concatenate(wide, axis=0), jnp.concatenate(narrow, axis=0)
     w, v = MODEL_WIDTH // parts, KEY_FEATURES // parts
-    for n, rows in enumerate(wide):
-        rows = rows.astype(BF16)
+    count = 6 * r // blocks
+    for b in range(blocks):
+        at, below = b * count, min((b + 1) * count, 2 * r)
         for p in range(parts):
-            send_ref[p, n * r : (n + 1) * r, :w] = rows[:, p * w : (p + 1) * w]
-    for n in range(len(wide)):
-        for p in range(parts):
-            if n < len(narrow):
-                rows = narrow[n][:, p * v : (p + 1) * v].astype(BF16)
-            else:
-                rows = jnp.zeros((r, v), BF16)
-            send_ref[p, n * r : (n + 1) * r, w:] = rows
-    first_ref[...] = mm_nt(gq[...], query_w[...])
-
-
-def adapters(scalars, parts, gq, gk, gv, query_out, kv_out, normed, lora_in, attended, lora_out,
-             branch, grad_lora, query_w):
+            table[b, p, :, :w] = wide[at : at + count, p * w : (p + 1) * w]
+            if below < at + count:
+                table[b, p, :, w:] = jnp.zeros((count, v), F32)
+            if at < below:
+                table[b, p, : below - at, w:] = narrow[at:below, p * v : (p + 1) * v]
+    for j, send in enumerate(send_refs):
+        send[...] = table[lax.rem(scalars[2] + 2 * blocks - 1 - j, blocks)].astype(BF16)
+
+
+def adapters(scalars, parts, gkvs, gq, query_out, kv_out, normed, lora_in, attended, lora_out,
+             branch, grad_lora):
     own = gq.shape[0]
+    blocks = len(gkvs)
+    share = (parts, 6 * ADAPTER_RANK // blocks, (MODEL_WIDTH + KEY_FEATURES) // parts)
     return call(
-        functools.partial(adapter_kernel, parts),
+        functools.partial(adapter_kernel, parts, blocks),
         scalars,
         1,
-        [
+        [whole(g) for g in gkvs]
+        + [
             whole(gq),
-            whole(gk),
-            whole(gv),
             chosen_whole(query_out),
             chosen_whole(kv_out),
             whole(normed),
@@ -597,24 +658,129 @@
             whole(lora_out),
             whole(branch),
             whole(grad_lora),
-            whole(query_w),
-        ],
+        ],
+        [whole_out(share, BF16) for _ in range(blocks)],
+        [pltpu.VMEM((blocks,) + share, F32)],
+        2 * own * MODEL_WIDTH * QUERY_FEATURES,
+    )
+
+
+def summed(received, choices, adapter, senders):
+    total = None
+    for n in range(senders):
+        rows = jnp.where(choices[n, :1, :1].astype(F32) == adapter, received(n), 0.0)
+        total = rows if total is None else total + rows
+    return total
+
+
+def expert_sum_kernel(wide, scalars, got, choices, up_in, up_out, down_in, down_out):
+    adapter = pl.program_id(0).astype(F32)
+    total = summed(lambda n: got[n].astype(F32), choices, adapter, got.shape[0])
+    r = ADAPTER_RANK
+    here = up_in.shape[1]
+    for e in range(here):
+        up_in[0, e] = total[e * 2 * r : (e + 1) * 2 * r, :wide]
+        down_out[0, e] = total[(2 * here + e) * r : (2 * here + e + 1) * r, :wide]
+        rows = total[e * 3 * r : (e + 1) * 3 * r]
+        up_out[0, e, 0] = rows[:r, wide:]
+        up_out[0, e, 1] = rows[r : 2 * r, wide:]
+        down_in[0, e] = rows[2 * r :, wide:]
+
+
+def expert_sum(scalars, got, here):
+    parts, _, width = got.shape
+    r = ADAPTER_RANK
+    rows = here * 3 * r
+    wide, narrow = MODEL_WIDTH // parts, EXPERT_HIDDEN // parts
+
+    def out(*shape):
+        return ((ADAPTER_CHOICES,) + shape, F32, (1,) + shape, lambda i, s: (i,) + (0,) * len(shape))
+
+    return call(
+        functools.partial(expert_sum_kernel, wide),
+        scalars,
+        ADAPTER_CHOICES,
         [
-            whole_out((parts, 6 * ADAPTER_RANK, (MODEL_WIDTH + KEY_FEATURES) // parts), BF16),
-            whole_out((own, MODEL_WIDTH), F32),
+            (got, (parts, rows, width), lambda i, s: (0, 0, 0)),
+            (got, (parts, 16, width), lambda i, s: (0, rows // 16, 0)),
+        ],
+        [
+            out(here, 2 * r, wide),
+            out(here, 2, r, narrow),
+            out(here, r, narrow),
+            out(here, r, wide),
         ],
         [],
-        2 * own * MODEL_WIDTH * QUERY_FEATURES * 2,
+        2 * ADAPTER_CHOICES * parts * rows * width,
+    )
+
+
+def share_kernel(parts, scalars, got, choices, out_ref):
+    each = [got[n].astype(F32) for n in range(parts)]
+    for a in range(ADAPTER_CHOICES):
+        out_ref[a] = summed(lambda n: each[n], choices, float(a), parts).astype(BF16)
+
+
+def share_sum(scalars, got, expert_got, rows):
+    parts = expert_got.shape[0]
+    width = got.shape[2]
+    return call(
+        functools.partial(share_kernel, parts),
+        scalars,
+        1,
+        [whole(got), (expert_got, (parts, 16, width), lambda i, s: (0, rows // 16, 0))],
+        [whole_out((ADAPTER_CHOICES,) + got.shape[1:], BF16)],
+        [],
+        2 * ADAPTER_CHOICES * got.size,
+    )[0]
+
+
+def place_kernel(blocks, wide, scalars, *refs):
+    shares, refs = refs[:blocks], refs[blocks:]
+    qkv_in, query_out, kv_out, proj_in, proj_out, placed = refs
+    for j, share in enumerate(shares):
+        placed[lax.rem(scalars[2] + blocks - j, blocks)] = share[...].astype(F32)
+    r = ADAPTER_RANK
+    rows = shares[0].shape[1]
+    for a in range(ADAPTER_CHOICES):
+        table = jnp.concatenate([placed[b, a] for b in range(blocks)], axis=0)
+        qkv_in[a] = table[: 3 * r, :wide]
+        query_out[a] = table[3 * r : 4 * r, :wide]
+        proj_in[a] = table[4 * r : 5 * r, :wide]
+        proj_out[a] = table[5 * r :, :wide]
+        kv_out[a, 0] = table[:r, wide:]
+        kv_out[a, 1] = table[r : 2 * r, wide:]
+
+
+def place(scalars, shares, parts):
+    r = ADAPTER_RANK
+    wide, narrow = MODEL_WIDTH // parts, KEY_FEATURES // parts
+
+    def out(*shape):
+        return whole_out((ADAPTER_CHOICES,) + shape, F32)
+
+    return call(
+        functools.partial(place_kernel, len(shares), wide),
+        scalars,
+        1,
+        [whole(s) for s in shares],
+        [
+            out(3 * r, wide),
+            out(r, wide),
+            out(2, r, narrow),
+            out(r, wide),
+            out(r, wide),
+        ],
+        [pltpu.VMEM((len(shares),) + shares[0].shape, F32)],
+        0,
     )
 
 
 def input_kernel(blocks, scalars, *refs):
-    gks, gvs, refs = refs[:blocks], refs[blocks : 2 * blocks], refs[2 * blocks :]
-    gq, first, kv_w, query_out, kv_out, down, x_ref, gain, grad_middle, out_ref = refs
-    grad_k, grad_v = [
-        functools.reduce(lambda a, b: a + b, [g[...].astype(F32) for g in gs]).astype(BF16)
-        for gs in (gks, gvs)
-    ]
+    gkvs, refs = refs[:blocks], refs[blocks:]
+    gq, query_w, kv_w, query_out, kv_out, down, x_ref, gain, grad_middle, out_ref = refs
+    grad_kv = functools.reduce(lambda a, b: a + b, [g[...].astype(F32) for g in gkvs])
+    grad_k, grad_v = key_and_value(lane_tiles(grad_kv.astype(BF16)))
     lora = jnp.concatenate(
         [
             mm_nt(gq[...], query_out[0]),
@@ -625,7 +791,7 @@
     )
     lora = (ADAPTER_SCALE * lora).astype(BF16)
     grad = (
-        first[...]
+        mm_nt(gq[...], query_w[...])
         + mm_nt(grad_k, kv_w[:, :KEY_FEATURES])
         + mm_nt(grad_v, kv_w[:, KEY_FEATURES:])
         + mm(lora, down[0])
@@ -640,17 +806,16 @@
     )
 
 
-def input_backward(scalars, gks, gvs, gq, first, kv_w, query_out, kv_out, down, x, gain, grad_middle):
+def input_backward(scalars, gkvs, gq, query_w, kv_w, query_out, kv_out, down, x, gain, grad_middle):
     own = x.shape[0]
-    blocked = [(a, (own, KEY_FEATURES), lambda i, s, b=b: (b, 0)) for a, b in gks + gvs]
     return call(
-        functools.partial(input_kernel, len(gks)),
+        functools.partial(input_kernel, len(gkvs)),
         scalars,
         1,
-        blocked
+        [whole(g) for g in gkvs]
         + [
             whole(gq),
-            whole(first),
+            whole(query_w),
             whole(kv_w),
             chosen_whole(query_out),
             chosen_whole(kv_out),
@@ -663,10 +828,6 @@
         [],
         4 * own * MODEL_WIDTH * KEY_FEATURES,
     )[0]
-
-
-def by_adapter(received, selector):
-    return jnp.einsum("as,srw->arw", selector, received.astype(F32), precision="highest")
 
 
 def shards(
@@ -707,11 +868,6 @@
 
     order = (rank - 1 - jnp.arange(ctx_size, dtype=jnp.int32)) % ctx_size
     positions = (order[:, None] * own + jnp.arange(own, dtype=jnp.int32)[None, :]).reshape(-1)
-    inputs = ring_gather(layer_input_rows[0], ctx_size)
-    route_blocks = ring_gather(routes[0], ctx_size)
-    cot_own, inputs[-2] = lax.optimization_barrier((cotangent[0], inputs[-2]))
-    cots = ring_gather(cot_own, ctx_size)
-
     size = HEAD_SIZE // 2
     frequency = ROPE_BASE ** (-jnp.arange(size, dtype=F32) / size)
     angles = positions.astype(F32)[:, None] * frequency[None, :]
@@ -721,13 +877,24 @@
     allowed = (positions[None, :] <= positions[:, None]) | (positions[None, :] < prefix[0])
     bias = jnp.where(allowed, 0.0, MASKED).astype(F32)
     bias_t = bias[-own:].T
-    expert_ids = jnp.arange(experts_all, dtype=jnp.int32)
+    qkv_in_t = adapter_query_key_value_input.transpose(0, 2, 1)
+    proj_in_t = adapter_projection_input.transpose(0, 2, 1)
+    router_t = jnp.pad(router_weight.T, ((0, LANES - experts_all), (0, 0)))
+
+    x_own, cot_own = layer_input_rows[0], cotangent[0]
+    step = functools.partial(lax.ppermute, axis_name="ctx", perm=rotation(ctx_size, 1))
+    inputs = [step(x_own)]
+    own_routes = after(routes[0], inputs[0])
+    inputs.append(step(after(inputs[0], cosine, sine, bias, bias_t, router_t, scalars)))
+    route_blocks = rotations(own_routes, ctx_size)
+    while len(inputs) < ctx_size - 1:
+        inputs.append(step(inputs[-1]))
+    inputs.append(x_own)
+    cots = rotations(after(cot_own, inputs[-2], *route_blocks[:-1]), ctx_size)
+    expert_ids = jnp.arange(LANES, dtype=jnp.int32)
     routes_all = jnp.concatenate(route_blocks, axis=0)
     named = jnp.any(routes_all[:, :, None] == expert_ids[None, None, :], axis=1).astype(F32)
 
-    qkv_in_t = adapter_query_key_value_input.transpose(0, 2, 1)
-    proj_in_t = adapter_projection_input.transpose(0, 2, 1)
-    router_t = router_weight.T
     q, k, v, normed, lora_in = qkv(
         scalars, inputs, gain_attn, qkv_in_t, query_weight, key_value_weight,
         adapter_query_output, adapter_key_value_output, cosine, sine,
@@ -748,91 +915,55 @@
         )
 
     normed_first, gates_first = attend_half(0, False)
-    rows_first, gg_first, wide, narrow = experts(
+    *rows_first, wide, narrow = experts(
         scalars, dp_size, cots[:half], normed_first, gates_first, tables, None
     )
+    q = after(q, rows_first[0])
     normed_last, gates_last, attended, lora_out, middle, inv = attend_half(1, True)
-    rows_last, gg_last, send = experts(
+    *rows_last, send = experts(
         scalars, dp_size, cots[half:], normed_last, gates_last, tables, (wide, narrow)
     )
 
-    def back(first, last, axis):
-        got = []
-        for j in range(ctx_size - 1):
-            source, at = (first, j) if j < half else (last, j - half)
-            block = lax.slice_in_dim(source, at * own, (at + 1) * own, axis=axis)
-            got.append((lax.ppermute(block, "ctx", rotation(ctx_size, -1 - j)), 0))
-        return got
-
-    gg_blocks = [b[:experts_here] for b, _ in back(gg_first, gg_last, 1)]
-    got = back(rows_first, rows_last, 0)
-    got.append((rows_last, half - 1))
-    gg_blocks.append(gg_last[:experts_here, -own:])
-    gate_grads = jnp.concatenate(gg_blocks, axis=0)
-    shift = (jnp.arange(experts_all, dtype=jnp.int32) - (rank + 1) * experts_here) % experts_all
-    gate_grads = jnp.take(gate_grads, shift, axis=0).T
+    got = send_back(rows_first, ctx_size, 0)
+    rows_last[0] = after(rows_last[0], *got)
+    got += send_back(rows_last[:-1], ctx_size, half) + rows_last[-1:]
     expert_got = lax.all_to_all(send, "dp", 0, 0, tiled=True)
 
-    grad_middle, branch, grad_lora, gq, gk, gv = middle_backward(
-        scalars, got, gate_grads, gates_last, router_t, middle, inv, gain_ffn, cot_own,
+    grad_middle, branch, grad_lora, gq, *gkvs = middle_backward(
+        scalars, got, experts_here, gates_last, router_t, middle, inv, gain_ffn, cot_own,
         projection_weight, proj_in_t, adapter_projection_output, q, k, v, bias_t, cosine, sine,
     )
-
-    def scatter(array):
-        blocks = []
-        for j in range(ctx_size - 1):
-            block = array[j * own : (j + 1) * own]
-            blocks.append((lax.ppermute(block, "ctx", rotation(ctx_size, -1 - j)), 0))
-        return blocks + [(array, ctx_size - 1)]
-
-    gks, gvs = scatter(gk), scatter(gv)
-    attention_rows, first = adapters(
-        scalars, dp_size, gq, gk, gv, adapter_query_output, adapter_key_value_output, normed,
-        lora_in, attended, lora_out, branch, grad_lora, query_weight,
-    )
+    shares = adapters(
+        scalars, dp_size, gkvs, after(gq, expert_got), adapter_query_output,
+        adapter_key_value_output, normed, lora_in, attended, lora_out, branch, grad_lora,
+    )
+    gkvs = send_back(gkvs[:-1], ctx_size, 0) + [gkvs[-1]]
+    shares = send_back([after(shares[0], gkvs[0])] + shares[1:-1], ctx_size, 0) + [shares[-1]]
+    up_in, up_out, down_in, down_out = expert_sum(scalars, expert_got, experts_here)
+    share = functools.reduce(lambda a, b: a + b, [s.astype(F32) for s in shares]).astype(BF16)
+    share = after(share, up_in, gkvs[-2])
+    attention_got = lax.all_to_all(share, "dp", 0, 0, tiled=True)
+    attention_got = after(attention_got, *gkvs[1:-2])
+    share = share_sum(scalars, attention_got, expert_got, experts_here * 3 * ADAPTER_RANK)
+    shares = rotations(share, ctx_size)
+    shares = shares[-1:] + shares[:-1]
     grad_inputs = input_backward(
-        scalars, gks, gvs, gq, first, key_value_weight, adapter_query_output,
-        adapter_key_value_output, qkv_in_t, layer_input_rows[0], gain_attn, grad_middle,
-    )
-
-    rows_count = 6 * ADAPTER_RANK // ctx_size
-    pieces = attention_rows.reshape(dp_size, ctx_size, rows_count, -1)
-
-    def piece(j):
-        return lax.dynamic_index_in_dim(pieces, (rank + j) % ctx_size, 1, keepdims=False)
-
-    choices = expert_got[:, experts_here * 3 * ADAPTER_RANK, 0].astype(F32)
-    selector = (jnp.arange(ADAPTER_CHOICES, dtype=F32)[:, None] == choices[None, :]).astype(F32)
-    share = piece(0).astype(F32)
-    for j in range(1, ctx_size):
-        share = share + lax.ppermute(piece(j), "ctx", rotation(ctx_size, j)).astype(F32)
-    share = lax.all_to_all(share.astype(BF16), "dp", 0, 0, tiled=True)
-    share = by_adapter(share, selector).astype(BF16)
-    attention_sum = [share]
-    for j in range(1, ctx_size):
-        attention_sum.append(lax.ppermute(share, "ctx", rotation(ctx_size, j)))
-    attention_sum = jnp.stack(attention_sum, axis=1)
-    back_order = (rank - jnp.arange(ctx_size, dtype=jnp.int32)) % ctx_size
-    attention_sum = jnp.take(attention_sum, back_order, axis=1)
-    attention_sum = attention_sum.reshape(ADAPTER_CHOICES, 6 * ADAPTER_RANK, -1).astype(F32)
-    expert_sum = by_adapter(expert_got[:, : experts_here * 3 * ADAPTER_RANK], selector)
-
-    wide_width = MODEL_WIDTH // dp_size
-    r = ADAPTER_RANK
-    attn_wide, attn_narrow = attention_sum[..., :wide_width], attention_sum[..., wide_width:]
-    by_expert = expert_sum.reshape(ADAPTER_CHOICES, experts_here, 3 * r, -1)
-    exp_wide, exp_narrow = by_expert[..., :wide_width], by_expert[..., wide_width:]
+        scalars, gkvs, after(gq, share), query_weight, key_value_weight, adapter_query_output,
+        adapter_key_value_output, qkv_in_t, x_own, gain_attn, grad_middle,
+    )
+    shares[1] = after(shares[1], grad_inputs)
+    qkv_in, query_out, kv_out, proj_in, proj_out = place(scalars, shares, dp_size)
     return (
         grad_inputs[None],
-        attn_wide[:, : 3 * r].transpose(0, 2, 1),
-        attn_wide[:, 3 * r : 4 * r],
-        attn_narrow[:, : 2 * r].reshape(ADAPTER_CHOICES, 2, r, -1),
-        attn_wide[:, 4 * r : 5 * r].transpose(0, 2, 1),
-        attn_wide[:, 5 * r :],
-        exp_wide[:, :, : 2 * r].transpose(0, 1, 3, 2),
-        exp_narrow[:, :, : 2 * r].reshape(ADAPTER_CHOICES, experts_here, 2, r, -1),
-        exp_narrow[:, :, 2 * r :].transpose(0, 1, 3, 2),
-        exp_wide[:, :, 2 * r :],
+        qkv_in.transpose(0, 2, 1),
+        query_out,
+        kv_out,
+        proj_in.transpose(0, 2, 1),
+        proj_out,
+        up_in.transpose(0, 1, 3, 2),
+        up_out,
+        down_in.transpose(0, 1, 3, 2),
+        down_out,
     )
 
 

time: 289 us -> 240 us (0.83)
  local copies, waits for them, and re-layouts: 35.5 us -> 7.8 us
  starting transfers between devices: 52.9 us -> 32.8 us
  Pallas kernels: 118 us -> 137 us
  waiting for transfers between devices: 69.6 us -> 51.6 us
    pallas_call x8 -> x11, Pallas kernels: 118 us -> 137 us  [call(): pl.pallas_call(kernel, grid_spec=pltpu.PrefetchScalarGridSpec(num_scalar_...]
    ppermute x27 -> x21, starting transfers between devices: 44.5 us -> 25.5 us  [the longest x9 13.1 us: rotations(): lax.ppermute(block, 'ctx', rotation(size, j))]
    ppermute x27 -> x21, waiting for transfers between devices: 65.3 us -> 49.2 us  [the longest x9 25.8 us: send_back(): lax.ppermute(b, 'ctx', rotation(size, -1 - j))]
    unnamed x105 -> x44, local copies, waits for them, and re-layouts: 17 us -> 2.73 us
    slice x15 -> x0, local copies, waits for them, and re-layouts: 8.51 us -> none  [the longest x4 2.9 us: back(): block = lax.slice_in_dim(source, at * own, (at + 1) * own, axis=axis)]
    gather x3 -> x0, local copies, waits for them, and re-layouts: 4.11 us -> none  [the longest x2 3.42 us: shards(): gate_grads = jnp.take(gate_grads, shift, axis=0).T]
  transfers between devices with their start and end apart: 29 -> 23, of which waited for: 11 -> 10; matrix products, arithmetic and copies ran while one was open for 10% -> 5% of each run, Pallas kernels for 32% -> 55%
where the time goes in v1:
time: 240 us; the launch traced here: 239 us
  Pallas kernels  137 us (57%)
  waiting for transfers between devices  51.6 us (22%)
  starting transfers between devices  32.8 us (14%)
  local copies, waits for them, and re-layouts  7.8 us (3%)
  other arithmetic  7.61 us (3%)
    pallas_call x11, Pallas kernels, call(): pl.pallas_call(kernel, grid_spec=pltpu.PrefetchScalarGridSpec(num_scalar_...  137 us
    ppermute x9, waiting for transfers between devices, send_back(): lax.ppermute(b, 'ctx', rotation(size, -1 - j))  25.8 us
    ppermute x9, starting transfers between devices, rotations(): lax.ppermute(block, 'ctx', rotation(size, j))  13.1 us
    ppermute x1, waiting for transfers between devices, shards(): step(after(inputs[0], cosine, sine, bias, bias_t, router_t, scalars))  12.1 us
    ppermute x9, starting transfers between devices, send_back(): lax.ppermute(b, 'ctx', rotation(size, -1 - j))  9.33 us
    ppermute x9, waiting for transfers between devices, rotations(): lax.ppermute(block, 'ctx', rotation(size, j))  7.02 us
  transfers between devices with their start and end apart: 23, of which 10 were waited for; matrix products, arithmetic and copies ran while one was open for 5% of the time, Pallas kernels for 55%

profile of v1, /device:TPU:0, one launch (start us, length us, event | category | flops | bytes accessed | tf_op | source)
XLA Modules:
  0.0 239.1 jit_solution(12238642975363084669)
XLA Ops:
  0.7 3.1 %collective-permute-start = (bf16[128,1536]{1,0:T(8,128)(2,1)}, bf16[128,1536]{1,0:T(8,128)(2,1)S(1)}, u32[]{:S(2)}, u32[]{:S(2)}) collective-permute-start(bf16[128,1536]{1,0:T(8,128)(2,1)} %bitcast.31), channel_id=1, source_target_pairs={{0,1},{1,2},{2,3},{3,0},{4,5},{5,6},{6,7},{7,4},{8,9},{9,10},{10,1... | collective-permute-start | bytes 1179656 | tf_op jit(solution)/shard_map/ppermute | solution.py:886
  7.1 1.7 pad.4.refs_10_.refs_5_
  8.8 1.3 pad_maximum_fusion
  10.8 4.3 %collective-permute-done.refs_0_ = bf16[128,1536]{1,0:T(8,128)(2,1)S(1)} collective-permute-done((bf16[128,1536]{1,0:T(8,128)(2,1)}, bf16[128,1536]{1,0:T(8,128)(2,1)S(1)}, u32[]{:S(2)}, u32[]{:S(2)}) %collective-permute-start) | collective-permute-done | bytes 393248 | tf_op jit(solution)/shard_map/ppermute | solution.py:886
  15.1 12.1 %collective-permute-done.1.refs_1_ = bf16[128,1536]{1,0:T(8,128)(2,1)S(1)} collective-permute-done((bf16[128,1536]{1,0:T(8,128)(2,1)S(1)}, bf16[128,1536]{1,0:T(8,128)(2,1)S(1)}, u32[]{:S(2)}, u32[]{:S(2)}) %collective-permute-start.1) | collective-permute-done | bytes 393248 | tf_op jit(solution)/shard_map/ppermute | solution.py:888
  27.2 3.8 %collective-permute-start.5 = (s32[128,8]{0,1:T(8,128)S(1)}, s32[128,8]{0,1:T(8,128)S(1)}, u32[]{:S(2)}, u32[]{:S(2)}) collective-permute-start(s32[128,8]{0,1:T(8,128)S(1)} %bitcast.44), channel_id=1, source_target_pairs={{0,3},{1,0},{2,1},{3,2},{4,7},{5,4},{6,5},{7,6},{8,11},{9,8},{10,9... | collective-permute-start | bytes 12296 | tf_op jit(solution)/shard_map/ppermute | solution.py:58
  31.6 2.9 %collective-permute-done.5 = s32[128,8]{0,1:T(8,128)S(1)} collective-permute-done((s32[128,8]{0,1:T(8,128)S(1)}, s32[128,8]{0,1:T(8,128)S(1)}, u32[]{:S(2)}, u32[]{:S(2)}) %collective-permute-start.5) | collective-permute-done | bytes 4128 | tf_op jit(solution)/shard_map/ppermute | solution.py:58
  34.6 1.4 collective-permute-done.4
  35.9 2.7 %collective-permute-done.3 = s32[128,8]{0,1:T(8,128)S(1)} collective-permute-done((s32[128,8]{0,1:T(8,128)S(1)}, s32[128,8]{0,1:T(8,128)S(1)}, u32[]{:S(2)}, u32[]{:S(2)}) %collective-permute-start.3) | collective-permute-done | bytes 4128 | tf_op jit(solution)/shard_map/ppermute | solution.py:58
  39.5 1.3 copy.40.refs_5_
  42.1 3.8 %collective-permute-start.10 = (bf16[128,1536]{1,0:T(8,128)(2,1)S(1)}, bf16[128,1536]{1,0:T(8,128)(2,1)}, u32[]{:S(2)}, u32[]{:S(2)}) collective-permute-start(bf16[128,1536]{1,0:T(8,128)(2,1)S(1)} %bitcast.41), channel_id=1, source_target_pairs={{0,3},{1,0},{2,1},{3,2},{4,7},{5,4},{6,5},{7,6},{8,11},{9,8},{10,9... | collective-permute-start | bytes 1179656 | tf_op jit(solution)/shard_map/ppermute | solution.py:58
  45.9 2.9 %fusion = pred[512,128]{1,0:T(8,128)(4,1)S(1)} fusion(s32[512,8]{1,0:T(8,128)S(1)} %copy.39), kind=kLoop, calls=%fused_computation.1 | loop fusion | flops 983040 | bytes 81920 | tf_op jit(solution)/shard_map/reduce_or | solution.py:896
  49.6 13.7 %shard_map.285 = (bf16[512,1536]{1,0:T(8,128)(2,1)}, bf16[512,512]{1,0:T(8,128)(2,1)}, bf16[512,512]{1,0:T(8,128)(2,1)}, bf16[512,1536]{1,0:T(8,128)(2,1)}, bf16[512,48]{1,0:T(8,128)(2,1)}) custom-call(s32[3]{0:T(128)} %pad_add_fusion.1.scalars, bf16[128,1536]{1,0:T(8,128)(2,1)} %copy-done.2, bf16[128,1536]{1,0:T(8,128)(2,1)} %copy-done.4, ...), custom_call_target="tpu_custom_call" | custom-call | tf_op jit(solution)/shard_map/pallas_call | solution.py:100
  63.3 16.6 %shard_map.286 = (bf16[256,1536]{1,0:T(8,128)(2,1)}, f32[256,128]{1,0:T(8,128)}) custom-call(s32[3]{0:T(128)} %pad_add_fusion.1.scalars, bf16[128,1536]{1,0:T(8,128)(2,1)} %copy-done.2, bf16[128,1536]{1,0:T(8,128)(2,1)} %copy-done.4, bf16[512,1536]{1,0:T(8,128)(2,1)} %get-tuple-element.72.refs_2_.refs_13_, ...), custom_call_target="tpu_custom_call" | custom-call | tf_op jit(solution)/shard_map/pallas_call | solution.py:100
  80.7 24.4 %shard_map.287 = (bf16[128,1664]{1,0:T(8,128)(2,1)}, bf16[128,1664]{1,0:T(8,128)(2,1)}, f32[240,1536]{1,0:T(8,128)}, f32[5,48,512]{2,1,0:T(8,128)}) custom-call(s32[3]{0:T(128)} %pad_add_fusion.1.scalars, bf16[128,1536]{1,0:T(8,128)(2,1)} %collective-permute-done.6.refs_0_, bf16[128,1536]{1,0:T(8,128)(2,1)} %copy-done.7, ...), custom_call_target="tpu_custom_call" | custom-call | tf_op jit(solution)/shard_map/pallas_call | solution.py:100
  106.7 17.1 %shard_map.288 = (bf16[256,1536]{1,0:T(8,128)(2,1)}, f32[256,128]{1,0:T(8,128)}, bf16[128,1536]{1,0:T(8,128)(2,1)}, bf16[128,16]{1,0:T(8,128)(2,1)}, f32[128,1536]{1,0:T(8,128)}, /*index=5*/f32[128,1]{1,0:T(8,128)}) custom-call(s32[3]{0:T(128)} %pad_add_fusion.1.scalars, bf16[128,1536]{1,0:T(8,128)(2,1)} %copy-done.3, bf16[128,1536]{1,0:T(8,128)(2,1)} %bitcast.33, ...), custom_call_target="tpu_custom_call" | custom-call | tf_op jit(solution)/shard_map/pallas_call | solution.py:100
  123.8 25.0 %shard_map.289 = (bf16[128,1664]{1,0:T(8,128)(2,1)}, bf16[128,1664]{1,0:T(8,128)(2,1)}, bf16[8,256,256]{2,1,0:T(8,128)(2,1)}) custom-call(s32[3]{0:T(128)} %pad_add_fusion.1.scalars, bf16[128,1536]{1,0:T(8,128)(2,1)} %collective-permute-done.10.refs_0_, bf16[128,1536]{1,0:T(8,128)(2,1)} %bitcast.37, bf16[256,1536]{1,0:T(8,128)(2,1)} %get-tuple-element.73.refs_2_, ...), custom_call_target="tpu_custom_call" | custom-call | tf_op jit(solution)/shard_map/pallas_call | solution.py:100
  148.8 3.7 %all-to-all-start = ((bf16[8,256,256]{2,1,0:T(8,128)(2,1)}), bf16[8,256,256]{2,1,0:T(8,128)(2,1)S(1)}, u32[]{:S(2)}, u32[]{:S(2)}) async-start(bf16[8,256,256]{2,1,0:T(8,128)(2,1)} %get-tuple-element.87), calls=%async_computation | async-start | bytes 2097152 | tf_op jit(solution)/shard_map/all_to_all | solution.py:930
  153.7 12.9 %collective-permute-done.11.refs_2_ = bf16[128,1664]{1,0:T(8,128)(2,1)} collective-permute-done((bf16[128,1664]{1,0:T(8,128)(2,1)S(1)}, bf16[128,1664]{1,0:T(8,128)(2,1)}, u32[]{:S(2)}, u32[]{:S(2)}) %collective-permute-start.11) | collective-permute-done | bytes 426016 | tf_op jit(solution)/shard_map/ppermute | solution.py:63
  166.6 15.4 %shard_map.290 = (f32[128,1536]{1,0:T(8,128)}, bf16[128,1536]{1,0:T(8,128)(2,1)}, bf16[128,16]{1,0:T(8,128)(2,1)}, bf16[128,1536]{1,0:T(8,128)(2,1)}, bf16[128,1...) custom-call(s32[3]{0:T(128)} %pad_add_fusion.1.scalars, ...), custom_call_target="tpu_custom_call" | custom-call | tf_op jit(solution)/shard_map/pallas_call | solution.py:100
  182.0 1.4 collective-permute-start.12
  183.4 5.0 %shard_map.291 = (bf16[8,24,256]{2,1,0:T(8,128)(2,1)}, bf16[8,24,256]{2,1,0:T(8,128)(2,1)}, bf16[8,24,256]{2,1,0:T(8,128)(2,1)}, bf16[8,24,256]{2,1,0:T(8,128)(2,1)}) custom-call(s32[3]{0:T(128)} %pad_add_fusion.1.scalars, bf16[128,1024]{1,0:T(8,128)(2,1)} %get-tuple-element.82.refs_0_, bf16[128,1024]{1,0:T(8,128)(2,1)} %get-tuple-element.83.refs_1_, ...), custom_call_target="tpu_custom_call" | custom-call | tf_op jit(solution)/shard_map/pallas_call | solution.py:100
  190.3 3.4 %collective-permute-start.15 = (bf16[8,24,256]{2,1,0:T(8,128)(2,1)}, bf16[8,24,256]{2,1,0:T(8,128)(2,1)S(1)}, u32[]{:S(2)}, u32[]{:S(2)}) collective-permute-start(bf16[8,24,256]{2,1,0:T(8,128)(2,1)} %get-tuple-element.96), channel_id=1, source_target_pairs={{0,3},{1,0},{2,1},{3,2},{4,7},{5,4},{6,5},{7,6},{8,11},{9,8},{10,9... | collective-permute-start | bytes 294920 | tf_op jit(solution)/shard_map/ppermute | solution.py:63
  194.4 6.0 %shard_map.292 = (f32[8,5,32,192]{3,2,1,0:T(8,128)}, f32[8,5,2,16,64]{4,3,2,1,0:T(8,128)}, f32[8,5,16,64]{3,2,1,0:T(8,128)}, f32[8,5,16,192]{3,2,1,0:T(8,128)}) custom-call(s32[3]{0:T(128)} %pad_add_fusion.1.scalars, bf16[8,256,256]{2,1,0:T(8,128)(2,1)} %copy-done, bf16[8,256,256]{2,1,0:T(8,128)(2,1)} %copy-done), custom_call_target="tpu_custom_call" | custom-call | tf_op jit(solution)/shard_map/pallas_call | solution.py:100
  200.4 9.2 %collective-permute-done.16 = bf16[8,24,256]{2,1,0:T(8,128)(2,1)S(1)} collective-permute-done((bf16[8,24,256]{2,1,0:T(8,128)(2,1)}, bf16[8,24,256]{2,1,0:T(8,128)(2,1)S(1)}, u32[]{:S(2)}, u32[]{:S(2)}) %collective-permute-start.16) | collective-permute-done | bytes 98336 | tf_op jit(solution)/shard_map/ppermute | solution.py:63
  210.4 3.6 %all-to-all-start.1 = ((bf16[8,24,256]{2,1,0:T(8,128)(2,1)}), bf16[8,24,256]{2,1,0:T(8,128)(2,1)S(1)}, u32[]{:S(2)}, u32[]{:S(2)}) async-start(bf16[8,24,256]{2,1,0:T(8,128)(2,1)} %add_convert_fusion), calls=%async_computation.1 | async-start | bytes 196608 | tf_op jit(solution)/shard_map/all_to_all | solution.py:945
  214.0 2.8 %collective-permute-done.13.refs_1_ = bf16[128,1024]{1,0:T(8,128)(2,1)S(1)} collective-permute-done((bf16[128,1024]{1,0:T(8,128)(2,1)S(1)}, bf16[128,1024]{1,0:T(8,128)(2,1)S(1)}, u32[]{:S(2)}, u32[]{:S(2)}) %collective-permute-start.13) | collective-permute-done | bytes 262176 | tf_op jit(solution)/shard_map/ppermute | solution.py:63
  216.8 2.4 all-to-all-done.1.got
  219.8 2.4 shard_map.293.refs_0_
  222.2 2.7 %collective-permute-start.18 = (bf16[8,24,256]{2,1,0:T(8,128)(2,1)}, bf16[8,24,256]{2,1,0:T(8,128)(2,1)S(1)}, u32[]{:S(2)}, u32[]{:S(2)}) collective-permute-start(bf16[8,24,256]{2,1,0:T(8,128)(2,1)} %shard_map.293.refs_0_), channel_id=1, source_target_pairs={{0,1},{1,2},{2,3},{3,0},{4,5},{5,6},{6,7},{7,4},{8,9},{9,10},{10,1... | collective-permute-start | bytes 294920 | tf_op jit(solution)/shard_map/ppermute | solution.py:58
  226.3 8.7 %shard_map.294 = f32[128,1536]{1,0:T(8,128)} custom-call(s32[3]{0:T(128)} %pad_add_fusion.1.scalars, bf16[128,1024]{1,0:T(8,128)(2,1)} %copy-done.11, bf16[128,1024]{1,0:T(8,128)(2,1)} %copy-done.13, bf16[128,1024]{1,0:T(8,128)(2,1)} %copy-done.12, bf16[128,1024]{1,0:T(8,128)(2,1)} %get-tuple-element.85.refs_3_, ...), custom_call_target="tpu_custom_call" | custom-call | tf_op jit(solution)/shard_map/pallas_call | solution.py:100
  236.3 2.8 %shard_map.295 = (f32[8,48,192]{2,1,0:T(8,128)}, f32[8,16,192]{2,1,0:T(8,128)}, f32[8,2,16,64]{3,2,1,0:T(8,128)}, f32[8,16,192]{2,1,0:T(8,128)}, f32[8,16,192]{2,1,0:T(8,128)}) custom-call(s32[3]{0:T(128)} %pad_add_fusion.1.scalars, bf16[8,24,256]{2,1,0:T(8,128)(2,1)} %shard_map.293.refs_0_, bf16[8,24,256]{2,1,0:T(8,128)(2,1)} %copy-done.14, ...), custom_call_target="tpu_custom_call" | custom-call | tf_op jit(solution)/shard_map/pallas_call | solution.py:100
  (87 shorter events, 16.5 us)
Async XLA Ops:
  0.6 26.6 %copy-start.20 = (s32[1,128,8]{1,2,0:T(8,128)S(1)}, s32[1,128,8]{1,2,0:T(8,128)}, u32[]{:S(2)}) copy-start(s32[1,128,8]{1,2,0:T(8,128)} %param.23) | copy-start | bytes 12292
  0.7 38.0 %copy-start.1 = (bf16[1,128,1536]{2,1,0:T(8,128)(2,1)S(1)}, bf16[1,128,1536]{2,1,0:T(8,128)(2,1)}, u32[]{:S(2)}) copy-start(bf16[1,128,1536]{2,1,0:T(8,128)(2,1)} %param.43) | copy-start | bytes 1179652
  0.7 14.4 %collective-permute-start = (bf16[128,1536]{1,0:T(8,128)(2,1)}, bf16[128,1536]{1,0:T(8,128)(2,1)S(1)}, u32[]{:S(2)}, u32[]{:S(2)}) collective-permute-start(bf16[128,1536]{1,0:T(8,128)(2,1)} %bitcast.31), channel_id=1, source_target_pairs={{0,1},{1,2},{2,3},{3,0},{4,5},{5,6},{6,7},{7,4},{8,9},{9,10},{10,1... | collective-permute-start | bytes 1179656 | tf_op jit(solution)/shard_map/ppermute | solution.py:886
  7.1 33.7 %copy-start.18 = (f32[1536]{0:T(1024)S(1)}, f32[1536]{0:T(1024)}, u32[]{:S(2)}) copy-start(f32[1536]{0:T(1024)} %param.27) | copy-start | bytes 18436
  7.1 34.3 %copy-start.19 = (f32[1536]{0:T(1024)S(1)}, f32[1536]{0:T(1024)}, u32[]{:S(2)}) copy-start(f32[1536]{0:T(1024)} %param.26) | copy-start | bytes 18436
  15.1 34.5 %copy-start.2 = (bf16[128,1536]{1,0:T(8,128)(2,1)}, bf16[128,1536]{1,0:T(8,128)(2,1)S(1)}, u32[]{:S(2)}) copy-start(bf16[128,1536]{1,0:T(8,128)(2,1)S(1)} %collective-permute-done.refs_0_) | copy-start | bytes 1179652
  15.1 12.1 %collective-permute-start.1 = (bf16[128,1536]{1,0:T(8,128)(2,1)S(1)}, bf16[128,1536]{1,0:T(8,128)(2,1)S(1)}, u32[]{:S(2)}, u32[]{:S(2)}) collective-permute-start(bf16[128,1536]{1,0:T(8,128)(2,1)S(1)} %collective-permute-done.refs_0_), channel_id=1, source_target_pairs={{0,1},{1,2},{2,3},{3,0},{4,5},{5,6},{6,7},{7,4},{8,9},{9,10},{10,1... | collective-permute-start | bytes 1179656 | tf_op jit(solution)/shard_map/ppermute | solution.py:888
  27.2 22.3 %copy-start.4 = (bf16[128,1536]{1,0:T(8,128)(2,1)}, bf16[128,1536]{1,0:T(8,128)(2,1)S(1)}, u32[]{:S(2)}) copy-start(bf16[128,1536]{1,0:T(8,128)(2,1)S(1)} %collective-permute-done.1.refs_1_) | copy-start | bytes 1179652
  27.2 11.4 %collective-permute-start.2 = (bf16[128,1536]{1,0:T(8,128)(2,1)S(1)}, bf16[128,1536]{1,0:T(8,128)(2,1)S(1)}, u32[]{:S(2)}, u32[]{:S(2)}) collective-permute-start(bf16[128,1536]{1,0:T(8,128)(2,1)S(1)} %collective-permute-done.1.refs_1_), channel_id=1, source_target_pairs={{0,1},{1,2},{2,3},{3,0},{4,5},{5,6},{6,7},{7,4},{8,9},{9,10},{10,1... | collective-permute-start | bytes 1179656 | tf_op jit(solution)/shard_map/ppermute | solution.py:891
  27.2 7.3 %collective-permute-start.5 = (s32[128,8]{0,1:T(8,128)S(1)}, s32[128,8]{0,1:T(8,128)S(1)}, u32[]{:S(2)}, u32[]{:S(2)}) collective-permute-start(s32[128,8]{0,1:T(8,128)S(1)} %bitcast.44), channel_id=1, source_target_pairs={{0,3},{1,0},{2,1},{3,2},{4,7},{5,4},{6,5},{7,6},{8,11},{9,8},{10,9... | collective-permute-start | bytes 12296 | tf_op jit(solution)/shard_map/ppermute | solution.py:58
  31.1 4.8 %collective-permute-start.4 = (s32[128,8]{0,1:T(8,128)S(1)}, s32[128,8]{0,1:T(8,128)S(1)}, u32[]{:S(2)}, u32[]{:S(2)}) collective-permute-start(s32[128,8]{0,1:T(8,128)S(1)} %bitcast.45), channel_id=1, source_target_pairs={{0,2},{1,3},{2,0},{3,1},{4,6},{5,7},{6,4},{7,5},{8,10},{9,11},{10,... | collective-permute-start | bytes 12296 | tf_op jit(solution)/shard_map/ppermute | solution.py:58
  31.1 7.6 %collective-permute-start.3 = (s32[128,8]{0,1:T(8,128)S(1)}, s32[128,8]{0,1:T(8,128)S(1)}, u32[]{:S(2)}, u32[]{:S(2)}) collective-permute-start(s32[128,8]{0,1:T(8,128)S(1)} %bitcast.46), channel_id=1, source_target_pairs={{0,1},{1,2},{2,3},{3,0},{4,5},{5,6},{6,7},{7,4},{8,9},{9,10},{10,1... | collective-permute-start | bytes 12296 | tf_op jit(solution)/shard_map/ppermute | solution.py:58
  38.6 41.3 %collective-permute-start.7 = (bf16[128,1536]{1,0:T(8,128)(2,1)S(1)}, bf16[128,1536]{1,0:T(8,128)(2,1)S(1)}, u32[]{:S(2)}, u32[]{:S(2)}) collective-permute-start(bf16[128,1536]{1,0:T(8,128)(2,1)S(1)} %bitcast.39), channel_id=1, source_target_pairs={{0,2},{1,3},{2,0},{3,1},{4,6},{5,7},{6,4},{7,5},{8,10},{9,11},{10,... | collective-permute-start | bytes 1179656 | tf_op jit(solution)/shard_map/ppermute | solution.py:58
  39.2 40.7 %collective-permute-start.6 = (bf16[128,1536]{1,0:T(8,128)(2,1)S(1)}, bf16[128,1536]{1,0:T(8,128)(2,1)}, u32[]{:S(2)}, u32[]{:S(2)}) collective-permute-start(bf16[128,1536]{1,0:T(8,128)(2,1)S(1)} %bitcast.40), channel_id=1, source_target_pairs={{0,1},{1,2},{2,3},{3,0},{4,5},{5,6},{6,7},{7,4},{8,9},{9,10},{10,1... | collective-permute-start | bytes 1179656 | tf_op jit(solution)/shard_map/ppermute | solution.py:58
  42.1 81.6 %collective-permute-start.10 = (bf16[128,1536]{1,0:T(8,128)(2,1)S(1)}, bf16[128,1536]{1,0:T(8,128)(2,1)}, u32[]{:S(2)}, u32[]{:S(2)}) collective-permute-start(bf16[128,1536]{1,0:T(8,128)(2,1)S(1)} %bitcast.41), channel_id=1, source_target_pairs={{0,3},{1,0},{2,1},{3,2},{4,7},{5,4},{6,5},{7,6},{8,11},{9,8},{10,9... | collective-permute-start | bytes 1179656 | tf_op jit(solution)/shard_map/ppermute | solution.py:58
  105.1 47.4 %collective-permute-start.9 = (bf16[128,1664]{1,0:T(8,128)(2,1)}, bf16[128,1664]{1,0:T(8,128)(2,1)S(1)}, u32[]{:S(2)}, u32[]{:S(2)}) collective-permute-start(bf16[128,1664]{1,0:T(8,128)(2,1)} %get-tuple-element.71), channel_id=1, source_target_pairs={{0,2},{1,3},{2,0},{3,1},{4,6},{5,7},{6,4},{7,5},{8,10},{9,11},{10,... | collective-permute-start | bytes 1277960 | tf_op jit(solution)/shard_map/ppermute | solution.py:63
  105.8 46.8 %collective-permute-start.8 = (bf16[128,1664]{1,0:T(8,128)(2,1)}, bf16[128,1664]{1,0:T(8,128)(2,1)S(1)}, u32[]{:S(2)}, u32[]{:S(2)}) collective-permute-start(bf16[128,1664]{1,0:T(8,128)(2,1)} %get-tuple-element.70), channel_id=1, source_target_pairs={{0,3},{1,0},{2,1},{3,2},{4,7},{5,4},{6,5},{7,6},{8,11},{9,8},{10,9... | collective-permute-start | bytes 1277960 | tf_op jit(solution)/shard_map/ppermute | solution.py:63
  148.8 34.6 %all-to-all-start = ((bf16[8,256,256]{2,1,0:T(8,128)(2,1)}), bf16[8,256,256]{2,1,0:T(8,128)(2,1)S(1)}, u32[]{:S(2)}, u32[]{:S(2)}) async-start(bf16[8,256,256]{2,1,0:T(8,128)(2,1)} %get-tuple-element.87), calls=%async_computation | async-start | bytes 2097152 | tf_op jit(solution)/shard_map/all_to_all | solution.py:930
  152.5 14.1 %collective-permute-start.11 = (bf16[128,1664]{1,0:T(8,128)(2,1)S(1)}, bf16[128,1664]{1,0:T(8,128)(2,1)}, u32[]{:S(2)}, u32[]{:S(2)}) collective-permute-start(bf16[128,1664]{1,0:T(8,128)(2,1)S(1)} %copy-done.21), channel_id=1, source_target_pairs={{0,1},{1,2},{2,3},{3,0},{4,5},{5,6},{6,7},{7,4},{8,9},{9,10},{10,1... | collective-permute-start | bytes 1277960 | tf_op jit(solution)/shard_map/ppermute | solution.py:63
  182.0 8.3 %collective-permute-start.12 = (bf16[128,1024]{1,0:T(8,128)(2,1)}, bf16[128,1024]{1,0:T(8,128)(2,1)S(1)}, u32[]{:S(2)}, u32[]{:S(2)}) collective-permute-start(bf16[128,1024]{1,0:T(8,128)(2,1)} %get-tuple-element.82.refs_0_), channel_id=1, source_target_pairs={{0,3},{1,0},{2,1},{3,2},{4,7},{5,4},{6,5},{7,6},{8,11},{9,8},{10,9... | collective-permute-start | bytes 786440 | tf_op jit(solution)/shard_map/ppermute | solution.py:63
  188.4 21.2 %copy-start.17 = (bf16[8,24,256]{2,1,0:T(8,128)(2,1)S(1)}, bf16[8,24,256]{2,1,0:T(8,128)(2,1)}, u32[]{:S(2)}) copy-start(bf16[8,24,256]{2,1,0:T(8,128)(2,1)} %get-tuple-element.99) | copy-start | bytes 294916
  188.4 21.2 %collective-permute-start.16 = (bf16[8,24,256]{2,1,0:T(8,128)(2,1)}, bf16[8,24,256]{2,1,0:T(8,128)(2,1)S(1)}, u32[]{:S(2)}, u32[]{:S(2)}) collective-permute-start(bf16[8,24,256]{2,1,0:T(8,128)(2,1)} %get-tuple-element.97), channel_id=1, source_target_pairs={{0,2},{1,3},{2,0},{3,1},{4,6},{5,7},{6,4},{7,5},{8,10},{9,11},{10,... | collective-permute-start | bytes 294920 | tf_op jit(solution)/shard_map/ppermute | solution.py:63
  188.5 21.2 %collective-permute-start.17 = (bf16[8,24,256]{2,1,0:T(8,128)(2,1)}, bf16[8,24,256]{2,1,0:T(8,128)(2,1)S(1)}, u32[]{:S(2)}, u32[]{:S(2)}) collective-permute-start(bf16[8,24,256]{2,1,0:T(8,128)(2,1)} %get-tuple-element.98), channel_id=1, source_target_pairs={{0,1},{1,2},{2,3},{3,0},{4,5},{5,6},{6,7},{7,4},{8,9},{9,10},{10,1... | collective-permute-start | bytes 294920 | tf_op jit(solution)/shard_map/ppermute | solution.py:63
  190.3 36.0 %copy-start.11 = (bf16[128,1024]{1,0:T(8,128)(2,1)}, bf16[128,1024]{1,0:T(8,128)(2,1)S(1)}, u32[]{:S(2)}) copy-start(bf16[128,1024]{1,0:T(8,128)(2,1)S(1)} %collective-permute-done.12.refs_0_) | copy-start | bytes 786436
  190.3 19.3 %collective-permute-start.15 = (bf16[8,24,256]{2,1,0:T(8,128)(2,1)}, bf16[8,24,256]{2,1,0:T(8,128)(2,1)S(1)}, u32[]{:S(2)}, u32[]{:S(2)}) collective-permute-start(bf16[8,24,256]{2,1,0:T(8,128)(2,1)} %get-tuple-element.96), channel_id=1, source_target_pairs={{0,3},{1,0},{2,1},{3,2},{4,7},{5,4},{6,5},{7,6},{8,11},{9,8},{10,9... | collective-permute-start | bytes 294920 | tf_op jit(solution)/shard_map/ppermute | solution.py:63
  193.7 16.6 %collective-permute-start.14 = (bf16[128,1024]{1,0:T(8,128)(2,1)S(1)}, bf16[128,1024]{1,0:T(8,128)(2,1)S(1)}, u32[]{:S(2)}, u32[]{:S(2)}) collective-permute-start(bf16[128,1024]{1,0:T(8,128)(2,1)S(1)} %copy-done.10), channel_id=1, source_target_pairs={{0,1},{1,2},{2,3},{3,0},{4,5},{5,6},{6,7},{7,4},{8,9},{9,10},{10,1... | collective-permute-start | bytes 786440 | tf_op jit(solution)/shard_map/ppermute | solution.py:63
  193.7 23.1 %collective-permute-start.13 = (bf16[128,1024]{1,0:T(8,128)(2,1)S(1)}, bf16[128,1024]{1,0:T(8,128)(2,1)S(1)}, u32[]{:S(2)}, u32[]{:S(2)}) collective-permute-start(bf16[128,1024]{1,0:T(8,128)(2,1)S(1)} %copy-done.9), channel_id=1, source_target_pairs={{0,2},{1,3},{2,0},{3,1},{4,6},{5,7},{6,4},{7,5},{8,10},{9,11},{10,... | collective-permute-start | bytes 786440 | tf_op jit(solution)/shard_map/ppermute | solution.py:63
  210.4 15.9 %copy-start.12 = (bf16[128,1024]{1,0:T(8,128)(2,1)}, bf16[128,1024]{1,0:T(8,128)(2,1)S(1)}, u32[]{:S(2)}) copy-start(bf16[128,1024]{1,0:T(8,128)(2,1)S(1)} %collective-permute-done.14.refs_2_) | copy-start | bytes 786436
  210.4 8.8 %all-to-all-start.1 = ((bf16[8,24,256]{2,1,0:T(8,128)(2,1)}), bf16[8,24,256]{2,1,0:T(8,128)(2,1)S(1)}, u32[]{:S(2)}, u32[]{:S(2)}) async-start(bf16[8,24,256]{2,1,0:T(8,128)(2,1)} %add_convert_fusion), calls=%async_computation.1 | async-start | bytes 196608 | tf_op jit(solution)/shard_map/all_to_all | solution.py:945
  222.2 12.8 %collective-permute-start.18 = (bf16[8,24,256]{2,1,0:T(8,128)(2,1)}, bf16[8,24,256]{2,1,0:T(8,128)(2,1)S(1)}, u32[]{:S(2)}, u32[]{:S(2)}) collective-permute-start(bf16[8,24,256]{2,1,0:T(8,128)(2,1)} %shard_map.293.refs_0_), channel_id=1, source_target_pairs={{0,1},{1,2},{2,3},{3,0},{4,5},{5,6},{6,7},{7,4},{8,9},{9,10},{10,1... | collective-permute-start | bytes 294920 | tf_op jit(solution)/shard_map/ppermute | solution.py:58
  224.8 10.2 %collective-permute-start.20 = (bf16[8,24,256]{2,1,0:T(8,128)(2,1)}, bf16[8,24,256]{2,1,0:T(8,128)(2,1)S(1)}, u32[]{:S(2)}, u32[]{:S(2)}) collective-permute-start(bf16[8,24,256]{2,1,0:T(8,128)(2,1)} %shard_map.293.refs_0_), channel_id=1, source_target_pairs={{0,3},{1,0},{2,1},{3,2},{4,7},{5,4},{6,5},{7,6},{8,11},{9,8},{10,9... | collective-permute-start | bytes 294920 | tf_op jit(solution)/shard_map/ppermute | solution.py:58
  226.0 9.0 %collective-permute-start.19 = (bf16[8,24,256]{2,1,0:T(8,128)(2,1)}, bf16[8,24,256]{2,1,0:T(8,128)(2,1)S(1)}, u32[]{:S(2)}, u32[]{:S(2)}) collective-permute-start(bf16[8,24,256]{2,1,0:T(8,128)(2,1)} %shard_map.293.refs_0_), channel_id=1, source_target_pairs={{0,2},{1,3},{2,0},{3,1},{4,6},{5,7},{6,4},{7,5},{8,10},{9,11},{10,... | collective-permute-start | bytes 294920 | tf_op jit(solution)/shard_map/ppermute | solution.py:58
  (13 other events, 81.4 us)

commit v2 on v1

v2 whole, which is shorter than its diff:
```python
import functools

import jax
import jax.numpy as jnp
from jax import lax
from jax.experimental import pallas as pl
from jax.experimental.pallas import tpu as pltpu
from jax.sharding import PartitionSpec as P

MODEL_WIDTH = 1536
QUERY_HEADS = 24
KEY_HEADS = 8
HEAD_SIZE = 64
EXPERT_HIDDEN = 512
TOPK = 8
ADAPTER_RANK = 16
ADAPTER_CHOICES = 8
QUERY_FEATURES = 1536
KEY_FEATURES = 512
LANES = 128
PAIRS = KEY_HEADS // 2
PAIR_QUERY = QUERY_FEATURES // PAIRS
GATE_LANES = 8
SENT = MODEL_WIDTH + LANES
COLUMNS = 512

EPS = 1e-05
ADAPTER_SCALE = 2.0
ROPE_BASE = 10000.0
MASKED = -1e30
SCALING = HEAD_SIZE ** (-0.5)
F32 = jnp.float32
BF16 = jnp.bfloat16
MIB = 1024 * 1024


def mm(left, right):
    return jnp.dot(left, right, preferred_element_type=F32)


def mm_nt(left, right):
    return lax.dot_general(left, right, (((1,), (1,)), ((), ())), preferred_element_type=F32)


def mm_tn(left, right):
    return lax.dot_general(left, right, (((0,), (0,)), ((), ())), preferred_element_type=F32)


def rotation(size, by):
    return [(i, (i + by) % size) for i in range(size)]


def after(value, *others):
    return lax.optimization_barrier((value, *others))[0]


def rotations(block, size):
    return [lax.ppermute(block, "ctx", rotation(size, j)) for j in range(1, size)] + [block]


def send_back(blocks, size, first):
    return [
        lax.ppermute(b, "ctx", rotation(size, -1 - j)) for j, b in enumerate(blocks, first)
    ]


def low_lanes(shape):
    return lax.broadcasted_iota(jnp.int32, shape, 1) % LANES < HEAD_SIZE


def turned(tile, cosine, sine):
    half = HEAD_SIZE // 2
    lane = lax.broadcasted_iota(jnp.int32, tile.shape, 1)
    other = jnp.where(
        lane % HEAD_SIZE < half, pltpu.roll(tile, LANES - half, 1), pltpu.roll(tile, half, 1)
    )
    return tile * cosine + other * sine


def variants(block, filler):
    tile, exchanged = lane_tiles(block)
    low = low_lanes(tile.shape)
    fill = jnp.full_like(tile, filler)
    return {
        (0, 0): jnp.where(low, tile, fill),
        (0, 1): jnp.where(low, fill, exchanged),
        (1, 0): jnp.where(low, exchanged, fill),
        (1, 1): jnp.where(low, fill, tile),
    }


def joined(refs):
    return jnp.concatenate([ref[...] for ref in refs], axis=0)


def lane_tiles(block):
    return [block[:, t * LANES : (t + 1) * LANES] for t in range(block.shape[1] // LANES)]


def call(kernel, scalars, grid, ins, outs, scratch, vmem=62, flops=0):
    return list(pl.pallas_call(
        kernel,
        grid_spec=pltpu.PrefetchScalarGridSpec(
            num_scalar_prefetch=1,
            grid=(grid,),
            in_specs=[pl.BlockSpec(b, m) for _, b, m in ins],
            out_specs=[pl.BlockSpec(b, m) for _, _, b, m in outs],
            scratch_shapes=scratch,
        ),
        out_shape=[jax.ShapeDtypeStruct(s, d) for s, d, _, _ in outs],
        compiler_params=pltpu.CompilerParams(
            vmem_limit_bytes=vmem * MIB, dimension_semantics=("arbitrary",)
        ),
        cost_estimate=pl.CostEstimate(
            flops=flops, bytes_accessed=0, transcendentals=0
        ),
    )(scalars, *[a for a, _, _ in ins]))


def whole(array):
    return (array, array.shape, lambda i, s, n=array.ndim: (0,) * n)


def whole_out(shape, dtype):
    return (shape, dtype, shape, lambda i, s, n=len(shape): (0,) * n)


def chosen_whole(table):
    rest = table.shape[1:]
    return (table, (1,) + rest, lambda i, s, n=len(rest): (s[0],) + (0,) * n)


def qkv_kernel(blocks, scalars, *refs):
    xs, refs = refs[:blocks], refs[blocks:]
    gain, down, query_w, kv_w, query_out, kv_out = refs[:6]
    cosines, sines, refs = refs[6 : 6 + blocks], refs[6 + blocks : 6 + 2 * blocks], refs[6 + 2 * blocks :]
    q_refs, k_refs, v_refs, normed_refs, lora_refs = [
        refs[n * blocks : (n + 1) * blocks] for n in range(5)
    ]
    normed, lora = refs[5 * blocks :]
    step = pl.program_id(0)
    q_steps = QUERY_FEATURES // COLUMNS
    own = xs[0].shape[0]
    r = ADAPTER_RANK

    @pl.when(step == 0)
    def _():
        for b, x_ref in enumerate(xs):
            x = x_ref[...].astype(F32)
            inv = lax.rsqrt(jnp.mean(x * x, axis=-1, keepdims=True) + EPS)
            rows = (x * inv * gain[...]).astype(BF16)
            normed[b * own : (b + 1) * own] = rows
            normed_refs[b][...] = rows
        lora[...] = mm_nt(normed[...], down[0]).astype(BF16)
        for b, lora_ref in enumerate(lora_refs):
            lora_ref[...] = lora[b * own : (b + 1) * own]

    def with_exchanged(out_ref, t, tile):
        out_ref[:, 2 * t * LANES : (2 * t + 1) * LANES] = tile.astype(BF16)
        out_ref[:, (2 * t + 1) * LANES : (2 * t + 2) * LANES] = pltpu.roll(
            tile, HEAD_SIZE, 1
        ).astype(BF16)

    @pl.when(step < q_steps)
    def _():
        pre = mm(normed[...], query_w[...])
        pre = pre + mm(lora[:, :r] * ADAPTER_SCALE, query_out[0])
        for b, q_ref in enumerate(q_refs):
            cos, sin = cosines[b][...] * SCALING, sines[b][...] * SCALING
            for t, tile in enumerate(lane_tiles(pre[b * own : (b + 1) * own])):
                q_ref[:, t * LANES : (t + 1) * LANES] = turned(tile, cos, sin).astype(BF16)

    @pl.when(step == q_steps)
    def _():
        pre = mm(normed[...], kv_w[...])
        pre = pre + mm(lora[:, r : 2 * r] * ADAPTER_SCALE, kv_out[0, 0])
        for b, k_ref in enumerate(k_refs):
            cos, sin = cosines[b][...], sines[b][...]
            for t, tile in enumerate(lane_tiles(pre[b * own : (b + 1) * own])):
                with_exchanged(k_ref, t, turned(tile, cos, sin))

    @pl.when(step == q_steps + 1)
    def _():
        pre = mm(normed[...], kv_w[...])
        pre = pre + mm(lora[:, 2 * r :] * ADAPTER_SCALE, kv_out[0, 1])
        for b, v_ref in enumerate(v_refs):
            for t, tile in enumerate(lane_tiles(pre[b * own : (b + 1) * own])):
                with_exchanged(v_ref, t, tile)


def qkv(scalars, xs, gain, down, query_w, kv_w, query_out, kv_out, cosine, sine, places):
    own = xs[0].shape[0]
    blocks = len(xs)
    q_steps = QUERY_FEATURES // COLUMNS
    last = q_steps - 1
    outs = call(
        functools.partial(qkv_kernel, blocks),
        scalars,
        q_steps + 2,
        [whole(x) for x in xs]
        + [
            whole(gain),
            chosen_whole(down),
            (query_w, (MODEL_WIDTH, COLUMNS), lambda i, s: (0, jnp.minimum(i, last))),
            (kv_w, (MODEL_WIDTH, COLUMNS), lambda i, s: (0, jnp.maximum(i - q_steps, 0))),
            (query_out, (1, ADAPTER_RANK, COLUMNS), lambda i, s: (s[0], 0, jnp.minimum(i, last))),
            chosen_whole(kv_out),
        ]
        + [
            (table, (own, LANES), lambda i, s, b=b: (b, 0))
            for table in (cosine, sine)
            for b in places
        ],
        [
            ((own, QUERY_FEATURES), BF16, (own, COLUMNS), lambda i, s: (0, jnp.minimum(i, last)))
            for _ in xs
        ]
        + [whole_out((own, 2 * KEY_FEATURES), BF16) for _ in xs + xs]
        + [whole_out((own, MODEL_WIDTH), BF16) for _ in xs]
        + [whole_out((own, 3 * ADAPTER_RANK), BF16) for _ in xs],
        [
            pltpu.VMEM((own * blocks, MODEL_WIDTH), BF16),
            pltpu.VMEM((own * blocks, 3 * ADAPTER_RANK), BF16),
        ],
        flops=10_000_000_000,
    )
    return [outs[n * blocks : (n + 1) * blocks] for n in range(5)]


def attend_kernel(blocks, scalars, *refs):
    xs, qs, ks, vs = [refs[n * blocks : (n + 1) * blocks] for n in range(4)]
    bias, proj_w, proj_in, proj_out, gain = refs[4 * blocks : 4 * blocks + 5]
    refs = refs[4 * blocks + 5 :]
    normed_refs, att_ref, lora_ref, middle_ref, inv_ref, total, rank_total = (
        refs[:2],
        *refs[2:],
    )
    step = pl.program_id(0)
    own = xs[0].shape[0]
    key_of, value_of = variants(joined(ks), 0), variants(joined(vs), 1)
    parts = []
    for n in range(blocks // 2):
        tiles = lane_tiles(joined(qs[2 * n : 2 * n + 2]))
        rows = slice(2 * n * own, (2 * n + 2) * own)
        heads = []
        for h in range(6):
            at = (h // 3, h % 2)
            scores = mm_nt(tiles[h // 2], key_of[at]) + bias[rows]
            shifted = jnp.exp(scores - jnp.max(scores, axis=-1, keepdims=True)).astype(BF16)
            sums = mm(shifted, value_of[at])
            heads.append(sums / pltpu.roll(sums, HEAD_SIZE, 1))
        low = low_lanes(heads[0].shape)
        parts.append(
            jnp.concatenate(
                [jnp.where(low, heads[2 * t], heads[2 * t + 1]) for t in range(3)], axis=1
            ).astype(BF16)
        )
    attended = jnp.concatenate(parts, axis=0)
    att_ref[...] = attended
    part = mm(attended, proj_w[...])
    rank_part = mm_nt(attended, proj_in[0])

    @pl.when(step == 0)
    def _():
        total[...] = part
        rank_total[...] = rank_part

    @pl.when(step > 0)
    def _():
        total[...] += part
        rank_total[...] += rank_part

    @pl.when(step == PAIRS - 1)
    def _():
        lora_out = rank_total[...].astype(BF16)
        branch = total[...] + mm(lora_out * ADAPTER_SCALE, proj_out[0])
        for b, x_ref in enumerate(xs):
            middle = x_ref[...].astype(F32) + branch[b * own : (b + 1) * own]
            inv = lax.rsqrt(jnp.mean(middle * middle, axis=-1, keepdims=True) + EPS)
            at = b % (blocks // 2)
            normed_refs[b // (blocks // 2)][at * own : (at + 1) * own] = (
                middle * inv * gain[...]
            ).astype(BF16)
            if b == blocks - 1:
                middle_ref[...] = middle
                inv_ref[...] = inv
                lora_ref[...] = lora_out[b * own : (b + 1) * own]


def attend(scalars, xs, qs, ks, vs, bias, proj_w, proj_in, proj_out, gain):
    own = xs[0].shape[0]
    rows = own * len(xs)
    return call(
        functools.partial(attend_kernel, len(xs)),
        scalars,
        PAIRS,
        [whole(x) for x in xs]
        + [(q, (own, PAIR_QUERY), lambda i, s: (0, i)) for q in qs]
        + [(k, (own, 2 * LANES), lambda i, s: (0, i)) for k in ks + vs]
        + [
            whole(bias),
            (proj_w, (PAIR_QUERY, MODEL_WIDTH), lambda i, s: (i, 0)),
            (proj_in, (1, ADAPTER_RANK, PAIR_QUERY), lambda i, s: (s[0], 0, i)),
            chosen_whole(proj_out),
            whole(gain),
        ],
        [
            whole_out((rows // 2, MODEL_WIDTH), BF16),
            whole_out((rows // 2, MODEL_WIDTH), BF16),
            ((rows, QUERY_FEATURES), BF16, (rows, PAIR_QUERY), lambda i, s: (0, i)),
            whole_out((own, ADAPTER_RANK), BF16),
            whole_out((own, MODEL_WIDTH), F32),
            whole_out((own, 1), F32),
        ],
        [pltpu.VMEM((rows, MODEL_WIDTH), F32), pltpu.VMEM((rows, ADAPTER_RANK), F32)],
    )


def expert_kernel(blocks, parts, first, scalars, *refs):
    cots, refs = refs[:blocks], refs[blocks:]
    x_ref, router, up_w, down_w, up_in, up_out, down_in, down_out = refs[:8]
    refs = refs[8:]
    if not first:
        (wide_old, narrow_old), refs = refs[:2], refs[2:]
    rows_refs, refs = refs[:blocks], refs[blocks:]
    if first:
        (wide_ref, narrow_ref), refs = refs[:2], refs[2:]
    else:
        (send_ref, gates_ref), refs = refs[:2], refs[2:]
    gates, cot_all, total, gg_all, rank_in_all, cot_mid_all, grad_rank_all, gated_all = refs
    step = pl.program_id(0)
    here = up_in.shape[1]
    own = cots[0].shape[0]
    r = ADAPTER_RANK
    up_in_rows = up_in[0].reshape(here * 2 * r, MODEL_WIDTH)
    x = x_ref[...]

    @pl.when(step == 0)
    def _():
        for b, cot in enumerate(cots):
            cot_all[b * own : (b + 1) * own] = cot[:, :MODEL_WIDTH]
        mask = jnp.concatenate([cot[:, MODEL_WIDTH:] for cot in cots], axis=0).astype(F32) > 0.0
        chosen = jnp.where(mask, mm_nt(x, router[...]), MASKED)
        shifted = jnp.exp(chosen - jnp.max(chosen, axis=-1, keepdims=True))
        shifted = jnp.where(mask, shifted, 0.0)
        gates[...] = shifted / jnp.sum(shifted, axis=-1, keepdims=True)
        if not first:
            gates_ref[...] = gates[-own:]
        gg_all[...] = jnp.zeros_like(gg_all)
        rank_in = mm_nt(x, up_in_rows).astype(BF16) * ADAPTER_SCALE
        down_out_rows = down_out[0].reshape(here * r, MODEL_WIDTH)
        cot_mid = ADAPTER_SCALE * mm_nt(cot_all[...], down_out_rows)
        for e in range(here):
            rank_in_all[e] = rank_in[:, e * 2 * r : (e + 1) * 2 * r]
            cot_mid_all[e] = cot_mid[:, e * r : (e + 1) * r]

    cot = cot_all[...]
    lane = lax.broadcasted_iota(jnp.int32, gates.shape, 1)
    gate_of = jnp.sum(
        jnp.where(lane == scalars[2] * here + step, gates[...], 0.0), axis=1, keepdims=True
    )
    rank_in2 = rank_in_all[step]
    none = jnp.zeros((r, EXPERT_HIDDEN), BF16)
    out_map = jnp.concatenate(
        [
            jnp.concatenate([up_out[0, 0, 0], none], axis=1),
            jnp.concatenate([none, up_out[0, 0, 1]], axis=1),
        ],
        axis=0,
    )
    pre = mm(x, up_w[0]) + mm(rank_in2, out_map)
    gate_pre, up_pre = pre[:, :EXPERT_HIDDEN], pre[:, EXPERT_HIDDEN:]
    cot_hidden = mm_nt(cot, down_w[0])
    sig = 0.5 * jnp.tanh(0.5 * gate_pre) + 0.5
    silu = gate_pre * sig
    hidden_wide = silu * up_pre
    hidden = hidden_wide.astype(BF16)
    rank_mid = mm_nt(hidden, down_in[0, 0]).astype(BF16).astype(F32)
    cot_mid = cot_mid_all[step]
    gate_grad = jnp.sum(hidden.astype(F32) * cot_hidden, axis=1, keepdims=True) + jnp.sum(
        rank_mid * cot_mid, axis=1, keepdims=True
    )
    gg_lane = lax.broadcasted_iota(jnp.int32, gg_all.shape, 1)
    gg_all[...] += jnp.where(gg_lane == step, gate_grad, 0.0)
    grad_rank_mid = (gate_of * cot_mid).astype(BF16)
    grad_hidden = gate_of * cot_hidden + mm(grad_rank_mid, down_in[0, 0])
    grad_gate = (grad_hidden * up_pre * (sig + silu * (1.0 - sig))).astype(BF16)
    grad_up = (grad_hidden * silu).astype(BF16)
    grad_both = jnp.concatenate([grad_gate, grad_up], axis=1)
    grad_rank_all[step] = (ADAPTER_SCALE * mm_nt(grad_both, out_map)).astype(BF16)
    gated_all[step] = (ADAPTER_SCALE * gate_of * rank_mid).astype(BF16)
    part = mm_nt(grad_both, up_w[0])

    @pl.when(step == 0)
    def _():
        total[...] = part

    @pl.when(step > 0)
    def _():
        total[...] += part

    both = mm_tn(
        jnp.concatenate([rank_in2, grad_rank_mid], axis=1),
        jnp.concatenate([grad_both, hidden], axis=1),
    )
    narrow = jnp.concatenate(
        [
            both[i * r : (i + 1) * r, i * EXPERT_HIDDEN : (i + 1) * EXPERT_HIDDEN]
            for i in range(3)
        ],
        axis=0,
    )
    w, v = MODEL_WIDTH // parts, EXPERT_HIDDEN // parts
    if first:
        narrow_ref[0] = narrow
    else:
        narrow = (narrow + narrow_old[0]).astype(BF16)
        at = pl.ds(pl.multiple_of(step * (3 * r), 16), 3 * r)
        for p in range(parts):
            send_ref[p, at, w:] = narrow[:, p * v : (p + 1) * v]

    @pl.when(step == here - 1)
    def _():
        grad_rank = jnp.concatenate([grad_rank_all[e] for e in range(here)], axis=1)
        gated = jnp.concatenate([gated_all[e] for e in range(here)], axis=1)
        rows = total[...] + mm(grad_rank, up_in_rows)
        high = gg_all[...].astype(BF16).astype(F32)
        both = high + pltpu.roll(gg_all[...] - high, GATE_LANES, 1)
        for b, rows_ref in enumerate(rows_refs):
            at = slice(b * own, (b + 1) * own)
            rows_ref[:, :MODEL_WIDTH] = rows[at].astype(BF16)
            rows_ref[:, MODEL_WIDTH:] = both[at].astype(BF16)
        wide = jnp.concatenate([mm_tn(grad_rank, x), mm_tn(gated, cot)], axis=0)
        if first:
            wide_ref[...] = wide
        else:
            wide = (wide + wide_old[...]).astype(BF16)
            rows = here * 3 * r
            chosen = jnp.full((16, w + v), scalars[0], jnp.int32).astype(F32).astype(BF16)
            for p in range(parts):
                send_ref[p, :rows, :w] = wide[:, p * w : (p + 1) * w]
                send_ref[p, rows:] = chosen


def experts(scalars, parts, cots, x, router, tables, before):
    up_w, down_w, up_in, up_out, down_in, down_out = tables
    own = cots[0].shape[0]
    rows = own * len(cots)
    here = up_w.shape[0]
    r = ADAPTER_RANK
    per_expert = lambda i, s: (i, 0, 0)
    ins = [whole(c) for c in cots] + [
        whole(x),
        whole(router),
        (up_w, (1,) + up_w.shape[1:], per_expert),
        (down_w, (1,) + down_w.shape[1:], per_expert),
        chosen_whole(up_in),
        (up_out, (1, 1) + up_out.shape[2:], lambda i, s: (s[0], i, 0, 0, 0)),
        (down_in, (1, 1) + down_in.shape[2:], lambda i, s: (s[0], i, 0, 0)),
        chosen_whole(down_out),
    ]
    outs = [whole_out((own, SENT), BF16) for _ in cots]
    if before is None:
        outs.append(whole_out((here * 3 * r, MODEL_WIDTH), F32))
        outs.append(((here, 3 * r, EXPERT_HIDDEN), F32, (1, 3 * r, EXPERT_HIDDEN), per_expert))
    else:
        wide, narrow = before
        ins += [whole(wide), (narrow, (1,) + narrow.shape[1:], per_expert)]
        width = (MODEL_WIDTH + EXPERT_HIDDEN) // parts
        outs.append(whole_out((parts, here * 3 * r + 16, width), BF16))
        outs.append(whole_out((own, LANES), F32))
    return call(
        functools.partial(expert_kernel, len(cots), parts, before is None),
        scalars,
        here,
        ins,
        outs,
        [
            pltpu.VMEM((rows, LANES), F32),
            pltpu.VMEM((rows, MODEL_WIDTH), BF16),
            pltpu.VMEM((rows, MODEL_WIDTH), F32),
            pltpu.VMEM((rows, LANES), F32),
            pltpu.VMEM((here, rows, 2 * r), BF16),
            pltpu.VMEM((here, rows, r), F32),
            pltpu.VMEM((here, rows, 2 * r), BF16),
            pltpu.VMEM((here, rows, r), BF16),
        ],
    )


def middle_kernel(blocks, here, scalars, *refs):
    parts, ks, vs, refs = refs[:blocks], refs[blocks : 2 * blocks], refs[2 * blocks : 3 * blocks], refs[3 * blocks :]
    gates, router, middle_ref, inv_ref, gain, cot = refs[:6]
    proj_w, proj_in, proj_out, q_ref, bias, cosine, sine = refs[6:13]
    grad_middle, branch_ref, lora_ref, gq_ref = refs[13:17]
    gkv_refs, grad_att = refs[17:-1], refs[-1]
    step = pl.program_id(0)
    own = q_ref.shape[0]

    @pl.when(step == 0)
    def _():
        gates_own = gates[...]
        lane = lax.broadcasted_iota(jnp.int32, gates_own.shape, 1)
        gg = jnp.zeros_like(gates_own)
        for j, part in enumerate(parts):
            both = part[:, MODEL_WIDTH:].astype(F32)
            both = both + pltpu.roll(both, LANES - GATE_LANES, 1)
            both = jnp.where(lane < here, both, 0.0)
            gg = gg + pltpu.roll(both, lax.rem(scalars[2] + 1 + j, blocks) * here, 1)
        chosen = gates_own * (gg - jnp.sum(gates_own * gg, axis=-1, keepdims=True))
        grad = mm(chosen.astype(BF16), router[...])
        for part in parts:
            grad = grad + part[:, :MODEL_WIDTH].astype(F32)
        scaled = grad * gain[...]
        middle, inv = middle_ref[...], inv_ref[...]
        grad = (
            cot[...].astype(F32)
            + inv * scaled
            - middle * (inv * inv * inv) * jnp.mean(scaled * middle, axis=-1, keepdims=True)
        )
        grad_middle[...] = grad
        branch = grad.astype(BF16)
        branch_ref[...] = branch
        lora = (ADAPTER_SCALE * mm_nt(branch, proj_out[0])).astype(BF16)
        lora_ref[...] = lora
        attended = (mm_nt(branch, proj_w[...]) + mm(lora, proj_in[0])).astype(BF16)
        for i in range(PAIRS):
            grad_att[i] = attended[:, i * PAIR_QUERY : (i + 1) * PAIR_QUERY]

    key_of, value_of = variants(joined(ks), 0), variants(joined(vs), 0)
    queries, grads = lane_tiles(q_ref[...]), lane_tiles(grad_att[step])
    low = low_lanes(queries[0].shape)
    none = jnp.zeros_like(queries[0])
    probs_of, scores_of, query_of, grad_of = [], [], [], []
    for h in range(6):
        at = (h // 3, h % 2)
        scores = mm_nt(key_of[at], queries[h // 2]) + bias[...]
        shifted = jnp.exp(scores - jnp.max(scores, axis=0, keepdims=True))
        probs = shifted * (1.0 / jnp.sum(shifted, axis=0, keepdims=True))
        grad_probs = mm_nt(value_of[at], grads[h // 2])
        grad_scores = probs * (grad_probs - jnp.sum(probs * grad_probs, axis=0, keepdims=True))
        probs_of.append(probs.astype(BF16))
        scores_of.append(grad_scores.astype(BF16))
        inside = low if h % 2 == 0 else jnp.logical_not(low)
        query_of.append(jnp.where(inside, queries[h // 2], none))
        grad_of.append(jnp.where(inside, grads[h // 2], none))

    def summed_over(lefts, rights):
        def over(chosen):
            return mm(
                jnp.concatenate([lefts[h] for h in chosen], axis=1),
                jnp.concatenate([rights[h] for h in chosen], axis=0),
            )

        return over([0, 2, 3, 5]) + pltpu.roll(over([1, 4]), HEAD_SIZE, 1)

    grad_key = summed_over(scores_of, query_of)
    grad_key = turned(grad_key, cosine[...], -sine[...]).astype(BF16)
    grad_value = summed_over(probs_of, grad_of).astype(BF16)
    for b, gkv_ref in enumerate(gkv_refs):
        gkv_ref[:, :LANES] = grad_key[b * own : (b + 1) * own]
        gkv_ref[:, LANES:] = grad_value[b * own : (b + 1) * own]
    key_t = {at: key_of[at].astype(F32).T.astype(BF16) for at in key_of}
    cos, sin = cosine[-own:], -sine[-own:]
    for t in range(3):
        pair = (2 * t, 2 * t + 1)
        tile = mm(
            jnp.concatenate([key_t[h // 3, h % 2] for h in pair], axis=1),
            jnp.concatenate([scores_of[h] for h in pair], axis=0),
        )
        gq_ref[:, t * LANES : (t + 1) * LANES] = turned(SCALING * tile.T, cos, sin).astype(BF16)


def middle_backward(
    scalars, parts, here, gates, router, middle, inv, gain, cot, proj_w, proj_in, proj_out,
    q, ks, vs, bias_t, cosine, sine,
):
    own = q.shape[0]
    return call(
        functools.partial(middle_kernel, len(parts), here),
        scalars,
        PAIRS,
        [whole(part) for part in parts]
        + [(k, (own, 2 * LANES), lambda i, s: (0, i)) for k in ks + vs]
        + [
            whole(gates),
            whole(router),
            whole(middle),
            whole(inv),
            whole(gain),
            (cot, (own, MODEL_WIDTH), lambda i, s: (0, 0)),
            whole(proj_w),
            chosen_whole(proj_in),
            chosen_whole(proj_out),
            (q, (own, PAIR_QUERY), lambda i, s: (0, i)),
            whole(bias_t),
            whole(cosine),
            whole(sine),
        ],
        [
            whole_out((own, MODEL_WIDTH), F32),
            whole_out((own, MODEL_WIDTH), BF16),
            whole_out((own, ADAPTER_RANK), BF16),
            ((own, QUERY_FEATURES), BF16, (own, PAIR_QUERY), lambda i, s: (0, i)),
        ]
        + [
            ((own, 2 * KEY_FEATURES), BF16, (own, 2 * LANES), lambda i, s: (0, i))
            for _ in parts
        ],
        [pltpu.VMEM((PAIRS, own, PAIR_QUERY), BF16)],
        flops=20_000_000_000,
    )


def key_and_value(columns):
    return jnp.concatenate(columns[0::2], axis=1), jnp.concatenate(columns[1::2], axis=1)


def package_sizes(parts, blocks):
    width = (MODEL_WIDTH + KEY_FEATURES) // parts
    tiles = -(-width // LANES)
    return width, tiles, parts * tiles + blocks + 1


def partial_kernel(parts, blocks, scalars, *refs):
    gkvs, lora_in = refs[:blocks], refs[blocks : 2 * blocks]
    gq, query_out, kv_out, lora_out, branch, grad_lora, package = refs[2 * blocks :]
    own = gq.shape[0]
    r = ADAPTER_RANK
    width, tiles, entries = package_sizes(parts, blocks)
    low2 = joined(lora_in) * ADAPTER_SCALE
    gk, gv = key_and_value(lane_tiles(joined(gkvs)))
    wide = jnp.concatenate(
        [mm_tn(low2[-own:, :r], gq[...]), mm_tn(lora_out[...] * ADAPTER_SCALE, branch[...])], axis=0
    ).astype(BF16)
    narrow = jnp.concatenate(
        [mm_tn(low2[:, r : 2 * r], gk), mm_tn(low2[:, 2 * r :], gv)], axis=0
    ).astype(BF16)
    w, v = MODEL_WIDTH // parts, KEY_FEATURES // parts
    for p in range(parts):
        block = [wide[:, p * w : (p + 1) * w], narrow[:, p * v : (p + 1) * v]]
        if width < tiles * LANES:
            block.append(jnp.zeros((2 * r, tiles * LANES - width), BF16))
        for t, tile in enumerate(lane_tiles(jnp.concatenate(block, axis=1))):
            package[p * tiles + t] = tile
    grad_kv = jnp.concatenate([mm_nt(kv_out[0, 0], gk), mm_nt(kv_out[0, 1], gv)], axis=0)
    grad_kv = (ADAPTER_SCALE * grad_kv).astype(BF16)
    for j in range(blocks):
        at = parts * tiles + lax.rem(scalars[2] + 2 * blocks - 1 - j, blocks)
        package[at] = grad_kv[:, j * own : (j + 1) * own]
    grad_q = (ADAPTER_SCALE * mm_nt(query_out[0], gq[...])).astype(BF16)
    grad_out = grad_lora[...].astype(F32).T.astype(BF16)
    package[entries - 1] = jnp.concatenate([grad_q, grad_out], axis=0)


def partials(scalars, parts, gkvs, lora_in, gq, query_out, kv_out, lora_out, branch, grad_lora):
    blocks = len(gkvs)
    entries = package_sizes(parts, blocks)[2]
    return call(
        functools.partial(partial_kernel, parts, blocks),
        scalars,
        1,
        [whole(g) for g in list(gkvs) + lora_in]
        + [
            whole(gq),
            chosen_whole(query_out),
            chosen_whole(kv_out),
            whole(lora_out),
            whole(branch),
            whole(grad_lora),
        ],
        [whole_out((entries, 2 * ADAPTER_RANK, LANES), BF16)],
        [],
    )[0]


def sequence_kernel(parts, blocks, scalars, *refs):
    packages, normed = refs[:blocks], refs[blocks : 2 * blocks]
    attended, send, total = refs[2 * blocks :]
    r = ADAPTER_RANK
    width, tiles, entries = package_sizes(parts, blocks)
    total[...] = functools.reduce(lambda a, b: a + b, [p[...].astype(F32) for p in packages])
    ends = [p[entries - 1] for p in packages]
    order = [lax.rem(scalars[2] + 2 * blocks - 1 - j, blocks) for j in range(blocks)]
    grad_kv = [total[parts * tiles + rank].astype(BF16) for rank in order]
    grad_in = jnp.concatenate(
        [jnp.concatenate([end[:r] for end in ends], axis=1), jnp.concatenate(grad_kv, axis=1)],
        axis=0,
    )
    grad_out = jnp.concatenate([end[r:] for end in ends], axis=1)
    wide = jnp.concatenate(
        [mm(grad_in, joined(normed)), mm(grad_out, attended[...])], axis=0
    ).astype(BF16)
    w = MODEL_WIDTH // parts
    for p in range(parts):
        block = jnp.concatenate([total[p * tiles + t] for t in range(tiles)], axis=1).astype(BF16)
        send[p, : 4 * r, :w] = wide[:, p * w : (p + 1) * w]
        send[p, 4 * r :, :w] = block[:, :w]
        send[p, : 2 * r, w:] = block[:, w:width]
        send[p, 2 * r :, w:] = jnp.zeros((4 * r, width - w), BF16)


def sequence_sums(scalars, parts, packages, normed, attended):
    blocks = len(packages)
    width, _, entries = package_sizes(parts, blocks)
    return call(
        functools.partial(sequence_kernel, parts, blocks),
        scalars,
        1,
        [whole(p) for p in packages + normed] + [whole(attended)],
        [whole_out((parts, 6 * ADAPTER_RANK, width), BF16)],
        [pltpu.VMEM((entries, 2 * ADAPTER_RANK, LANES), F32)],
    )[0]


def summed(received, choices, adapter, senders):
    total = None
    for n in range(senders):
        rows = jnp.where(choices[n, :1, :1].astype(F32) == adapter, received(n), 0.0)
        total = rows if total is None else total + rows
    return total


def expert_sum_kernel(wide, scalars, got, choices, up_in, up_out, down_in, down_out):
    adapter = pl.program_id(0).astype(F32)
    total = summed(lambda n: got[n].astype(F32), choices, adapter, got.shape[0])
    r = ADAPTER_RANK
    here = up_in.shape[1]
    for e in range(here):
        up_in[0, e] = total[e * 2 * r : (e + 1) * 2 * r, :wide]
        down_out[0, e] = total[(2 * here + e) * r : (2 * here + e + 1) * r, :wide]
        rows = total[e * 3 * r : (e + 1) * 3 * r]
        up_out[0, e, 0] = rows[:r, wide:]
        up_out[0, e, 1] = rows[r : 2 * r, wide:]
        down_in[0, e] = rows[2 * r :, wide:]


def expert_sum(scalars, got, here):
    parts, _, width = got.shape
    r = ADAPTER_RANK
    rows = here * 3 * r
    wide, narrow = MODEL_WIDTH // parts, EXPERT_HIDDEN // parts

    def out(*shape):
        return ((ADAPTER_CHOICES,) + shape, F32, (1,) + shape, lambda i, s: (i,) + (0,) * len(shape))

    return call(
        functools.partial(expert_sum_kernel, wide),
        scalars,
        ADAPTER_CHOICES,
        [
            (got, (parts, rows, width), lambda i, s: (0, 0, 0)),
            (got, (parts, 16, width), lambda i, s: (0, rows // 16, 0)),
        ],
        [
            out(here, 2 * r, wide),
            out(here, 2, r, narrow),
            out(here, r, narrow),
            out(here, r, wide),
        ],
        [],
    )


def attention_sum_kernel(wide, scalars, got, choices, qkv_in, query_out, kv_out, proj_in, proj_out):
    adapter = pl.program_id(0).astype(F32)
    total = summed(lambda n: got[n].astype(F32), choices, adapter, got.shape[0])
    r = ADAPTER_RANK
    qkv_in[0] = total[: 3 * r, :wide]
    proj_in[0] = total[3 * r : 4 * r, :wide]
    query_out[0] = total[4 * r : 5 * r, :wide]
    proj_out[0] = total[5 * r :, :wide]
    kv_out[0, 0] = total[:r, wide:]
    kv_out[0, 1] = total[r : 2 * r, wide:]


def attention_sum(scalars, got, expert_got, rows):
    parts, _, width = got.shape
    r = ADAPTER_RANK
    wide, narrow = MODEL_WIDTH // parts, KEY_FEATURES // parts

    def out(*shape):
        return ((ADAPTER_CHOICES,) + shape, F32, (1,) + shape, lambda i, s: (i,) + (0,) * len(shape))

    return call(
        functools.partial(attention_sum_kernel, wide),
        scalars,
        ADAPTER_CHOICES,
        [whole(got), (expert_got, (parts, 16, width), lambda i, s: (0, rows // 16, 0))],
        [
            out(3 * r, wide),
            out(r, wide),
            out(2, r, narrow),
            out(r, wide),
            out(r, wide),
        ],
        [],
    )


def query_kernel(scalars, gq, query_w, out_ref):
    out_ref[...] = mm_nt(gq[...], query_w[...])


def query_backward(scalars, gq, query_w):
    steps = 3
    return call(
        query_kernel,
        scalars,
        steps,
        [whole(gq), (query_w, (MODEL_WIDTH // steps, QUERY_FEATURES), lambda i, s: (i, 0))],
        [(gq.shape, F32, (gq.shape[0], MODEL_WIDTH // steps), lambda i, s: (0, i))],
        [],
    )[0]


def input_kernel(blocks, scalars, *refs):
    gkvs, refs = refs[:blocks], refs[blocks:]
    gq, first, kv_w, query_out, kv_out, down, x_ref, gain, grad_middle, out_ref = refs
    grad_kv = functools.reduce(lambda a, b: a + b, [g[...].astype(F32) for g in gkvs])
    grad_k, grad_v = key_and_value(lane_tiles(grad_kv.astype(BF16)))
    lora = jnp.concatenate(
        [
            mm_nt(gq[...], query_out[0]),
            mm_nt(grad_k, kv_out[0, 0]),
            mm_nt(grad_v, kv_out[0, 1]),
        ],
        axis=1,
    )
    lora = (ADAPTER_SCALE * lora).astype(BF16)
    grad = (
        first[...]
        + mm_nt(grad_k, kv_w[:, :KEY_FEATURES])
        + mm_nt(grad_v, kv_w[:, KEY_FEATURES:])
        + mm(lora, down[0])
    )
    x = x_ref[...].astype(F32)
    inv = lax.rsqrt(jnp.mean(x * x, axis=-1, keepdims=True) + EPS)
    scaled = grad * gain[...]
    out_ref[...] = (
        grad_middle[...]
        + inv * scaled
        - x * (inv * inv * inv) * jnp.mean(scaled * x, axis=-1, keepdims=True)
    )


def input_backward(scalars, gkvs, gq, first, kv_w, query_out, kv_out, down, x, gain, grad_middle):
    own = x.shape[0]
    return call(
        functools.partial(input_kernel, len(gkvs)),
        scalars,
        1,
        [whole(g) for g in gkvs]
        + [
            whole(gq),
            whole(first),
            whole(kv_w),
            chosen_whole(query_out),
            chosen_whole(kv_out),
            chosen_whole(down),
            whole(x),
            whole(gain),
            whole(grad_middle),
        ],
        [whole_out((own, MODEL_WIDTH), F32)],
        [],
        flops=20_000_000_000,
    )[0]


def shards(
    layer_input_rows,
    routes,
    prefix,
    sequence_adapter_index,
    attention_norm_gain,
    expert_norm_gain,
    query_weight,
    key_value_weight,
    projection_weight,
    router_weight,
    gate_up_weight,
    down_weight,
    adapter_query_key_value_input,
    adapter_query_output,
    adapter_key_value_output,
    adapter_projection_input,
    adapter_projection_output,
    adapter_gate_up_input,
    adapter_gate_up_output,
    adapter_down_input,
    adapter_down_output,
    cotangent,
):
    ctx_size = lax.axis_size("ctx")
    dp_size = lax.axis_size("dp")
    rank = lax.axis_index("ctx")
    own = layer_input_rows.shape[1]
    span = own * ctx_size
    experts_here = gate_up_weight.shape[0]
    experts_all = experts_here * ctx_size
    half = ctx_size // 2
    scalars = jnp.stack([sequence_adapter_index[0], prefix[0], rank]).astype(jnp.int32)
    gain_attn = attention_norm_gain[None]
    gain_ffn = expert_norm_gain[None]

    order = (rank - 1 - jnp.arange(ctx_size, dtype=jnp.int32)) % ctx_size
    positions = (order[:, None] * own + jnp.arange(own, dtype=jnp.int32)[None, :]).reshape(-1)
    size = HEAD_SIZE // 2
    frequency = ROPE_BASE ** (-jnp.arange(size, dtype=F32) / size)
    angles = positions.astype(F32)[:, None] * frequency[None, :]
    cosine, sine = jnp.cos(angles), jnp.sin(angles)
    cosine = jnp.concatenate([cosine] * 4, axis=1)
    sine = jnp.concatenate([-sine, sine] * 2, axis=1)
    allowed = (positions[None, :] <= positions[:, None]) | (positions[None, :] < prefix[0])
    bias = jnp.where(allowed, 0.0, MASKED).astype(F32)
    bias_t = bias[-own:].T
    qkv_in_t = adapter_query_key_value_input.transpose(0, 2, 1)
    proj_in_t = adapter_projection_input.transpose(0, 2, 1)
    router_t = jnp.pad(router_weight.T, ((0, LANES - experts_all), (0, 0)))

    expert_ids = jnp.arange(LANES, dtype=jnp.int32)
    named = jnp.any(routes[0][:, :, None] == expert_ids[None, None, :], axis=1).astype(BF16)
    cot_own = jnp.concatenate([cotangent[0], named], axis=1)
    x_own = layer_input_rows[0]
    step = functools.partial(lax.ppermute, axis_name="ctx", perm=rotation(ctx_size, 1))
    inputs = [step(x_own)]
    inputs.append(step(after(inputs[0], cosine, sine, bias, bias_t, router_t, scalars, cot_own)))
    while len(inputs) < ctx_size - 1:
        inputs.append(step(inputs[-1]))
    inputs.append(x_own)
    cots = None
    q, k, v, normed, lora_in = [], [], [], [], []
    now = scalars
    for some in ([ctx_size - 1] + list(range(ctx_size - 2)), [ctx_size - 2]):
        made = qkv(
            now, [inputs[b] for b in some], gain_attn, qkv_in_t, query_weight, key_value_weight,
            adapter_query_output, adapter_key_value_output, cosine, sine, some,
        )
        for all_of, some_of in zip((q, k, v, normed, lora_in), made):
            all_of += some_of
        now = after(scalars, q[0])
        if cots is None:
            cots = rotations(after(cot_own, q[0]), ctx_size)
    q, k, v, normed, lora_in = [a[1:] + a[:1] for a in (q, k, v, normed, lora_in)]
    tables = (
        gate_up_weight,
        down_weight,
        adapter_gate_up_input.transpose(0, 1, 3, 2),
        adapter_gate_up_output,
        adapter_down_input.transpose(0, 1, 3, 2),
        adapter_down_output,
    )

    normed_first, normed_last, attended, lora_out, middle, inv = attend(
        scalars, inputs, q, k, v, bias, projection_weight, proj_in_t, adapter_projection_output,
        gain_ffn,
    )
    *rows_first, wide, narrow = experts(
        scalars, dp_size, cots[:half], normed_first, router_t, tables, None
    )
    *rows_last, send, gates = experts(
        scalars, dp_size, cots[half:], normed_last, router_t, tables, (wide, narrow)
    )

    got = send_back(rows_first, ctx_size, 0)
    rows_last[0] = after(rows_last[0], *got)
    got += send_back(rows_last[:-1], ctx_size, half) + rows_last[-1:]
    grad_middle, branch, grad_lora, gq, *gkvs = middle_backward(
        scalars, got, experts_here, gates, router_t, middle, inv, gain_ffn, cot_own,
        projection_weight, proj_in_t, adapter_projection_output, q[-1], k, v, bias_t, cosine, sine,
    )
    expert_got = lax.all_to_all(send, "dp", 0, 0, tiled=True)
    package = partials(
        scalars, dp_size, gkvs, lora_in, after(gq, expert_got), adapter_query_output, adapter_key_value_output,
        lora_out, branch, grad_lora,
    )
    gkvs = list(gkvs)
    gkvs[0] = send_back(gkvs[:1], ctx_size, 0)[0]
    packages = rotations(after(package, gkvs[0]), ctx_size)
    first = query_backward(scalars, after(gq, package), query_weight)
    up_in, up_out, down_in, down_out = expert_sum(
        scalars, after(expert_got, first), experts_here
    )
    later = [after(g, first, up_in, *packages[:-1]) for g in gkvs[1:-1]]
    gkvs[1:-1] = send_back(later, ctx_size, 1)
    packages[1] = after(packages[1], first, up_in)
    attention_send = sequence_sums(scalars, dp_size, packages, normed, attended)
    attention_got = lax.all_to_all(attention_send, "dp", 0, 0, tiled=True)
    grad_inputs = input_backward(
        scalars, gkvs, after(gq, attention_send), first, key_value_weight, adapter_query_output,
        adapter_key_value_output, qkv_in_t, x_own, gain_attn, grad_middle,
    )
    attention_got = after(attention_got, grad_inputs)
    qkv_in, query_out, kv_out, proj_in, proj_out = attention_sum(
        scalars, attention_got, expert_got, experts_here * 3 * ADAPTER_RANK
    )
    return (
        grad_inputs[None],
        qkv_in.transpose(0, 2, 1),
        query_out,
        kv_out,
        proj_in.transpose(0, 2, 1),
        proj_out,
        up_in.transpose(0, 1, 3, 2),
        up_out,
        down_in.transpose(0, 1, 3, 2),
        down_out,
    )


def solution(mesh):
    placed = (
        P("dp", "ctx", None),
        P("dp", "ctx", None),
        P("dp"),
        P("dp"),
        P(),
        P(),
        P(),
        P(),
        P(),
        P(),
        P("ctx", None, None),
        P("ctx", None, None),
        P(),
        P(),
        P(),
        P(),
        P(),
        P(None, "ctx", None, None),
        P(None, "ctx", None, None, None),
        P(None, "ctx", None, None),
        P(None, "ctx", None, None),
        P("dp", "ctx", None),
    )
    return jax.shard_map(
        shards,
        mesh=mesh,
        in_specs=placed,
        out_specs=(
            P("dp", "ctx", None),
            P(None, "dp", None),
            P(None, None, "dp"),
            P(None, None, None, "dp"),
            P(None, "dp", None),
            P(None, None, "dp"),
            P(None, "ctx", "dp", None),
            P(None, "ctx", None, None, "dp"),
            P(None, "ctx", "dp", None),
            P(None, "ctx", None, "dp"),
        ),
        check_vma=False,
    )
```

time: 240 us -> 219 us (0.912)
  waiting for transfers between devices: 51.6 us -> 31.9 us
  Pallas kernels: 137 us -> 145 us
  starting transfers between devices: 32.8 us -> 27.2 us
  other arithmetic: 7.61 us -> 3.55 us
    pallas_call x11 -> x12, Pallas kernels: 137 us -> 145 us  [call(): pl.pallas_call(kernel, grid_spec=pltpu.PrefetchScalarGridSpec(num_scalar_...]
    ppermute x9 -> x6, waiting for transfers between devices: 7.02 us -> 0.02 us  [rotations(): lax.ppermute(block, 'ctx', rotation(size, j))]
    ppermute x9 -> x6, waiting for transfers between devices: 25.8 us -> 18.9 us  [send_back(): lax.ppermute(b, 'ctx', rotation(size, -1 - j))]
    ppermute x9 -> x6, starting transfers between devices: 13.1 us -> 9.28 us  [rotations(): lax.ppermute(block, 'ctx', rotation(size, j))]
    reduce_or x1, other arithmetic: 2.9 us -> 0.26 us  [shards(): jnp.any(routes[0][:, :, None] == expert_ids[None, None, :], axis=1)]
    ppermute x1, waiting for transfers between devices: 12.1 us -> 9.71 us  [shards(): step(after(inputs[0], cosine, sine, bias, bias_t, router_t, scalars, cot_...]
    ppermute x9 -> x6, starting transfers between devices: 9.33 us -> 7.85 us  [send_back(): lax.ppermute(b, 'ctx', rotation(size, -1 - j))]
  transfers between devices with their start and end apart: 23 -> 17, of which waited for: 10 -> 5; matrix products, arithmetic and copies ran while one was open for 5% -> 4% of each run, Pallas kernels for 55% -> 64%
where the time goes in v2:
time: 219 us; the launch traced here: 218 us
  Pallas kernels  145 us (66%)
  waiting for transfers between devices  31.9 us (15%)
  starting transfers between devices  27.2 us (12%)
  local copies, waits for them, and re-layouts  8.93 us (4%)
  other arithmetic  3.55 us (2%)
  between operations  2.32 us (1%)
    pallas_call x12, Pallas kernels, call(): pl.pallas_call(kernel, grid_spec=pltpu.PrefetchScalarGridSpec(num_scalar_...  145 us
    ppermute x6, waiting for transfers between devices, send_back(): lax.ppermute(b, 'ctx', rotation(size, -1 - j))  18.9 us
    ppermute x1, waiting for transfers between devices, shards(): step(after(inputs[0], cosine, sine, bias, bias_t, router_t, scalars, cot_...  9.71 us
    ppermute x6, starting transfers between devices, rotations(): lax.ppermute(block, 'ctx', rotation(size, j))  9.28 us
    ppermute x6, starting transfers between devices, send_back(): lax.ppermute(b, 'ctx', rotation(size, -1 - j))  7.85 us
  transfers between devices with their start and end apart: 17, of which 5 were waited for; matrix products, arithmetic and copies ran while one was open for 4% of the time, Pallas kernels for 64%

profile of v2, /device:TPU:0, one launch (start us, length us, event | category | flops | bytes accessed | tf_op | source)
XLA Modules:
  0.0 218.5 jit_solution(2060079134852270674)
XLA Ops:
  0.7 3.1 %collective-permute-start = (bf16[128,1536]{1,0:T(8,128)(2,1)}, bf16[128,1536]{1,0:T(8,128)(2,1)S(1)}, u32[]{:S(2)}, u32[]{:S(2)}) collective-permute-start(bf16[128,1536]{1,0:T(8,128)(2,1)} %bitcast.30), channel_id=1, source_target_pairs={{0,1},{1,2},{2,3},{3,0},{4,5},{5,6},{6,7},{7,4},{8,9},{9,10},{10,1... | collective-permute-start | bytes 1179656 | tf_op jit(solution)/shard_map/ppermute | solution.py:927
  5.0 0.8 copy.36
  7.3 1.0 fusion.1
  8.9 1.7 pad.4.refs_3_.refs_13_
  10.6 1.3 pad_maximum_fusion.1
  11.9 3.2 %collective-permute-done.refs_1_.refs_0_ = bf16[128,1536]{1,0:T(8,128)(2,1)S(1)} collective-permute-done((bf16[128,1536]{1,0:T(8,128)(2,1)}, bf16[128,1536]{1,0:T(8,128)(2,1)S(1)}, u32[]{:S(2)}, u32[]{:S(2)}) %collective-permute-start) | collective-permute-done | bytes 393248 | tf_op jit(solution)/shard_map/ppermute | solution.py:927
  15.1 1.3 copy.38.refs_16_
  17.6 9.7 %collective-permute-done.1.refs_2_.refs_1_ = bf16[128,1536]{1,0:T(8,128)(2,1)} collective-permute-done((bf16[128,1536]{1,0:T(8,128)(2,1)S(1)}, bf16[128,1536]{1,0:T(8,128)(2,1)}, u32[]{:S(2)}, u32[]{:S(2)}) %collective-permute-start.1) | collective-permute-done | bytes 393248 | tf_op jit(solution)/shard_map/ppermute | solution.py:928
  27.3 12.2 %shard_map.285 = (bf16[128,1536]{1,0:T(8,128)(2,1)}, bf16[128,1536]{1,0:T(8,128)(2,1)}, bf16[128,1536]{1,0:T(8,128)(2,1)}, bf16[128,1024]{1,0:T(8,128)(2,1)}, bf...) custom-call(s32[3]{0:T(128)} %pad_add_fusion.scalars, ...), custom_call_target="tpu_custom_call" | custom-call | flops 10000000000 | tf_op jit(solution)/shard_map/pallas_call | solution.py:101
  39.6 4.4 %collective-permute-start.3 = (bf16[128,1664]{1,0:T(8,128)(2,1)S(1)}, bf16[128,1664]{1,0:T(8,128)(2,1)S(1)}, u32[]{:S(2)}, u32[]{:S(2)}) collective-permute-start(bf16[128,1664]{1,0:T(8,128)(2,1)S(1)} %pad_maximum_fusion.refs_1_.refs_17_), channel_id=1, source_target_pairs={{0,2},{1,3},{2,0},{3,1},{4,6},{5,7},{6,4},{7,5},{8,10},{9,11},{10,... | collective-permute-start | bytes 1277960 | tf_op jit(solution)/shard_map/ppermute | solution.py:58
  44.0 8.7 %shard_map.286 = (bf16[128,1536]{1,0:T(8,128)(2,1)}, bf16[128,1024]{1,0:T(8,128)(2,1)}, bf16[128,1024]{1,0:T(8,128)(2,1)}, bf16[128,1536]{1,0:T(8,128)(2,1)}, bf16[128,48]{1,0:T(8,128)(2,1)}) custom-call(s32[3]{0:T(128)} %pad_add_fusion.scalars, bf16[128,1536]{1,0:T(8,128)(2,1)} %collective-permute-done.4.refs_0_.refs_2_, ...), custom_call_target="tpu_custom_call" | custom-call | flops 10000000000 | tf_op jit(solution)/shard_map/pallas_call | solution.py:101
  52.7 27.0 %shard_map.287 = (bf16[256,1536]{1,0:T(8,128)(2,1)}, bf16[256,1536]{1,0:T(8,128)(2,1)}, bf16[512,1536]{1,0:T(8,128)(2,1)}, bf16[128,16]{1,0:T(8,128)(2,1)}, f32[128,1536]{1,0:T(8,128)}, /*index=5*/f32[128,1]{1,0:T(8,128)}) custom-call(s32[3]{0:T(128)} %pad_add_fusion.scalars, bf16[128,1536]{1,0:T(8,128)(2,1)} %copy-done.6, ...), custom_call_target="tpu_custom_call" | custom-call | tf_op jit(solution)/shard_map/pallas_call | solution.py:101
  80.7 24.6 %shard_map.288 = (bf16[128,1664]{1,0:T(8,128)(2,1)}, bf16[128,1664]{1,0:T(8,128)(2,1)}, f32[240,1536]{1,0:T(8,128)}, f32[5,48,512]{2,1,0:T(8,128)}) custom-call(s32[3]{0:T(128)} %pad_add_fusion.scalars, bf16[128,1664]{1,0:T(8,128)(2,1)} %copy-done.4, bf16[128,1664]{1,0:T(8,128)(2,1)} %copy-done.5, bf16[256,1536]{1,0:T(8,128)(2,1)} %get-tuple-element.89.refs_2_, ...), custom_call_target="tpu_custom_call" | custom-call | tf_op jit(solution)/shard_map/pallas_call | solution.py:101
  105.3 1.7 collective-permute-start.5
  107.0 2.0 collective-permute-start.6
  109.0 0.8 copy-done.3
  109.8 25.3 %shard_map.289 = (bf16[128,1664]{1,0:T(8,128)(2,1)}, bf16[128,1664]{1,0:T(8,128)(2,1)}, bf16[8,256,256]{2,1,0:T(8,128)(2,1)}, f32[128,128]{1,0:T(8,128)}) custom-call(s32[3]{0:T(128)} %pad_add_fusion.scalars, bf16[128,1664]{1,0:T(8,128)(2,1)} %copy-done.3, bf16[128,1664]{1,0:T(8,128)(2,1)} %copy-done.1, bf16[256,1536]{1,0:T(8,128)(2,1)} %get-tuple-element.92.refs_2_, ...), custom_call_target="tpu_custom_call" | custom-call | tf_op jit(solution)/shard_map/pallas_call | solution.py:101
  135.3 3.6 %all-to-all-start = ((bf16[8,256,256]{2,1,0:T(8,128)(2,1)}), bf16[8,256,256]{2,1,0:T(8,128)(2,1)S(1)}, u32[]{:S(2)}, u32[]{:S(2)}) async-start(bf16[8,256,256]{2,1,0:T(8,128)(2,1)} %get-tuple-element.110), calls=%async_computation | async-start | bytes 2097152 | tf_op jit(solution)/shard_map/all_to_all | solution.py:973
  138.8 8.0 %collective-permute-done.8.refs_2_ = bf16[128,1664]{1,0:T(8,128)(2,1)} collective-permute-done((bf16[128,1664]{1,0:T(8,128)(2,1)}, bf16[128,1664]{1,0:T(8,128)(2,1)}, u32[]{:S(2)}, u32[]{:S(2)}) %collective-permute-start.8) | collective-permute-done | bytes 426016 | tf_op jit(solution)/shard_map/ppermute | solution.py:63
  146.9 16.0 %shard_map.290 = (f32[128,1536]{1,0:T(8,128)}, bf16[128,1536]{1,0:T(8,128)(2,1)}, bf16[128,16]{1,0:T(8,128)(2,1)}, bf16[128,1536]{1,0:T(8,128)(2,1)}, bf16[128,1...) custom-call(s32[3]{0:T(128)} %pad_add_fusion.scalars, ...), custom_call_target="tpu_custom_call" | custom-call | flops 20000000000 | tf_op jit(solution)/shard_map/pallas_call | solution.py:101
  162.9 1.8 collective-permute-start.9
  164.7 3.8 %shard_map.291.refs_3_ = bf16[21,32,128]{2,1,0:T(8,128)(2,1)} custom-call(s32[3]{0:T(128)} %pad_add_fusion.scalars, bf16[128,1024]{1,0:T(8,128)(2,1)} %get-tuple-element.101.refs_0_, bf16[128,1024]{1,0:T(8,128)(2,1)} %get-tuple-element.119.refs_1_, bf16[128,1024]{1,0:T(8,128)(2,1)} %get-tuple-element.120.refs_2_, ...), custom_call_target="tpu_custom_call" | custom-call | tf_op jit(solution)/shard_map/pallas_call | solution.py:101
  168.4 2.4 %collective-permute-done.9.refs_0_ = bf16[128,1024]{1,0:T(8,128)(2,1)} collective-permute-done((bf16[128,1024]{1,0:T(8,128)(2,1)}, bf16[128,1024]{1,0:T(8,128)(2,1)}, u32[]{:S(2)}, u32[]{:S(2)}) %collective-permute-start.9) | collective-permute-done | bytes 262176 | tf_op jit(solution)/shard_map/ppermute | solution.py:63
  170.9 4.8 %collective-permute-start.11 = (bf16[21,32,128]{2,1,0:T(8,128)(2,1)}, bf16[21,32,128]{2,1,0:T(8,128)(2,1)S(1)}, u32[]{:S(2)}, u32[]{:S(2)}) collective-permute-start(bf16[21,32,128]{2,1,0:T(8,128)(2,1)} %shard_map.291.refs_3_), channel_id=1, source_target_pairs={{0,2},{1,3},{2,0},{3,1},{4,6},{5,7},{6,4},{7,5},{8,10},{9,11},{10,... | collective-permute-start | bytes 516104 | tf_op jit(solution)/shard_map/ppermute | solution.py:58
  175.7 5.7 %shard_map.292.refs_5_ = f32[128,1536]{1,0:T(8,128)} custom-call(s32[3]{0:T(128)} %pad_add_fusion.scalars, bf16[128,1536]{1,0:T(8,128)(2,1)} %get-tuple-element.127.refs_8_.gq.refs_4_, bf16[1536,1536]{1,0:T(8,128)(2,1)} %query_w.1), custom_call_target="tpu_custom_call" | custom-call | tf_op jit(solution)/shard_map/pallas_call | solution.py:101
  181.4 6.0 %shard_map.293 = (f32[8,5,32,192]{3,2,1,0:T(8,128)}, f32[8,5,2,16,64]{4,3,2,1,0:T(8,128)}, f32[8,5,16,64]{3,2,1,0:T(8,128)}, f32[8,5,16,192]{3,2,1,0:T(8,128)}) custom-call(s32[3]{0:T(128)} %pad_add_fusion.scalars, bf16[8,256,256]{2,1,0:T(8,128)(2,1)} %copy-done, bf16[8,256,256]{2,1,0:T(8,128)(2,1)} %copy-done), custom_call_target="tpu_custom_call" | custom-call | tf_op jit(solution)/shard_map/pallas_call | solution.py:101
  187.4 1.5 collective-permute-start.13
  189.6 4.2 %shard_map.294 = bf16[8,96,256]{2,1,0:T(8,128)(2,1)} custom-call(s32[3]{0:T(128)} %pad_add_fusion.scalars, bf16[21,32,128]{2,1,0:T(8,128)(2,1)} %copy-done.10, bf16[21,32,128]{2,1,0:T(8,128)(2,1)} %copy-done.11, bf16[21,32,128]{2,1,0:T(8,128)(2,1)} %collective-permute-done.12.refs_2_, bf16[21,32,128]{2,1,0:T(8,128)(2,1)} %shard_map.291.refs_3_, ...), custom_call_target="tpu_custom_call" | custom-call | tf_op jit(solution)/shard_map/pallas_call | solution.py:101
  193.9 3.5 %all-to-all-start.1 = ((bf16[8,96,256]{2,1,0:T(8,128)(2,1)}), bf16[8,96,256]{2,1,0:T(8,128)(2,1)S(1)}, u32[]{:S(2)}, u32[]{:S(2)}) async-start(bf16[8,96,256]{2,1,0:T(8,128)(2,1)} %shard_map.294), calls=%async_computation.1 | async-start | bytes 786432 | tf_op jit(solution)/shard_map/all_to_all | solution.py:989
  197.3 8.5 %collective-permute-done.13.refs_1_ = bf16[128,1024]{1,0:T(8,128)(2,1)S(1)} collective-permute-done((bf16[128,1024]{1,0:T(8,128)(2,1)S(1)}, bf16[128,1024]{1,0:T(8,128)(2,1)S(1)}, u32[]{:S(2)}, u32[]{:S(2)}) %collective-permute-start.13) | collective-permute-done | bytes 262176 | tf_op jit(solution)/shard_map/ppermute | solution.py:63
  206.6 6.1 %shard_map.295 = f32[128,1536]{1,0:T(8,128)} custom-call(s32[3]{0:T(128)} %pad_add_fusion.scalars, bf16[128,1024]{1,0:T(8,128)(2,1)} %collective-permute-done.9.refs_0_, bf16[128,1024]{1,0:T(8,128)(2,1)} %copy-done.16, bf16[128,1024]{1,0:T(8,128)(2,1)} %copy-done.17, bf16[128,1024]{1,0:T(8,128)(2,1)} %get-tuple-element.105.refs_3_, ...), custom_call_target="tpu_custom_call" | custom-call | flops 20000000000 | tf_op jit(solution)/shard_map/pallas_call | solution.py:101
  213.5 4.8 %shard_map.296 = (f32[8,48,192]{2,1,0:T(8,128)}, f32[8,16,192]{2,1,0:T(8,128)}, f32[8,2,16,64]{3,2,1,0:T(8,128)}, f32[8,16,192]{2,1,0:T(8,128)}, f32[8,16,192]{2,1,0:T(8,128)}) custom-call(s32[3]{0:T(128)} %pad_add_fusion.scalars, bf16[8,96,256]{2,1,0:T(8,128)(2,1)} %copy-done.2, bf16[8,256,256]{2,1,0:T(8,128)(2,1)} %copy-done), custom_call_target="tpu_custom_call" | custom-call | tf_op jit(solution)/shard_map/pallas_call | solution.py:101
  (67 shorter events, 6.6 us)
Async XLA Ops:
  0.6 11.2 %copy-start.7 = (bf16[1,128,1536]{2,1,0:T(8,128)(2,1)S(1)}, bf16[1,128,1536]{2,1,0:T(8,128)(2,1)}, u32[]{:S(2)}) copy-start(bf16[1,128,1536]{2,1,0:T(8,128)(2,1)} %param.43) | copy-start | bytes 1179652
  0.7 14.4 %collective-permute-start = (bf16[128,1536]{1,0:T(8,128)(2,1)}, bf16[128,1536]{1,0:T(8,128)(2,1)S(1)}, u32[]{:S(2)}, u32[]{:S(2)}) collective-permute-start(bf16[128,1536]{1,0:T(8,128)(2,1)} %bitcast.30), channel_id=1, source_target_pairs={{0,1},{1,2},{2,3},{3,0},{4,5},{5,6},{6,7},{7,4},{8,9},{9,10},{10,1... | collective-permute-start | bytes 1179656 | tf_op jit(solution)/shard_map/ppermute | solution.py:927
  6.5 9.9 %copy-start.12 = (f32[1536]{0:T(1024)S(1)}, f32[1536]{0:T(1024)}, u32[]{:S(2)}) copy-start(f32[1536]{0:T(1024)} %param.26) | copy-start | bytes 18436
  6.5 10.5 %copy-start.13 = (f32[1536]{0:T(1024)S(1)}, f32[1536]{0:T(1024)}, u32[]{:S(2)}) copy-start(f32[1536]{0:T(1024)} %param.27) | copy-start | bytes 18436
  11.9 32.1 %copy-start.1 = (bf16[128,1664]{1,0:T(8,128)(2,1)}, bf16[128,1664]{1,0:T(8,128)(2,1)S(1)}, u32[]{:S(2)}) copy-start(bf16[128,1664]{1,0:T(8,128)(2,1)S(1)} %pad_maximum_fusion.refs_1_.refs_17_) | copy-start | bytes 1277956
  15.1 12.2 %copy-start.6 = (bf16[128,1536]{1,0:T(8,128)(2,1)}, bf16[128,1536]{1,0:T(8,128)(2,1)S(1)}, u32[]{:S(2)}) copy-start(bf16[128,1536]{1,0:T(8,128)(2,1)S(1)} %collective-permute-done.refs_1_.refs_0_) | copy-start | bytes 1179652
  15.1 12.2 %collective-permute-start.1 = (bf16[128,1536]{1,0:T(8,128)(2,1)S(1)}, bf16[128,1536]{1,0:T(8,128)(2,1)}, u32[]{:S(2)}, u32[]{:S(2)}) collective-permute-start(bf16[128,1536]{1,0:T(8,128)(2,1)S(1)} %collective-permute-done.refs_1_.refs_0_), channel_id=1, source_target_pairs={{0,1},{1,2},{2,3},{3,0},{4,5},{5,6},{6,7},{7,4},{8,9},{9,10},{10,1... | collective-permute-start | bytes 1179656 | tf_op jit(solution)/shard_map/ppermute | solution.py:928
  27.3 16.7 %collective-permute-start.4 = (bf16[128,1536]{1,0:T(8,128)(2,1)}, bf16[128,1536]{1,0:T(8,128)(2,1)}, u32[]{:S(2)}, u32[]{:S(2)}) collective-permute-start(bf16[128,1536]{1,0:T(8,128)(2,1)} %collective-permute-done.1.refs_2_.refs_1_), channel_id=1, source_target_pairs={{0,1},{1,2},{2,3},{3,0},{4,5},{5,6},{6,7},{7,4},{8,9},{9,10},{10,1... | collective-permute-start | bytes 1179656 | tf_op jit(solution)/shard_map/ppermute | solution.py:930
  39.5 40.2 %collective-permute-start.2 = (bf16[128,1664]{1,0:T(8,128)(2,1)S(1)}, bf16[128,1664]{1,0:T(8,128)(2,1)S(1)}, u32[]{:S(2)}, u32[]{:S(2)}) collective-permute-start(bf16[128,1664]{1,0:T(8,128)(2,1)S(1)} %pad_maximum_fusion.refs_1_.refs_17_), channel_id=1, source_target_pairs={{0,1},{1,2},{2,3},{3,0},{4,5},{5,6},{6,7},{7,4},{8,9},{9,10},{10,1... | collective-permute-start | bytes 1277960 | tf_op jit(solution)/shard_map/ppermute | solution.py:58
  39.6 40.2 %collective-permute-start.3 = (bf16[128,1664]{1,0:T(8,128)(2,1)S(1)}, bf16[128,1664]{1,0:T(8,128)(2,1)S(1)}, u32[]{:S(2)}, u32[]{:S(2)}) collective-permute-start(bf16[128,1664]{1,0:T(8,128)(2,1)S(1)} %pad_maximum_fusion.refs_1_.refs_17_), channel_id=1, source_target_pairs={{0,2},{1,3},{2,0},{3,1},{4,6},{5,7},{6,4},{7,5},{8,10},{9,11},{10,... | collective-permute-start | bytes 1277960 | tf_op jit(solution)/shard_map/ppermute | solution.py:58
  44.0 65.0 %collective-permute-start.7 = (bf16[128,1664]{1,0:T(8,128)(2,1)S(1)}, bf16[128,1664]{1,0:T(8,128)(2,1)S(1)}, u32[]{:S(2)}, u32[]{:S(2)}) collective-permute-start(bf16[128,1664]{1,0:T(8,128)(2,1)S(1)} %pad_maximum_fusion.refs_1_.refs_17_), channel_id=1, source_target_pairs={{0,3},{1,0},{2,1},{3,2},{4,7},{5,4},{6,5},{7,6},{8,11},{9,8},{10,9... | collective-permute-start | bytes 1277960 | tf_op jit(solution)/shard_map/ppermute | solution.py:58
  79.8 0.8 copy-start.4
  79.8 0.9 copy-start.5
  105.3 29.8 %collective-permute-start.5 = (bf16[128,1664]{1,0:T(8,128)(2,1)}, bf16[128,1664]{1,0:T(8,128)(2,1)S(1)}, u32[]{:S(2)}, u32[]{:S(2)}) collective-permute-start(bf16[128,1664]{1,0:T(8,128)(2,1)} %get-tuple-element.90), channel_id=1, source_target_pairs={{0,3},{1,0},{2,1},{3,2},{4,7},{5,4},{6,5},{7,6},{8,11},{9,8},{10,9... | collective-permute-start | bytes 1277960 | tf_op jit(solution)/shard_map/ppermute | solution.py:63
  107.0 28.1 %collective-permute-start.6 = (bf16[128,1664]{1,0:T(8,128)(2,1)}, bf16[128,1664]{1,0:T(8,128)(2,1)S(1)}, u32[]{:S(2)}, u32[]{:S(2)}) collective-permute-start(bf16[128,1664]{1,0:T(8,128)(2,1)} %get-tuple-element.91), channel_id=1, source_target_pairs={{0,2},{1,3},{2,0},{3,1},{4,6},{5,7},{6,4},{7,5},{8,10},{9,11},{10,... | collective-permute-start | bytes 1277960 | tf_op jit(solution)/shard_map/ppermute | solution.py:63
  135.1 11.8 %copy-start.14 = (bf16[128,1664]{1,0:T(8,128)(2,1)}, bf16[128,1664]{1,0:T(8,128)(2,1)S(1)}, u32[]{:S(2)}) copy-start(bf16[128,1664]{1,0:T(8,128)(2,1)S(1)} %collective-permute-done.5.refs_0_) | copy-start | bytes 1277956
  135.1 11.7 %copy-start.15 = (bf16[128,1664]{1,0:T(8,128)(2,1)}, bf16[128,1664]{1,0:T(8,128)(2,1)S(1)}, u32[]{:S(2)}) copy-start(bf16[128,1664]{1,0:T(8,128)(2,1)S(1)} %collective-permute-done.6.refs_1_) | copy-start | bytes 1277956
  135.1 11.7 %collective-permute-start.8 = (bf16[128,1664]{1,0:T(8,128)(2,1)}, bf16[128,1664]{1,0:T(8,128)(2,1)}, u32[]{:S(2)}, u32[]{:S(2)}) collective-permute-start(bf16[128,1664]{1,0:T(8,128)(2,1)} %get-tuple-element.96), channel_id=1, source_target_pairs={{0,1},{1,2},{2,3},{3,0},{4,5},{5,6},{6,7},{7,4},{8,9},{9,10},{10,1... | collective-permute-start | bytes 1277960 | tf_op jit(solution)/shard_map/ppermute | solution.py:63
  135.3 29.4 %all-to-all-start = ((bf16[8,256,256]{2,1,0:T(8,128)(2,1)}), bf16[8,256,256]{2,1,0:T(8,128)(2,1)S(1)}, u32[]{:S(2)}, u32[]{:S(2)}) async-start(bf16[8,256,256]{2,1,0:T(8,128)(2,1)} %get-tuple-element.110), calls=%async_computation | async-start | bytes 2097152 | tf_op jit(solution)/shard_map/all_to_all | solution.py:973
  162.9 8.0 %collective-permute-start.9 = (bf16[128,1024]{1,0:T(8,128)(2,1)}, bf16[128,1024]{1,0:T(8,128)(2,1)}, u32[]{:S(2)}, u32[]{:S(2)}) collective-permute-start(bf16[128,1024]{1,0:T(8,128)(2,1)} %get-tuple-element.101.refs_0_), channel_id=1, source_target_pairs={{0,3},{1,0},{2,1},{3,2},{4,7},{5,4},{6,5},{7,6},{8,11},{9,8},{10,9... | collective-permute-start | bytes 786440 | tf_op jit(solution)/shard_map/ppermute | solution.py:63
  164.7 16.7 %copy-start = (bf16[8,256,256]{2,1,0:T(8,128)(2,1)}, bf16[8,256,256]{2,1,0:T(8,128)(2,1)S(1)}, u32[]{:S(2)}) copy-start(bf16[8,256,256]{2,1,0:T(8,128)(2,1)S(1)} %all-to-all-done.got.choices) | copy-start | bytes 3145732
  168.4 19.0 %copy-start.9 = (bf16[128,1024]{1,0:T(8,128)(2,1)S(1)}, bf16[128,1024]{1,0:T(8,128)(2,1)}, u32[]{:S(2)}) copy-start(bf16[128,1024]{1,0:T(8,128)(2,1)} %get-tuple-element.119.refs_1_) | copy-start | bytes 786436
  168.4 20.5 %copy-start.8 = (bf16[128,1024]{1,0:T(8,128)(2,1)S(1)}, bf16[128,1024]{1,0:T(8,128)(2,1)}, u32[]{:S(2)}) copy-start(bf16[128,1024]{1,0:T(8,128)(2,1)} %get-tuple-element.120.refs_2_) | copy-start | bytes 786436
  170.8 16.5 %collective-permute-start.10 = (bf16[21,32,128]{2,1,0:T(8,128)(2,1)}, bf16[21,32,128]{2,1,0:T(8,128)(2,1)S(1)}, u32[]{:S(2)}, u32[]{:S(2)}) collective-permute-start(bf16[21,32,128]{2,1,0:T(8,128)(2,1)} %shard_map.291.refs_3_), channel_id=1, source_target_pairs={{0,1},{1,2},{2,3},{3,0},{4,5},{5,6},{6,7},{7,4},{8,9},{9,10},{10,1... | collective-permute-start | bytes 516104 | tf_op jit(solution)/shard_map/ppermute | solution.py:58
  170.9 16.6 %collective-permute-start.11 = (bf16[21,32,128]{2,1,0:T(8,128)(2,1)}, bf16[21,32,128]{2,1,0:T(8,128)(2,1)S(1)}, u32[]{:S(2)}, u32[]{:S(2)}) collective-permute-start(bf16[21,32,128]{2,1,0:T(8,128)(2,1)} %shard_map.291.refs_3_), channel_id=1, source_target_pairs={{0,2},{1,3},{2,0},{3,1},{4,6},{5,7},{6,4},{7,5},{8,10},{9,11},{10,... | collective-permute-start | bytes 516104 | tf_op jit(solution)/shard_map/ppermute | solution.py:58
  175.7 11.7 %collective-permute-start.12 = (bf16[21,32,128]{2,1,0:T(8,128)(2,1)}, bf16[21,32,128]{2,1,0:T(8,128)(2,1)}, u32[]{:S(2)}, u32[]{:S(2)}) collective-permute-start(bf16[21,32,128]{2,1,0:T(8,128)(2,1)} %shard_map.291.refs_3_), channel_id=1, source_target_pairs={{0,3},{1,0},{2,1},{3,2},{4,7},{5,4},{6,5},{7,6},{8,11},{9,8},{10,9... | collective-permute-start | bytes 516104 | tf_op jit(solution)/shard_map/ppermute | solution.py:58
  187.4 2.2 %copy-start.10 = (bf16[21,32,128]{2,1,0:T(8,128)(2,1)}, bf16[21,32,128]{2,1,0:T(8,128)(2,1)S(1)}, u32[]{:S(2)}) copy-start(bf16[21,32,128]{2,1,0:T(8,128)(2,1)S(1)} %collective-permute-done.10.refs_0_) | copy-start | bytes 516100
  187.4 2.2 %copy-start.11 = (bf16[21,32,128]{2,1,0:T(8,128)(2,1)}, bf16[21,32,128]{2,1,0:T(8,128)(2,1)S(1)}, u32[]{:S(2)}) copy-start(bf16[21,32,128]{2,1,0:T(8,128)(2,1)S(1)} %collective-permute-done.11.refs_1_) | copy-start | bytes 516100
  187.4 18.4 %collective-permute-start.13 = (bf16[128,1024]{1,0:T(8,128)(2,1)S(1)}, bf16[128,1024]{1,0:T(8,128)(2,1)S(1)}, u32[]{:S(2)}, u32[]{:S(2)}) collective-permute-start(bf16[128,1024]{1,0:T(8,128)(2,1)S(1)} %copy-done.9), channel_id=1, source_target_pairs={{0,2},{1,3},{2,0},{3,1},{4,6},{5,7},{6,4},{7,5},{8,10},{9,11},{10,... | collective-permute-start | bytes 786440 | tf_op jit(solution)/shard_map/ppermute | solution.py:63
  189.0 16.9 %collective-permute-start.14 = (bf16[128,1024]{1,0:T(8,128)(2,1)S(1)}, bf16[128,1024]{1,0:T(8,128)(2,1)S(1)}, u32[]{:S(2)}, u32[]{:S(2)}) collective-permute-start(bf16[128,1024]{1,0:T(8,128)(2,1)S(1)} %copy-done.8), channel_id=1, source_target_pairs={{0,1},{1,2},{2,3},{3,0},{4,5},{5,6},{6,7},{7,4},{8,9},{9,10},{10,1... | collective-permute-start | bytes 786440 | tf_op jit(solution)/shard_map/ppermute | solution.py:63
  193.9 18.9 %all-to-all-start.1 = ((bf16[8,96,256]{2,1,0:T(8,128)(2,1)}), bf16[8,96,256]{2,1,0:T(8,128)(2,1)S(1)}, u32[]{:S(2)}, u32[]{:S(2)}) async-start(bf16[8,96,256]{2,1,0:T(8,128)(2,1)} %shard_map.294), calls=%async_computation.1 | async-start | bytes 786432 | tf_op jit(solution)/shard_map/all_to_all | solution.py:989
  205.9 0.8 copy-start.17
  (3 other events, 2.2 us)

commit v3 on v2

--- a/solution.py
+++ b/solution.py
@@ -22,6 +22,7 @@
 PAIR_QUERY = QUERY_FEATURES // PAIRS
 GATE_LANES = 8
 SENT = MODEL_WIDTH + LANES
+AHEAD = 2
 COLUMNS = 512
 
 EPS = 1e-05
@@ -238,23 +239,28 @@
     step = pl.program_id(0)
     own = xs[0].shape[0]
     key_of, value_of = variants(joined(ks), 0), variants(joined(vs), 1)
+    tiles = [lane_tiles(joined(qs[2 * n : 2 * n + 2])) for n in range(blocks // 2)]
+
+    def scores_of(n, h):
+        rows = slice(2 * n * own, (2 * n + 2) * own)
+        return mm_nt(tiles[n][h // 2], key_of[h // 3, h % 2]) + bias[rows]
+
+    todo = [(n, h) for n in range(blocks // 2) for h in range(6)]
+    waiting = [scores_of(*item) for item in todo[:AHEAD]]
+    heads = []
+    for i, (n, h) in enumerate(todo):
+        scores = waiting.pop(0)
+        if i + AHEAD < len(todo):
+            waiting.append(scores_of(*todo[i + AHEAD]))
+        shifted = jnp.exp(scores - jnp.max(scores, axis=-1, keepdims=True)).astype(BF16)
+        sums = mm(shifted, value_of[h // 3, h % 2])
+        heads.append(sums / pltpu.roll(sums, HEAD_SIZE, 1))
+    low = low_lanes(heads[0].shape)
     parts = []
     for n in range(blocks // 2):
-        tiles = lane_tiles(joined(qs[2 * n : 2 * n + 2]))
-        rows = slice(2 * n * own, (2 * n + 2) * own)
-        heads = []
-        for h in range(6):
-            at = (h // 3, h % 2)
-            scores = mm_nt(tiles[h // 2], key_of[at]) + bias[rows]
-            shifted = jnp.exp(scores - jnp.max(scores, axis=-1, keepdims=True)).astype(BF16)
-            sums = mm(shifted, value_of[at])
-            heads.append(sums / pltpu.roll(sums, HEAD_SIZE, 1))
-        low = low_lanes(heads[0].shape)
-        parts.append(
-            jnp.concatenate(
-                [jnp.where(low, heads[2 * t], heads[2 * t + 1]) for t in range(3)], axis=1
-            ).astype(BF16)
-        )
+        some = heads[6 * n : 6 * n + 6]
+        pairs = [jnp.where(low, some[2 * t], some[2 * t + 1]) for t in range(3)]
+        parts.append(jnp.concatenate(pairs, axis=1).astype(BF16))
     attended = jnp.concatenate(parts, axis=0)
     att_ref[...] = attended
     part = mm(attended, proj_w[...])
@@ -532,12 +538,19 @@
     low = low_lanes(queries[0].shape)
     none = jnp.zeros_like(queries[0])
     probs_of, scores_of, query_of, grad_of = [], [], [], []
-    for h in range(6):
+
+    def products(h):
         at = (h // 3, h % 2)
         scores = mm_nt(key_of[at], queries[h // 2]) + bias[...]
+        return scores, mm_nt(value_of[at], grads[h // 2])
+
+    waiting = [products(h) for h in range(AHEAD)]
+    for h in range(6):
+        scores, grad_probs = waiting.pop(0)
+        if h + AHEAD < 6:
+            waiting.append(products(h + AHEAD))
         shifted = jnp.exp(scores - jnp.max(scores, axis=0, keepdims=True))
         probs = shifted * (1.0 / jnp.sum(shifted, axis=0, keepdims=True))
-        grad_probs = mm_nt(value_of[at], grads[h // 2])
         grad_scores = probs * (grad_probs - jnp.sum(probs * grad_probs, axis=0, keepdims=True))
         probs_of.append(probs.astype(BF16))
         scores_of.append(grad_scores.astype(BF16))

time: 219 us -> 210 us (0.959)
  Pallas kernels: 145 us -> 137 us
  waiting for transfers between devices: 31.9 us -> 25.7 us
  starting transfers between devices: 27.2 us -> 31.4 us
    pallas_call x12, Pallas kernels: 145 us -> 137 us  [call(): pl.pallas_call(kernel, grid_spec=pltpu.PrefetchScalarGridSpec(num_scalar_...]
    ppermute x6, waiting for transfers between devices: 18.9 us -> 12.8 us  [send_back(): lax.ppermute(b, 'ctx', rotation(size, -1 - j))]
    ppermute x6, starting transfers between devices: 7.85 us -> 11.8 us  [send_back(): lax.ppermute(b, 'ctx', rotation(size, -1 - j))]
  transfers between devices with their start and end apart: 17 -> 17, of which waited for: 5 -> 5; matrix products, arithmetic and copies ran while one was open for 4% -> 4% of each run, Pallas kernels for 64% -> 63%
where the time goes in v3:
time: 210 us; the launch traced here: 209 us
  Pallas kernels  137 us (65%)
  starting transfers between devices  31.4 us (15%)
  waiting for transfers between devices  25.7 us (12%)
  local copies, waits for them, and re-layouts  8.93 us (4%)
  other arithmetic  3.55 us (2%)
  between operations  2.31 us (1%)
    pallas_call x12, Pallas kernels, call(): pl.pallas_call(kernel, grid_spec=pltpu.PrefetchScalarGridSpec(num_scalar_...  137 us
    ppermute x6, waiting for transfers between devices, send_back(): lax.ppermute(b, 'ctx', rotation(size, -1 - j))  12.8 us
    ppermute x6, starting transfers between devices, send_back(): lax.ppermute(b, 'ctx', rotation(size, -1 - j))  11.8 us
    ppermute x1, waiting for transfers between devices, shards(): step(after(inputs[0], cosine, sine, bias, bias_t, router_t, scalars, cot_...  9.71 us
    ppermute x6, starting transfers between devices, rotations(): lax.ppermute(block, 'ctx', rotation(size, j))  9.28 us
  transfers between devices with their start and end apart: 17, of which 5 were waited for; matrix products, arithmetic and copies ran while one was open for 4% of the time, Pallas kernels for 63%

profile of v3, /device:TPU:0, one launch (start us, length us, event | category | flops | bytes accessed | tf_op | source)
XLA Modules:
  0.0 209.2 jit_solution(17199228538490347708)
XLA Ops:
  0.7 3.1 %collective-permute-start = (bf16[128,1536]{1,0:T(8,128)(2,1)}, bf16[128,1536]{1,0:T(8,128)(2,1)S(1)}, u32[]{:S(2)}, u32[]{:S(2)}) collective-permute-start(bf16[128,1536]{1,0:T(8,128)(2,1)} %bitcast.30), channel_id=1, source_target_pairs={{0,1},{1,2},{2,3},{3,0},{4,5},{5,6},{6,7},{7,4},{8,9},{9,10},{10,1... | collective-permute-start | bytes 1179656 | tf_op jit(solution)/shard_map/ppermute | solution.py:940
  5.0 0.8 copy.36
  7.3 1.0 fusion.1
  8.9 1.7 pad.4.refs_3_.refs_13_
  10.6 1.3 pad_maximum_fusion.1
  11.9 3.2 %collective-permute-done.refs_1_.refs_0_ = bf16[128,1536]{1,0:T(8,128)(2,1)S(1)} collective-permute-done((bf16[128,1536]{1,0:T(8,128)(2,1)}, bf16[128,1536]{1,0:T(8,128)(2,1)S(1)}, u32[]{:S(2)}, u32[]{:S(2)}) %collective-permute-start) | collective-permute-done | bytes 393248 | tf_op jit(solution)/shard_map/ppermute | solution.py:940
  15.1 1.3 copy.38.refs_16_
  17.6 9.7 %collective-permute-done.1.refs_2_.refs_1_ = bf16[128,1536]{1,0:T(8,128)(2,1)} collective-permute-done((bf16[128,1536]{1,0:T(8,128)(2,1)S(1)}, bf16[128,1536]{1,0:T(8,128)(2,1)}, u32[]{:S(2)}, u32[]{:S(2)}) %collective-permute-start.1) | collective-permute-done | bytes 393248 | tf_op jit(solution)/shard_map/ppermute | solution.py:941
  27.3 12.3 %shard_map.285 = (bf16[128,1536]{1,0:T(8,128)(2,1)}, bf16[128,1536]{1,0:T(8,128)(2,1)}, bf16[128,1536]{1,0:T(8,128)(2,1)}, bf16[128,1024]{1,0:T(8,128)(2,1)}, bf...) custom-call(s32[3]{0:T(128)} %pad_add_fusion.scalars, ...), custom_call_target="tpu_custom_call" | custom-call | flops 10000000000 | tf_op jit(solution)/shard_map/pallas_call | solution.py:102
  39.6 4.4 %collective-permute-start.3 = (bf16[128,1664]{1,0:T(8,128)(2,1)S(1)}, bf16[128,1664]{1,0:T(8,128)(2,1)S(1)}, u32[]{:S(2)}, u32[]{:S(2)}) collective-permute-start(bf16[128,1664]{1,0:T(8,128)(2,1)S(1)} %pad_maximum_fusion.refs_1_.refs_17_), channel_id=1, source_target_pairs={{0,2},{1,3},{2,0},{3,1},{4,6},{5,7},{6,4},{7,5},{8,10},{9,11},{10,... | collective-permute-start | bytes 1277960 | tf_op jit(solution)/shard_map/ppermute | solution.py:59
  44.0 8.7 %shard_map.286 = (bf16[128,1536]{1,0:T(8,128)(2,1)}, bf16[128,1024]{1,0:T(8,128)(2,1)}, bf16[128,1024]{1,0:T(8,128)(2,1)}, bf16[128,1536]{1,0:T(8,128)(2,1)}, bf16[128,48]{1,0:T(8,128)(2,1)}) custom-call(s32[3]{0:T(128)} %pad_add_fusion.scalars, bf16[128,1536]{1,0:T(8,128)(2,1)} %collective-permute-done.4.refs_0_.refs_2_, ...), custom_call_target="tpu_custom_call" | custom-call | flops 10000000000 | tf_op jit(solution)/shard_map/pallas_call | solution.py:102
  52.7 19.8 %shard_map.287 = (bf16[256,1536]{1,0:T(8,128)(2,1)}, bf16[256,1536]{1,0:T(8,128)(2,1)}, bf16[512,1536]{1,0:T(8,128)(2,1)}, bf16[128,16]{1,0:T(8,128)(2,1)}, f32[128,1536]{1,0:T(8,128)}, /*index=5*/f32[128,1]{1,0:T(8,128)}) custom-call(s32[3]{0:T(128)} %pad_add_fusion.scalars, bf16[128,1536]{1,0:T(8,128)(2,1)} %copy-done.6, ...), custom_call_target="tpu_custom_call" | custom-call | tf_op jit(solution)/shard_map/pallas_call | solution.py:102
  73.4 24.7 %shard_map.288 = (bf16[128,1664]{1,0:T(8,128)(2,1)}, bf16[128,1664]{1,0:T(8,128)(2,1)}, f32[240,1536]{1,0:T(8,128)}, f32[5,48,512]{2,1,0:T(8,128)}) custom-call(s32[3]{0:T(128)} %pad_add_fusion.scalars, bf16[128,1664]{1,0:T(8,128)(2,1)} %copy-done.4, bf16[128,1664]{1,0:T(8,128)(2,1)} %copy-done.5, bf16[256,1536]{1,0:T(8,128)(2,1)} %get-tuple-element.89.refs_2_, ...), custom_call_target="tpu_custom_call" | custom-call | tf_op jit(solution)/shard_map/pallas_call | solution.py:102
  98.1 5.3 %collective-permute-start.5 = (bf16[128,1664]{1,0:T(8,128)(2,1)}, bf16[128,1664]{1,0:T(8,128)(2,1)S(1)}, u32[]{:S(2)}, u32[]{:S(2)}) collective-permute-start(bf16[128,1664]{1,0:T(8,128)(2,1)} %get-tuple-element.90), channel_id=1, source_target_pairs={{0,3},{1,0},{2,1},{3,2},{4,7},{5,4},{6,5},{7,6},{8,11},{9,8},{10,9... | collective-permute-start | bytes 1277960 | tf_op jit(solution)/shard_map/ppermute | solution.py:64
  103.4 0.8 copy-done.3
  104.2 25.3 %shard_map.289 = (bf16[128,1664]{1,0:T(8,128)(2,1)}, bf16[128,1664]{1,0:T(8,128)(2,1)}, bf16[8,256,256]{2,1,0:T(8,128)(2,1)}, f32[128,128]{1,0:T(8,128)}) custom-call(s32[3]{0:T(128)} %pad_add_fusion.scalars, bf16[128,1664]{1,0:T(8,128)(2,1)} %copy-done.3, bf16[128,1664]{1,0:T(8,128)(2,1)} %copy-done.1, bf16[256,1536]{1,0:T(8,128)(2,1)} %get-tuple-element.92.refs_2_, ...), custom_call_target="tpu_custom_call" | custom-call | tf_op jit(solution)/shard_map/pallas_call | solution.py:102
  130.2 3.6 %all-to-all-start = ((bf16[8,256,256]{2,1,0:T(8,128)(2,1)}), bf16[8,256,256]{2,1,0:T(8,128)(2,1)S(1)}, u32[]{:S(2)}, u32[]{:S(2)}) async-start(bf16[8,256,256]{2,1,0:T(8,128)(2,1)} %get-tuple-element.110), calls=%async_computation | async-start | bytes 2097152 | tf_op jit(solution)/shard_map/all_to_all | solution.py:986
  133.8 7.2 %collective-permute-done.8.refs_2_ = bf16[128,1664]{1,0:T(8,128)(2,1)} collective-permute-done((bf16[128,1664]{1,0:T(8,128)(2,1)}, bf16[128,1664]{1,0:T(8,128)(2,1)}, u32[]{:S(2)}, u32[]{:S(2)}) %collective-permute-start.8) | collective-permute-done | bytes 426016 | tf_op jit(solution)/shard_map/ppermute | solution.py:64
  141.0 16.0 %shard_map.290 = (f32[128,1536]{1,0:T(8,128)}, bf16[128,1536]{1,0:T(8,128)(2,1)}, bf16[128,16]{1,0:T(8,128)(2,1)}, bf16[128,1536]{1,0:T(8,128)(2,1)}, bf16[128,1...) custom-call(s32[3]{0:T(128)} %pad_add_fusion.scalars, ...), custom_call_target="tpu_custom_call" | custom-call | flops 20000000000 | tf_op jit(solution)/shard_map/pallas_call | solution.py:102
  157.0 1.8 collective-permute-start.9
  158.8 3.8 %shard_map.291.refs_3_ = bf16[21,32,128]{2,1,0:T(8,128)(2,1)} custom-call(s32[3]{0:T(128)} %pad_add_fusion.scalars, bf16[128,1024]{1,0:T(8,128)(2,1)} %get-tuple-element.101.refs_0_, bf16[128,1024]{1,0:T(8,128)(2,1)} %get-tuple-element.119.refs_1_, bf16[128,1024]{1,0:T(8,128)(2,1)} %get-tuple-element.120.refs_2_, ...), custom_call_target="tpu_custom_call" | custom-call | tf_op jit(solution)/shard_map/pallas_call | solution.py:102
  162.6 2.4 %collective-permute-done.9.refs_0_ = bf16[128,1024]{1,0:T(8,128)(2,1)} collective-permute-done((bf16[128,1024]{1,0:T(8,128)(2,1)}, bf16[128,1024]{1,0:T(8,128)(2,1)}, u32[]{:S(2)}, u32[]{:S(2)}) %collective-permute-start.9) | collective-permute-done | bytes 262176 | tf_op jit(solution)/shard_map/ppermute | solution.py:64
  164.9 4.8 %collective-permute-start.11 = (bf16[21,32,128]{2,1,0:T(8,128)(2,1)}, bf16[21,32,128]{2,1,0:T(8,128)(2,1)S(1)}, u32[]{:S(2)}, u32[]{:S(2)}) collective-permute-start(bf16[21,32,128]{2,1,0:T(8,128)(2,1)} %shard_map.291.refs_3_), channel_id=1, source_target_pairs={{0,2},{1,3},{2,0},{3,1},{4,6},{5,7},{6,4},{7,5},{8,10},{9,11},{10,... | collective-permute-start | bytes 516104 | tf_op jit(solution)/shard_map/ppermute | solution.py:59
  169.8 5.7 %shard_map.292.refs_5_ = f32[128,1536]{1,0:T(8,128)} custom-call(s32[3]{0:T(128)} %pad_add_fusion.scalars, bf16[128,1536]{1,0:T(8,128)(2,1)} %get-tuple-element.127.refs_8_.gq.refs_4_, bf16[1536,1536]{1,0:T(8,128)(2,1)} %query_w.1), custom_call_target="tpu_custom_call" | custom-call | tf_op jit(solution)/shard_map/pallas_call | solution.py:102
  175.5 6.0 %shard_map.293 = (f32[8,5,32,192]{3,2,1,0:T(8,128)}, f32[8,5,2,16,64]{4,3,2,1,0:T(8,128)}, f32[8,5,16,64]{3,2,1,0:T(8,128)}, f32[8,5,16,192]{3,2,1,0:T(8,128)}) custom-call(s32[3]{0:T(128)} %pad_add_fusion.scalars, bf16[8,256,256]{2,1,0:T(8,128)(2,1)} %copy-done, bf16[8,256,256]{2,1,0:T(8,128)(2,1)} %copy-done), custom_call_target="tpu_custom_call" | custom-call | tf_op jit(solution)/shard_map/pallas_call | solution.py:102
  181.5 1.5 collective-permute-start.13
  183.1 2.5 %collective-permute-start.14 = (bf16[128,1024]{1,0:T(8,128)(2,1)S(1)}, bf16[128,1024]{1,0:T(8,128)(2,1)S(1)}, u32[]{:S(2)}, u32[]{:S(2)}) collective-permute-start(bf16[128,1024]{1,0:T(8,128)(2,1)S(1)} %copy-done.8), channel_id=1, source_target_pairs={{0,1},{1,2},{2,3},{3,0},{4,5},{5,6},{6,7},{7,4},{8,9},{9,10},{10,1... | collective-permute-start | bytes 786440 | tf_op jit(solution)/shard_map/ppermute | solution.py:64
  185.6 4.2 %shard_map.294 = bf16[8,96,256]{2,1,0:T(8,128)(2,1)} custom-call(s32[3]{0:T(128)} %pad_add_fusion.scalars, bf16[21,32,128]{2,1,0:T(8,128)(2,1)} %copy-done.10, bf16[21,32,128]{2,1,0:T(8,128)(2,1)} %copy-done.11, bf16[21,32,128]{2,1,0:T(8,128)(2,1)} %collective-permute-done.12.refs_2_, bf16[21,32,128]{2,1,0:T(8,128)(2,1)} %shard_map.291.refs_3_, ...), custom_call_target="tpu_custom_call" | custom-call | tf_op jit(solution)/shard_map/pallas_call | solution.py:102
  189.8 3.6 %all-to-all-start.1 = ((bf16[8,96,256]{2,1,0:T(8,128)(2,1)}), bf16[8,96,256]{2,1,0:T(8,128)(2,1)S(1)}, u32[]{:S(2)}, u32[]{:S(2)}) async-start(bf16[8,96,256]{2,1,0:T(8,128)(2,1)} %shard_map.294), calls=%async_computation.1 | async-start | bytes 786432 | tf_op jit(solution)/shard_map/all_to_all | solution.py:1002
  193.4 3.2 %collective-permute-done.13.refs_1_ = bf16[128,1024]{1,0:T(8,128)(2,1)S(1)} collective-permute-done((bf16[128,1024]{1,0:T(8,128)(2,1)S(1)}, bf16[128,1024]{1,0:T(8,128)(2,1)S(1)}, u32[]{:S(2)}, u32[]{:S(2)}) %collective-permute-start.13) | collective-permute-done | bytes 262176 | tf_op jit(solution)/shard_map/ppermute | solution.py:64
  197.4 6.1 %shard_map.295 = f32[128,1536]{1,0:T(8,128)} custom-call(s32[3]{0:T(128)} %pad_add_fusion.scalars, bf16[128,1024]{1,0:T(8,128)(2,1)} %collective-permute-done.9.refs_0_, bf16[128,1024]{1,0:T(8,128)(2,1)} %copy-done.16, bf16[128,1024]{1,0:T(8,128)(2,1)} %copy-done.17, bf16[128,1024]{1,0:T(8,128)(2,1)} %get-tuple-element.105.refs_3_, ...), custom_call_target="tpu_custom_call" | custom-call | flops 20000000000 | tf_op jit(solution)/shard_map/pallas_call | solution.py:102
  204.3 4.8 %shard_map.296 = (f32[8,48,192]{2,1,0:T(8,128)}, f32[8,16,192]{2,1,0:T(8,128)}, f32[8,2,16,64]{3,2,1,0:T(8,128)}, f32[8,16,192]{2,1,0:T(8,128)}, f32[8,16,192]{2,1,0:T(8,128)}) custom-call(s32[3]{0:T(128)} %pad_add_fusion.scalars, bf16[8,96,256]{2,1,0:T(8,128)(2,1)} %copy-done.2, bf16[8,256,256]{2,1,0:T(8,128)(2,1)} %copy-done), custom_call_target="tpu_custom_call" | custom-call | tf_op jit(solution)/shard_map/pallas_call | solution.py:102
  (67 shorter events, 6.5 us)
Async XLA Ops:
  0.6 11.2 %copy-start.7 = (bf16[1,128,1536]{2,1,0:T(8,128)(2,1)S(1)}, bf16[1,128,1536]{2,1,0:T(8,128)(2,1)}, u32[]{:S(2)}) copy-start(bf16[1,128,1536]{2,1,0:T(8,128)(2,1)} %param.43) | copy-start | bytes 1179652
  0.7 14.4 %collective-permute-start = (bf16[128,1536]{1,0:T(8,128)(2,1)}, bf16[128,1536]{1,0:T(8,128)(2,1)S(1)}, u32[]{:S(2)}, u32[]{:S(2)}) collective-permute-start(bf16[128,1536]{1,0:T(8,128)(2,1)} %bitcast.30), channel_id=1, source_target_pairs={{0,1},{1,2},{2,3},{3,0},{4,5},{5,6},{6,7},{7,4},{8,9},{9,10},{10,1... | collective-permute-start | bytes 1179656 | tf_op jit(solution)/shard_map/ppermute | solution.py:940
  6.5 9.9 %copy-start.12 = (f32[1536]{0:T(1024)S(1)}, f32[1536]{0:T(1024)}, u32[]{:S(2)}) copy-start(f32[1536]{0:T(1024)} %param.26) | copy-start | bytes 18436
  6.5 10.5 %copy-start.13 = (f32[1536]{0:T(1024)S(1)}, f32[1536]{0:T(1024)}, u32[]{:S(2)}) copy-start(f32[1536]{0:T(1024)} %param.27) | copy-start | bytes 18436
  11.9 32.1 %copy-start.1 = (bf16[128,1664]{1,0:T(8,128)(2,1)}, bf16[128,1664]{1,0:T(8,128)(2,1)S(1)}, u32[]{:S(2)}) copy-start(bf16[128,1664]{1,0:T(8,128)(2,1)S(1)} %pad_maximum_fusion.refs_1_.refs_17_) | copy-start | bytes 1277956
  15.1 12.2 %copy-start.6 = (bf16[128,1536]{1,0:T(8,128)(2,1)}, bf16[128,1536]{1,0:T(8,128)(2,1)S(1)}, u32[]{:S(2)}) copy-start(bf16[128,1536]{1,0:T(8,128)(2,1)S(1)} %collective-permute-done.refs_1_.refs_0_) | copy-start | bytes 1179652
  15.1 12.2 %collective-permute-start.1 = (bf16[128,1536]{1,0:T(8,128)(2,1)S(1)}, bf16[128,1536]{1,0:T(8,128)(2,1)}, u32[]{:S(2)}, u32[]{:S(2)}) collective-permute-start(bf16[128,1536]{1,0:T(8,128)(2,1)S(1)} %collective-permute-done.refs_1_.refs_0_), channel_id=1, source_target_pairs={{0,1},{1,2},{2,3},{3,0},{4,5},{5,6},{6,7},{7,4},{8,9},{9,10},{10,1... | collective-permute-start | bytes 1179656 | tf_op jit(solution)/shard_map/ppermute | solution.py:941
  27.3 16.7 %collective-permute-start.4 = (bf16[128,1536]{1,0:T(8,128)(2,1)}, bf16[128,1536]{1,0:T(8,128)(2,1)}, u32[]{:S(2)}, u32[]{:S(2)}) collective-permute-start(bf16[128,1536]{1,0:T(8,128)(2,1)} %collective-permute-done.1.refs_2_.refs_1_), channel_id=1, source_target_pairs={{0,1},{1,2},{2,3},{3,0},{4,5},{5,6},{6,7},{7,4},{8,9},{9,10},{10,1... | collective-permute-start | bytes 1179656 | tf_op jit(solution)/shard_map/ppermute | solution.py:943
  39.6 32.9 %collective-permute-start.2 = (bf16[128,1664]{1,0:T(8,128)(2,1)S(1)}, bf16[128,1664]{1,0:T(8,128)(2,1)S(1)}, u32[]{:S(2)}, u32[]{:S(2)}) collective-permute-start(bf16[128,1664]{1,0:T(8,128)(2,1)S(1)} %pad_maximum_fusion.refs_1_.refs_17_), channel_id=1, source_target_pairs={{0,1},{1,2},{2,3},{3,0},{4,5},{5,6},{6,7},{7,4},{8,9},{9,10},{10,1... | collective-permute-start | bytes 1277960 | tf_op jit(solution)/shard_map/ppermute | solution.py:59
  39.6 32.9 %collective-permute-start.3 = (bf16[128,1664]{1,0:T(8,128)(2,1)S(1)}, bf16[128,1664]{1,0:T(8,128)(2,1)S(1)}, u32[]{:S(2)}, u32[]{:S(2)}) collective-permute-start(bf16[128,1664]{1,0:T(8,128)(2,1)S(1)} %pad_maximum_fusion.refs_1_.refs_17_), channel_id=1, source_target_pairs={{0,2},{1,3},{2,0},{3,1},{4,6},{5,7},{6,4},{7,5},{8,10},{9,11},{10,... | collective-permute-start | bytes 1277960 | tf_op jit(solution)/shard_map/ppermute | solution.py:59
  44.0 59.4 %collective-permute-start.7 = (bf16[128,1664]{1,0:T(8,128)(2,1)S(1)}, bf16[128,1664]{1,0:T(8,128)(2,1)S(1)}, u32[]{:S(2)}, u32[]{:S(2)}) collective-permute-start(bf16[128,1664]{1,0:T(8,128)(2,1)S(1)} %pad_maximum_fusion.refs_1_.refs_17_), channel_id=1, source_target_pairs={{0,3},{1,0},{2,1},{3,2},{4,7},{5,4},{6,5},{7,6},{8,11},{9,8},{10,9... | collective-permute-start | bytes 1277960 | tf_op jit(solution)/shard_map/ppermute | solution.py:59
  72.5 0.8 copy-start.4
  72.5 0.9 copy-start.5
  98.1 31.4 %collective-permute-start.5 = (bf16[128,1664]{1,0:T(8,128)(2,1)}, bf16[128,1664]{1,0:T(8,128)(2,1)S(1)}, u32[]{:S(2)}, u32[]{:S(2)}) collective-permute-start(bf16[128,1664]{1,0:T(8,128)(2,1)} %get-tuple-element.90), channel_id=1, source_target_pairs={{0,3},{1,0},{2,1},{3,2},{4,7},{5,4},{6,5},{7,6},{8,11},{9,8},{10,9... | collective-permute-start | bytes 1277960 | tf_op jit(solution)/shard_map/ppermute | solution.py:64
  103.4 26.1 %collective-permute-start.6 = (bf16[128,1664]{1,0:T(8,128)(2,1)}, bf16[128,1664]{1,0:T(8,128)(2,1)S(1)}, u32[]{:S(2)}, u32[]{:S(2)}) collective-permute-start(bf16[128,1664]{1,0:T(8,128)(2,1)} %get-tuple-element.91), channel_id=1, source_target_pairs={{0,2},{1,3},{2,0},{3,1},{4,6},{5,7},{6,4},{7,5},{8,10},{9,11},{10,... | collective-permute-start | bytes 1277960 | tf_op jit(solution)/shard_map/ppermute | solution.py:64
  129.5 11.5 %copy-start.14 = (bf16[128,1664]{1,0:T(8,128)(2,1)}, bf16[128,1664]{1,0:T(8,128)(2,1)S(1)}, u32[]{:S(2)}) copy-start(bf16[128,1664]{1,0:T(8,128)(2,1)S(1)} %collective-permute-done.5.refs_0_) | copy-start | bytes 1277956
  129.5 11.5 %copy-start.15 = (bf16[128,1664]{1,0:T(8,128)(2,1)}, bf16[128,1664]{1,0:T(8,128)(2,1)S(1)}, u32[]{:S(2)}) copy-start(bf16[128,1664]{1,0:T(8,128)(2,1)S(1)} %collective-permute-done.6.refs_1_) | copy-start | bytes 1277956
  129.5 11.5 %collective-permute-start.8 = (bf16[128,1664]{1,0:T(8,128)(2,1)}, bf16[128,1664]{1,0:T(8,128)(2,1)}, u32[]{:S(2)}, u32[]{:S(2)}) collective-permute-start(bf16[128,1664]{1,0:T(8,128)(2,1)} %get-tuple-element.96), channel_id=1, source_target_pairs={{0,1},{1,2},{2,3},{3,0},{4,5},{5,6},{6,7},{7,4},{8,9},{9,10},{10,1... | collective-permute-start | bytes 1277960 | tf_op jit(solution)/shard_map/ppermute | solution.py:64
  130.2 28.6 %all-to-all-start = ((bf16[8,256,256]{2,1,0:T(8,128)(2,1)}), bf16[8,256,256]{2,1,0:T(8,128)(2,1)S(1)}, u32[]{:S(2)}, u32[]{:S(2)}) async-start(bf16[8,256,256]{2,1,0:T(8,128)(2,1)} %get-tuple-element.110), calls=%async_computation | async-start | bytes 2097152 | tf_op jit(solution)/shard_map/all_to_all | solution.py:986
  157.0 8.0 %collective-permute-start.9 = (bf16[128,1024]{1,0:T(8,128)(2,1)}, bf16[128,1024]{1,0:T(8,128)(2,1)}, u32[]{:S(2)}, u32[]{:S(2)}) collective-permute-start(bf16[128,1024]{1,0:T(8,128)(2,1)} %get-tuple-element.101.refs_0_), channel_id=1, source_target_pairs={{0,3},{1,0},{2,1},{3,2},{4,7},{5,4},{6,5},{7,6},{8,11},{9,8},{10,9... | collective-permute-start | bytes 786440 | tf_op jit(solution)/shard_map/ppermute | solution.py:64
  158.8 16.7 %copy-start = (bf16[8,256,256]{2,1,0:T(8,128)(2,1)}, bf16[8,256,256]{2,1,0:T(8,128)(2,1)S(1)}, u32[]{:S(2)}) copy-start(bf16[8,256,256]{2,1,0:T(8,128)(2,1)S(1)} %all-to-all-done.got.choices) | copy-start | bytes 3145732
  162.5 19.0 %copy-start.9 = (bf16[128,1024]{1,0:T(8,128)(2,1)S(1)}, bf16[128,1024]{1,0:T(8,128)(2,1)}, u32[]{:S(2)}) copy-start(bf16[128,1024]{1,0:T(8,128)(2,1)} %get-tuple-element.119.refs_1_) | copy-start | bytes 786436
  162.6 20.5 %copy-start.8 = (bf16[128,1024]{1,0:T(8,128)(2,1)S(1)}, bf16[128,1024]{1,0:T(8,128)(2,1)}, u32[]{:S(2)}) copy-start(bf16[128,1024]{1,0:T(8,128)(2,1)} %get-tuple-element.120.refs_2_) | copy-start | bytes 786436
  164.9 16.5 %collective-permute-start.10 = (bf16[21,32,128]{2,1,0:T(8,128)(2,1)}, bf16[21,32,128]{2,1,0:T(8,128)(2,1)S(1)}, u32[]{:S(2)}, u32[]{:S(2)}) collective-permute-start(bf16[21,32,128]{2,1,0:T(8,128)(2,1)} %shard_map.291.refs_3_), channel_id=1, source_target_pairs={{0,1},{1,2},{2,3},{3,0},{4,5},{5,6},{6,7},{7,4},{8,9},{9,10},{10,1... | collective-permute-start | bytes 516104 | tf_op jit(solution)/shard_map/ppermute | solution.py:59
  164.9 16.6 %collective-permute-start.11 = (bf16[21,32,128]{2,1,0:T(8,128)(2,1)}, bf16[21,32,128]{2,1,0:T(8,128)(2,1)S(1)}, u32[]{:S(2)}, u32[]{:S(2)}) collective-permute-start(bf16[21,32,128]{2,1,0:T(8,128)(2,1)} %shard_map.291.refs_3_), channel_id=1, source_target_pairs={{0,2},{1,3},{2,0},{3,1},{4,6},{5,7},{6,4},{7,5},{8,10},{9,11},{10,... | collective-permute-start | bytes 516104 | tf_op jit(solution)/shard_map/ppermute | solution.py:59
  169.8 11.7 %collective-permute-start.12 = (bf16[21,32,128]{2,1,0:T(8,128)(2,1)}, bf16[21,32,128]{2,1,0:T(8,128)(2,1)}, u32[]{:S(2)}, u32[]{:S(2)}) collective-permute-start(bf16[21,32,128]{2,1,0:T(8,128)(2,1)} %shard_map.291.refs_3_), channel_id=1, source_target_pairs={{0,3},{1,0},{2,1},{3,2},{4,7},{5,4},{6,5},{7,6},{8,11},{9,8},{10,9... | collective-permute-start | bytes 516104 | tf_op jit(solution)/shard_map/ppermute | solution.py:59
  181.5 4.1 %copy-start.10 = (bf16[21,32,128]{2,1,0:T(8,128)(2,1)}, bf16[21,32,128]{2,1,0:T(8,128)(2,1)S(1)}, u32[]{:S(2)}) copy-start(bf16[21,32,128]{2,1,0:T(8,128)(2,1)S(1)} %collective-permute-done.10.refs_0_) | copy-start | bytes 516100
  181.5 4.1 %copy-start.11 = (bf16[21,32,128]{2,1,0:T(8,128)(2,1)}, bf16[21,32,128]{2,1,0:T(8,128)(2,1)S(1)}, u32[]{:S(2)}) copy-start(bf16[21,32,128]{2,1,0:T(8,128)(2,1)S(1)} %collective-permute-done.11.refs_1_) | copy-start | bytes 516100
  181.5 15.1 %collective-permute-start.13 = (bf16[128,1024]{1,0:T(8,128)(2,1)S(1)}, bf16[128,1024]{1,0:T(8,128)(2,1)S(1)}, u32[]{:S(2)}, u32[]{:S(2)}) collective-permute-start(bf16[128,1024]{1,0:T(8,128)(2,1)S(1)} %copy-done.9), channel_id=1, source_target_pairs={{0,2},{1,3},{2,0},{3,1},{4,6},{5,7},{6,4},{7,5},{8,10},{9,11},{10,... | collective-permute-start | bytes 786440 | tf_op jit(solution)/shard_map/ppermute | solution.py:64
  183.1 13.5 %collective-permute-start.14 = (bf16[128,1024]{1,0:T(8,128)(2,1)S(1)}, bf16[128,1024]{1,0:T(8,128)(2,1)S(1)}, u32[]{:S(2)}, u32[]{:S(2)}) collective-permute-start(bf16[128,1024]{1,0:T(8,128)(2,1)S(1)} %copy-done.8), channel_id=1, source_target_pairs={{0,1},{1,2},{2,3},{3,0},{4,5},{5,6},{6,7},{7,4},{8,9},{9,10},{10,1... | collective-permute-start | bytes 786440 | tf_op jit(solution)/shard_map/ppermute | solution.py:64
  189.8 13.7 %all-to-all-start.1 = ((bf16[8,96,256]{2,1,0:T(8,128)(2,1)}), bf16[8,96,256]{2,1,0:T(8,128)(2,1)S(1)}, u32[]{:S(2)}, u32[]{:S(2)}) async-start(bf16[8,96,256]{2,1,0:T(8,128)(2,1)} %shard_map.294), calls=%async_computation.1 | async-start | bytes 786432 | tf_op jit(solution)/shard_map/all_to_all | solution.py:1002
  196.6 0.8 copy-start.17
  (3 other events, 2.2 us)

commit v4 on v3

--- a/solution.py
+++ b/solution.py
@@ -726,45 +726,36 @@
     )[0]
 
 
-def summed(received, choices, adapter, senders):
-    total = None
-    for n in range(senders):
-        rows = jnp.where(choices[n, :1, :1].astype(F32) == adapter, received(n), 0.0)
-        total = rows if total is None else total + rows
-    return total
-
-
-def expert_sum_kernel(wide, scalars, got, choices, up_in, up_out, down_in, down_out):
-    adapter = pl.program_id(0).astype(F32)
-    total = summed(lambda n: got[n].astype(F32), choices, adapter, got.shape[0])
+def expert_sum_kernel(wide, scalars, got, up_in, up_out, down_in, down_out):
+    for out in (up_in, up_out, down_in, down_out):
+        out[...] = jnp.zeros_like(out)
     r = ADAPTER_RANK
     here = up_in.shape[1]
-    for e in range(here):
-        up_in[0, e] = total[e * 2 * r : (e + 1) * 2 * r, :wide]
-        down_out[0, e] = total[(2 * here + e) * r : (2 * here + e + 1) * r, :wide]
-        rows = total[e * 3 * r : (e + 1) * 3 * r]
-        up_out[0, e, 0] = rows[:r, wide:]
-        up_out[0, e, 1] = rows[r : 2 * r, wide:]
-        down_in[0, e] = rows[2 * r :, wide:]
+    for n in range(got.shape[0]):
+        a = scalars[3 + n]
+        rows = got[n].astype(F32)
+        for e in range(here):
+            up_in[a, e] += rows[e * 2 * r : (e + 1) * 2 * r, :wide]
+            down_out[a, e] += rows[(2 * here + e) * r : (2 * here + e + 1) * r, :wide]
+            at = e * 3 * r
+            up_out[a, e, 0] += rows[at : at + r, wide:]
+            up_out[a, e, 1] += rows[at + r : at + 2 * r, wide:]
+            down_in[a, e] += rows[at + 2 * r : at + 3 * r, wide:]
 
 
 def expert_sum(scalars, got, here):
-    parts, _, width = got.shape
+    parts = got.shape[0]
     r = ADAPTER_RANK
-    rows = here * 3 * r
     wide, narrow = MODEL_WIDTH // parts, EXPERT_HIDDEN // parts
 
     def out(*shape):
-        return ((ADAPTER_CHOICES,) + shape, F32, (1,) + shape, lambda i, s: (i,) + (0,) * len(shape))
+        return whole_out((ADAPTER_CHOICES,) + shape, F32)
 
     return call(
         functools.partial(expert_sum_kernel, wide),
         scalars,
-        ADAPTER_CHOICES,
-        [
-            (got, (parts, rows, width), lambda i, s: (0, 0, 0)),
-            (got, (parts, 16, width), lambda i, s: (0, rows // 16, 0)),
-        ],
+        1,
+        [whole(got)],
         [
             out(here, 2 * r, wide),
             out(here, 2, r, narrow),
@@ -775,31 +766,34 @@
     )
 
 
-def attention_sum_kernel(wide, scalars, got, choices, qkv_in, query_out, kv_out, proj_in, proj_out):
-    adapter = pl.program_id(0).astype(F32)
-    total = summed(lambda n: got[n].astype(F32), choices, adapter, got.shape[0])
+def attention_sum_kernel(wide, scalars, got, qkv_in, query_out, kv_out, proj_in, proj_out):
+    for out in (qkv_in, query_out, kv_out, proj_in, proj_out):
+        out[...] = jnp.zeros_like(out)
     r = ADAPTER_RANK
-    qkv_in[0] = total[: 3 * r, :wide]
-    proj_in[0] = total[3 * r : 4 * r, :wide]
-    query_out[0] = total[4 * r : 5 * r, :wide]
-    proj_out[0] = total[5 * r :, :wide]
-    kv_out[0, 0] = total[:r, wide:]
-    kv_out[0, 1] = total[r : 2 * r, wide:]
-
-
-def attention_sum(scalars, got, expert_got, rows):
-    parts, _, width = got.shape
+    for n in range(got.shape[0]):
+        a = scalars[3 + n]
+        rows = got[n].astype(F32)
+        qkv_in[a] += rows[: 3 * r, :wide]
+        proj_in[a] += rows[3 * r : 4 * r, :wide]
+        query_out[a] += rows[4 * r : 5 * r, :wide]
+        proj_out[a] += rows[5 * r :, :wide]
+        kv_out[a, 0] += rows[:r, wide:]
+        kv_out[a, 1] += rows[r : 2 * r, wide:]
+
+
+def attention_sum(scalars, got):
+    parts = got.shape[0]
     r = ADAPTER_RANK
     wide, narrow = MODEL_WIDTH // parts, KEY_FEATURES // parts
 
     def out(*shape):
-        return ((ADAPTER_CHOICES,) + shape, F32, (1,) + shape, lambda i, s: (i,) + (0,) * len(shape))
+        return whole_out((ADAPTER_CHOICES,) + shape, F32)
 
     return call(
         functools.partial(attention_sum_kernel, wide),
         scalars,
-        ADAPTER_CHOICES,
-        [whole(got), (expert_got, (parts, 16, width), lambda i, s: (0, rows // 16, 0))],
+        1,
+        [whole(got)],
         [
             out(3 * r, wide),
             out(r, wide),
@@ -913,7 +907,7 @@
     experts_here = gate_up_weight.shape[0]
     experts_all = experts_here * ctx_size
     half = ctx_size // 2
-    scalars = jnp.stack([sequence_adapter_index[0], prefix[0], rank]).astype(jnp.int32)
+    scalars = jnp.concatenate([sequence_adapter_index, prefix, rank[None]])
     gain_attn = attention_norm_gain[None]
     gain_ffn = expert_norm_gain[None]
 
@@ -991,9 +985,11 @@
     gkvs = list(gkvs)
     gkvs[0] = send_back(gkvs[:1], ctx_size, 0)[0]
     packages = rotations(after(package, gkvs[0]), ctx_size)
-    first = query_backward(scalars, after(gq, package), query_weight)
+    choices = expert_got[:, experts_here * 3 * ADAPTER_RANK, 0].astype(jnp.int32)
+    with_choices = jnp.concatenate([scalars, choices])
+    first = query_backward(scalars, after(gq, package, gkvs[0], with_choices), query_weight)
     up_in, up_out, down_in, down_out = expert_sum(
-        scalars, after(expert_got, first), experts_here
+        with_choices, after(expert_got, first), experts_here
     )
     later = [after(g, first, up_in, *packages[:-1]) for g in gkvs[1:-1]]
     gkvs[1:-1] = send_back(later, ctx_size, 1)
@@ -1006,7 +1002,7 @@
     )
     attention_got = after(attention_got, grad_inputs)
     qkv_in, query_out, kv_out, proj_in, proj_out = attention_sum(
-        scalars, attention_got, expert_got, experts_here * 3 * ADAPTER_RANK
+        with_choices, attention_got
     )
     return (
         grad_inputs[None],

time: 210 us -> 208 us (level)
  Pallas kernels: 137 us -> 133 us
    pallas_call x12, Pallas kernels: 137 us -> 133 us  [call(): pl.pallas_call(kernel, grid_spec=pltpu.PrefetchScalarGridSpec(num_scalar_...]
  transfers between devices with their start and end apart: 17 -> 17, of which waited for: 5 -> 5; matrix products, arithmetic and copies ran while one was open for 4% -> 5% of each run, Pallas kernels for 63% -> 63%
where the time goes in v4:
time: 208 us; the launch traced here: 207 us
  Pallas kernels  133 us (64%)
  starting transfers between devices  33.3 us (16%)
  waiting for transfers between devices  25 us (12%)
  local copies, waits for them, and re-layouts  8.94 us (4%)
  other arithmetic  4.46 us (2%)
  between operations  2.17 us (1%)
    pallas_call x12, Pallas kernels, call(): pl.pallas_call(kernel, grid_spec=pltpu.PrefetchScalarGridSpec(num_scalar_...  133 us
    ppermute x6, starting transfers between devices, send_back(): lax.ppermute(b, 'ctx', rotation(size, -1 - j))  13.1 us
    ppermute x6, waiting for transfers between devices, send_back(): lax.ppermute(b, 'ctx', rotation(size, -1 - j))  12.1 us
    ppermute x1, waiting for transfers between devices, shards(): step(after(inputs[0], cosine, sine, bias, bias_t, router_t, scalars, cot_...  9.71 us
    ppermute x6, starting transfers between devices, rotations(): lax.ppermute(block, 'ctx', rotation(size, j))  9.32 us
    all_to_all x1, starting transfers between devices, shards(): attention_got = lax.all_to_all(attention_send, 'dp', 0, 0, tiled=True)  4.21 us
  transfers between devices with their start and end apart: 17, of which 5 were waited for; matrix products, arithmetic and copies ran while one was open for 5% of the time, Pallas kernels for 63%

profile of v4, /device:TPU:0, one launch (start us, length us, event | category | flops | bytes accessed | tf_op | source)
XLA Modules:
  0.0 207.1 jit_solution(13446231218203201065)
XLA Ops:
  0.7 3.1 %collective-permute-start = (bf16[128,1536]{1,0:T(8,128)(2,1)}, bf16[128,1536]{1,0:T(8,128)(2,1)S(1)}, u32[]{:S(2)}, u32[]{:S(2)}) collective-permute-start(bf16[128,1536]{1,0:T(8,128)(2,1)} %bitcast.30), channel_id=1, source_target_pairs={{0,1},{1,2},{2,3},{3,0},{4,5},{5,6},{6,7},{7,4},{8,9},{9,10},{10,1... | collective-permute-start | bytes 1179656 | tf_op jit(solution)/shard_map/ppermute | solution.py:934
  5.0 0.8 copy.38
  7.3 1.0 fusion.1
  8.9 1.7 pad.4.refs_3_.refs_13_
  10.6 1.3 pad_maximum_fusion.1
  11.9 3.2 %collective-permute-done.refs_1_.refs_0_ = bf16[128,1536]{1,0:T(8,128)(2,1)S(1)} collective-permute-done((bf16[128,1536]{1,0:T(8,128)(2,1)}, bf16[128,1536]{1,0:T(8,128)(2,1)S(1)}, u32[]{:S(2)}, u32[]{:S(2)}) %collective-permute-start) | collective-permute-done | bytes 393248 | tf_op jit(solution)/shard_map/ppermute | solution.py:934
  15.1 1.3 copy.40.refs_16_
  17.6 9.7 %collective-permute-done.1.refs_2_.refs_1_ = bf16[128,1536]{1,0:T(8,128)(2,1)} collective-permute-done((bf16[128,1536]{1,0:T(8,128)(2,1)S(1)}, bf16[128,1536]{1,0:T(8,128)(2,1)}, u32[]{:S(2)}, u32[]{:S(2)}) %collective-permute-start.1) | collective-permute-done | bytes 393248 | tf_op jit(solution)/shard_map/ppermute | solution.py:935
  27.3 12.2 %shard_map.285 = (bf16[128,1536]{1,0:T(8,128)(2,1)}, bf16[128,1536]{1,0:T(8,128)(2,1)}, bf16[128,1536]{1,0:T(8,128)(2,1)}, bf16[128,1024]{1,0:T(8,128)(2,1)}, bf...) custom-call(s32[3]{0:T(128)} %pad_add_fusion.scalars, ...), custom_call_target="tpu_custom_call" | custom-call | flops 10000000000 | tf_op jit(solution)/shard_map/pallas_call | solution.py:102
  39.6 4.4 %collective-permute-start.3 = (bf16[128,1664]{1,0:T(8,128)(2,1)S(1)}, bf16[128,1664]{1,0:T(8,128)(2,1)S(1)}, u32[]{:S(2)}, u32[]{:S(2)}) collective-permute-start(bf16[128,1664]{1,0:T(8,128)(2,1)S(1)} %pad_maximum_fusion.refs_1_.refs_17_), channel_id=1, source_target_pairs={{0,2},{1,3},{2,0},{3,1},{4,6},{5,7},{6,4},{7,5},{8,10},{9,11},{10,... | collective-permute-start | bytes 1277960 | tf_op jit(solution)/shard_map/ppermute | solution.py:59
  44.0 8.7 %shard_map.286 = (bf16[128,1536]{1,0:T(8,128)(2,1)}, bf16[128,1024]{1,0:T(8,128)(2,1)}, bf16[128,1024]{1,0:T(8,128)(2,1)}, bf16[128,1536]{1,0:T(8,128)(2,1)}, bf16[128,48]{1,0:T(8,128)(2,1)}) custom-call(s32[3]{0:T(128)} %pad_add_fusion.scalars, bf16[128,1536]{1,0:T(8,128)(2,1)} %collective-permute-done.4.refs_0_.refs_2_, ...), custom_call_target="tpu_custom_call" | custom-call | flops 10000000000 | tf_op jit(solution)/shard_map/pallas_call | solution.py:102
  52.7 19.7 %shard_map.287 = (bf16[256,1536]{1,0:T(8,128)(2,1)}, bf16[256,1536]{1,0:T(8,128)(2,1)}, bf16[512,1536]{1,0:T(8,128)(2,1)}, bf16[128,16]{1,0:T(8,128)(2,1)}, f32[128,1536]{1,0:T(8,128)}, /*index=5*/f32[128,1]{1,0:T(8,128)}) custom-call(s32[3]{0:T(128)} %pad_add_fusion.scalars, bf16[128,1536]{1,0:T(8,128)(2,1)} %copy-done.6, ...), custom_call_target="tpu_custom_call" | custom-call | tf_op jit(solution)/shard_map/pallas_call | solution.py:102
  73.4 24.7 %shard_map.288 = (bf16[128,1664]{1,0:T(8,128)(2,1)}, bf16[128,1664]{1,0:T(8,128)(2,1)}, f32[240,1536]{1,0:T(8,128)}, f32[5,48,512]{2,1,0:T(8,128)}) custom-call(s32[3]{0:T(128)} %pad_add_fusion.scalars, bf16[128,1664]{1,0:T(8,128)(2,1)} %copy-done.4, bf16[128,1664]{1,0:T(8,128)(2,1)} %copy-done.5, bf16[256,1536]{1,0:T(8,128)(2,1)} %get-tuple-element.89.refs_2_, ...), custom_call_target="tpu_custom_call" | custom-call | tf_op jit(solution)/shard_map/pallas_call | solution.py:102
  98.0 5.4 %collective-permute-start.5 = (bf16[128,1664]{1,0:T(8,128)(2,1)}, bf16[128,1664]{1,0:T(8,128)(2,1)S(1)}, u32[]{:S(2)}, u32[]{:S(2)}) collective-permute-start(bf16[128,1664]{1,0:T(8,128)(2,1)} %get-tuple-element.90), channel_id=1, source_target_pairs={{0,3},{1,0},{2,1},{3,2},{4,7},{5,4},{6,5},{7,6},{8,11},{9,8},{10,9... | collective-permute-start | bytes 1277960 | tf_op jit(solution)/shard_map/ppermute | solution.py:64
  103.5 0.8 copy-done.3
  104.2 25.3 %shard_map.289 = (bf16[128,1664]{1,0:T(8,128)(2,1)}, bf16[128,1664]{1,0:T(8,128)(2,1)}, bf16[8,256,256]{2,1,0:T(8,128)(2,1)}, f32[128,128]{1,0:T(8,128)}) custom-call(s32[3]{0:T(128)} %pad_add_fusion.scalars, bf16[128,1664]{1,0:T(8,128)(2,1)} %copy-done.3, bf16[128,1664]{1,0:T(8,128)(2,1)} %copy-done.1, bf16[256,1536]{1,0:T(8,128)(2,1)} %get-tuple-element.92.refs_2_, ...), custom_call_target="tpu_custom_call" | custom-call | tf_op jit(solution)/shard_map/pallas_call | solution.py:102
  130.2 3.6 %all-to-all-start = ((bf16[8,256,256]{2,1,0:T(8,128)(2,1)}), bf16[8,256,256]{2,1,0:T(8,128)(2,1)S(1)}, u32[]{:S(2)}, u32[]{:S(2)}) async-start(bf16[8,256,256]{2,1,0:T(8,128)(2,1)} %get-tuple-element.110), calls=%async_computation | async-start | bytes 2097152 | tf_op jit(solution)/shard_map/all_to_all | solution.py:980
  133.9 7.2 %collective-permute-done.8.refs_2_ = bf16[128,1664]{1,0:T(8,128)(2,1)} collective-permute-done((bf16[128,1664]{1,0:T(8,128)(2,1)}, bf16[128,1664]{1,0:T(8,128)(2,1)}, u32[]{:S(2)}, u32[]{:S(2)}) %collective-permute-start.8) | collective-permute-done | bytes 426016 | tf_op jit(solution)/shard_map/ppermute | solution.py:64
  141.1 16.0 %shard_map.290 = (f32[128,1536]{1,0:T(8,128)}, bf16[128,1536]{1,0:T(8,128)(2,1)}, bf16[128,16]{1,0:T(8,128)(2,1)}, bf16[128,1536]{1,0:T(8,128)(2,1)}, bf16[128,1...) custom-call(s32[3]{0:T(128)} %pad_add_fusion.scalars, ...), custom_call_target="tpu_custom_call" | custom-call | flops 20000000000 | tf_op jit(solution)/shard_map/pallas_call | solution.py:102
  157.1 1.8 collective-permute-start.9
  158.9 3.8 %shard_map.291.refs_3_ = bf16[21,32,128]{2,1,0:T(8,128)(2,1)} custom-call(s32[3]{0:T(128)} %pad_add_fusion.scalars, bf16[128,1024]{1,0:T(8,128)(2,1)} %get-tuple-element.101.refs_0_, bf16[128,1024]{1,0:T(8,128)(2,1)} %get-tuple-element.119.refs_1_, bf16[128,1024]{1,0:T(8,128)(2,1)} %get-tuple-element.120.refs_2_, ...), custom_call_target="tpu_custom_call" | custom-call | tf_op jit(solution)/shard_map/pallas_call | solution.py:102
  162.6 2.4 %collective-permute-done.9.refs_0_ = bf16[128,1024]{1,0:T(8,128)(2,1)S(1)} collective-permute-done((bf16[128,1024]{1,0:T(8,128)(2,1)}, bf16[128,1024]{1,0:T(8,128)(2,1)S(1)}, u32[]{:S(2)}, u32[]{:S(2)}) %collective-permute-start.9) | collective-permute-done | bytes 262176 | tf_op jit(solution)/shard_map/ppermute | solution.py:64
  165.1 4.7 %collective-permute-start.11 = (bf16[21,32,128]{2,1,0:T(8,128)(2,1)}, bf16[21,32,128]{2,1,0:T(8,128)(2,1)S(1)}, u32[]{:S(2)}, u32[]{:S(2)}) collective-permute-start(bf16[21,32,128]{2,1,0:T(8,128)(2,1)} %shard_map.291.refs_3_), channel_id=1, source_target_pairs={{0,2},{1,3},{2,0},{3,1},{4,6},{5,7},{6,4},{7,5},{8,10},{9,11},{10,... | collective-permute-start | bytes 516104 | tf_op jit(solution)/shard_map/ppermute | solution.py:59
  170.8 5.8 %shard_map.292.refs_5_ = f32[128,1536]{1,0:T(8,128)} custom-call(s32[3]{0:T(128)} %pad_add_fusion.scalars, bf16[128,1536]{1,0:T(8,128)(2,1)} %get-tuple-element.127.refs_8_.gq.refs_4_, bf16[1536,1536]{1,0:T(8,128)(2,1)} %query_w.1), custom_call_target="tpu_custom_call" | custom-call | tf_op jit(solution)/shard_map/pallas_call | solution.py:102
  176.6 3.9 %shard_map.293 = (f32[8,5,32,192]{3,2,1,0:T(8,128)}, f32[8,5,2,16,64]{4,3,2,1,0:T(8,128)}, f32[8,5,16,64]{3,2,1,0:T(8,128)}, f32[8,5,16,192]{3,2,1,0:T(8,128)}) custom-call(s32[11]{0:T(128)} %pad_add_fusion.1.scalars, bf16[8,256,256]{2,1,0:T(8,128)(2,1)} %copy-done), custom_call_target="tpu_custom_call" | custom-call | tf_op jit(solution)/shard_map/pallas_call | solution.py:102
  180.5 1.4 collective-permute-start.13
  181.9 3.8 %collective-permute-start.14 = (bf16[128,1024]{1,0:T(8,128)(2,1)S(1)}, bf16[128,1024]{1,0:T(8,128)(2,1)S(1)}, u32[]{:S(2)}, u32[]{:S(2)}) collective-permute-start(bf16[128,1024]{1,0:T(8,128)(2,1)S(1)} %copy-done.8), channel_id=1, source_target_pairs={{0,1},{1,2},{2,3},{3,0},{4,5},{5,6},{6,7},{7,4},{8,9},{9,10},{10,1... | collective-permute-start | bytes 786440 | tf_op jit(solution)/shard_map/ppermute | solution.py:64
  185.8 4.2 %shard_map.294 = bf16[8,96,256]{2,1,0:T(8,128)(2,1)} custom-call(s32[3]{0:T(128)} %pad_add_fusion.scalars, bf16[21,32,128]{2,1,0:T(8,128)(2,1)} %copy-done.10, bf16[21,32,128]{2,1,0:T(8,128)(2,1)} %copy-done.11, bf16[21,32,128]{2,1,0:T(8,128)(2,1)} %collective-permute-done.12.refs_2_, bf16[21,32,128]{2,1,0:T(8,128)(2,1)} %shard_map.291.refs_3_, ...), custom_call_target="tpu_custom_call" | custom-call | tf_op jit(solution)/shard_map/pallas_call | solution.py:102
  190.0 4.2 %all-to-all-start.1 = ((bf16[8,96,256]{2,1,0:T(8,128)(2,1)}), bf16[8,96,256]{2,1,0:T(8,128)(2,1)S(1)}, u32[]{:S(2)}, u32[]{:S(2)}) async-start(bf16[8,96,256]{2,1,0:T(8,128)(2,1)} %shard_map.294), calls=%async_computation.1 | async-start | bytes 786432 | tf_op jit(solution)/shard_map/all_to_all | solution.py:998
  194.2 2.4 %collective-permute-done.13.refs_1_ = bf16[128,1024]{1,0:T(8,128)(2,1)S(1)} collective-permute-done((bf16[128,1024]{1,0:T(8,128)(2,1)S(1)}, bf16[128,1024]{1,0:T(8,128)(2,1)S(1)}, u32[]{:S(2)}, u32[]{:S(2)}) %collective-permute-start.13) | collective-permute-done | bytes 262176 | tf_op jit(solution)/shard_map/ppermute | solution.py:64
  197.5 6.1 %shard_map.295 = f32[128,1536]{1,0:T(8,128)} custom-call(s32[3]{0:T(128)} %pad_add_fusion.scalars, bf16[128,1024]{1,0:T(8,128)(2,1)} %copy-done.16, bf16[128,1024]{1,0:T(8,128)(2,1)} %copy-done.17, bf16[128,1024]{1,0:T(8,128)(2,1)} %copy-done.18, bf16[128,1024]{1,0:T(8,128)(2,1)} %get-tuple-element.105.refs_3_, ...), custom_call_target="tpu_custom_call" | custom-call | flops 20000000000 | tf_op jit(solution)/shard_map/pallas_call | solution.py:102
  204.4 2.7 %shard_map.296 = (f32[8,48,192]{2,1,0:T(8,128)}, f32[8,16,192]{2,1,0:T(8,128)}, f32[8,2,16,64]{3,2,1,0:T(8,128)}, f32[8,16,192]{2,1,0:T(8,128)}, f32[8,16,192]{2,1,0:T(8,128)}) custom-call(s32[11]{0:T(128)} %pad_add_fusion.1.scalars, bf16[8,96,256]{2,1,0:T(8,128)(2,1)} %copy-done.2), custom_call_target="tpu_custom_call" | custom-call | tf_op jit(solution)/shard_map/pallas_call | solution.py:102
  (71 shorter events, 7.5 us)
Async XLA Ops:
  0.6 11.2 %copy-start.7 = (bf16[1,128,1536]{2,1,0:T(8,128)(2,1)S(1)}, bf16[1,128,1536]{2,1,0:T(8,128)(2,1)}, u32[]{:S(2)}) copy-start(bf16[1,128,1536]{2,1,0:T(8,128)(2,1)} %param.43) | copy-start | bytes 1179652
  0.7 14.4 %collective-permute-start = (bf16[128,1536]{1,0:T(8,128)(2,1)}, bf16[128,1536]{1,0:T(8,128)(2,1)S(1)}, u32[]{:S(2)}, u32[]{:S(2)}) collective-permute-start(bf16[128,1536]{1,0:T(8,128)(2,1)} %bitcast.30), channel_id=1, source_target_pairs={{0,1},{1,2},{2,3},{3,0},{4,5},{5,6},{6,7},{7,4},{8,9},{9,10},{10,1... | collective-permute-start | bytes 1179656 | tf_op jit(solution)/shard_map/ppermute | solution.py:934
  6.5 9.9 %copy-start.12 = (f32[1536]{0:T(1024)S(1)}, f32[1536]{0:T(1024)}, u32[]{:S(2)}) copy-start(f32[1536]{0:T(1024)} %param.26) | copy-start | bytes 18436
  6.5 10.5 %copy-start.13 = (f32[1536]{0:T(1024)S(1)}, f32[1536]{0:T(1024)}, u32[]{:S(2)}) copy-start(f32[1536]{0:T(1024)} %param.27) | copy-start | bytes 18436
  11.9 32.1 %copy-start.1 = (bf16[128,1664]{1,0:T(8,128)(2,1)}, bf16[128,1664]{1,0:T(8,128)(2,1)S(1)}, u32[]{:S(2)}) copy-start(bf16[128,1664]{1,0:T(8,128)(2,1)S(1)} %pad_maximum_fusion.refs_1_.refs_17_) | copy-start | bytes 1277956
  15.1 12.2 %copy-start.6 = (bf16[128,1536]{1,0:T(8,128)(2,1)}, bf16[128,1536]{1,0:T(8,128)(2,1)S(1)}, u32[]{:S(2)}) copy-start(bf16[128,1536]{1,0:T(8,128)(2,1)S(1)} %collective-permute-done.refs_1_.refs_0_) | copy-start | bytes 1179652
  15.1 12.2 %collective-permute-start.1 = (bf16[128,1536]{1,0:T(8,128)(2,1)S(1)}, bf16[128,1536]{1,0:T(8,128)(2,1)}, u32[]{:S(2)}, u32[]{:S(2)}) collective-permute-start(bf16[128,1536]{1,0:T(8,128)(2,1)S(1)} %collective-permute-done.refs_1_.refs_0_), channel_id=1, source_target_pairs={{0,1},{1,2},{2,3},{3,0},{4,5},{5,6},{6,7},{7,4},{8,9},{9,10},{10,1... | collective-permute-start | bytes 1179656 | tf_op jit(solution)/shard_map/ppermute | solution.py:935
  27.3 16.7 %collective-permute-start.4 = (bf16[128,1536]{1,0:T(8,128)(2,1)}, bf16[128,1536]{1,0:T(8,128)(2,1)}, u32[]{:S(2)}, u32[]{:S(2)}) collective-permute-start(bf16[128,1536]{1,0:T(8,128)(2,1)} %collective-permute-done.1.refs_2_.refs_1_), channel_id=1, source_target_pairs={{0,1},{1,2},{2,3},{3,0},{4,5},{5,6},{6,7},{7,4},{8,9},{9,10},{10,1... | collective-permute-start | bytes 1179656 | tf_op jit(solution)/shard_map/ppermute | solution.py:937
  39.5 32.9 %collective-permute-start.2 = (bf16[128,1664]{1,0:T(8,128)(2,1)S(1)}, bf16[128,1664]{1,0:T(8,128)(2,1)S(1)}, u32[]{:S(2)}, u32[]{:S(2)}) collective-permute-start(bf16[128,1664]{1,0:T(8,128)(2,1)S(1)} %pad_maximum_fusion.refs_1_.refs_17_), channel_id=1, source_target_pairs={{0,1},{1,2},{2,3},{3,0},{4,5},{5,6},{6,7},{7,4},{8,9},{9,10},{10,1... | collective-permute-start | bytes 1277960 | tf_op jit(solution)/shard_map/ppermute | solution.py:59
  39.6 32.9 %collective-permute-start.3 = (bf16[128,1664]{1,0:T(8,128)(2,1)S(1)}, bf16[128,1664]{1,0:T(8,128)(2,1)S(1)}, u32[]{:S(2)}, u32[]{:S(2)}) collective-permute-start(bf16[128,1664]{1,0:T(8,128)(2,1)S(1)} %pad_maximum_fusion.refs_1_.refs_17_), channel_id=1, source_target_pairs={{0,2},{1,3},{2,0},{3,1},{4,6},{5,7},{6,4},{7,5},{8,10},{9,11},{10,... | collective-permute-start | bytes 1277960 | tf_op jit(solution)/shard_map/ppermute | solution.py:59
  44.0 59.5 %collective-permute-start.7 = (bf16[128,1664]{1,0:T(8,128)(2,1)S(1)}, bf16[128,1664]{1,0:T(8,128)(2,1)S(1)}, u32[]{:S(2)}, u32[]{:S(2)}) collective-permute-start(bf16[128,1664]{1,0:T(8,128)(2,1)S(1)} %pad_maximum_fusion.refs_1_.refs_17_), channel_id=1, source_target_pairs={{0,3},{1,0},{2,1},{3,2},{4,7},{5,4},{6,5},{7,6},{8,11},{9,8},{10,9... | collective-permute-start | bytes 1277960 | tf_op jit(solution)/shard_map/ppermute | solution.py:59
  72.5 0.9 copy-start.5
  98.0 31.5 %collective-permute-start.5 = (bf16[128,1664]{1,0:T(8,128)(2,1)}, bf16[128,1664]{1,0:T(8,128)(2,1)S(1)}, u32[]{:S(2)}, u32[]{:S(2)}) collective-permute-start(bf16[128,1664]{1,0:T(8,128)(2,1)} %get-tuple-element.90), channel_id=1, source_target_pairs={{0,3},{1,0},{2,1},{3,2},{4,7},{5,4},{6,5},{7,6},{8,11},{9,8},{10,9... | collective-permute-start | bytes 1277960 | tf_op jit(solution)/shard_map/ppermute | solution.py:64
  103.4 26.1 %collective-permute-start.6 = (bf16[128,1664]{1,0:T(8,128)(2,1)}, bf16[128,1664]{1,0:T(8,128)(2,1)S(1)}, u32[]{:S(2)}, u32[]{:S(2)}) collective-permute-start(bf16[128,1664]{1,0:T(8,128)(2,1)} %get-tuple-element.91), channel_id=1, source_target_pairs={{0,2},{1,3},{2,0},{3,1},{4,6},{5,7},{6,4},{7,5},{8,10},{9,11},{10,... | collective-permute-start | bytes 1277960 | tf_op jit(solution)/shard_map/ppermute | solution.py:64
  129.5 11.6 %copy-start.14 = (bf16[128,1664]{1,0:T(8,128)(2,1)}, bf16[128,1664]{1,0:T(8,128)(2,1)S(1)}, u32[]{:S(2)}) copy-start(bf16[128,1664]{1,0:T(8,128)(2,1)S(1)} %collective-permute-done.5.refs_0_) | copy-start | bytes 1277956
  129.6 11.6 %copy-start.15 = (bf16[128,1664]{1,0:T(8,128)(2,1)}, bf16[128,1664]{1,0:T(8,128)(2,1)S(1)}, u32[]{:S(2)}) copy-start(bf16[128,1664]{1,0:T(8,128)(2,1)S(1)} %collective-permute-done.6.refs_1_) | copy-start | bytes 1277956
  129.6 11.5 %collective-permute-start.8 = (bf16[128,1664]{1,0:T(8,128)(2,1)}, bf16[128,1664]{1,0:T(8,128)(2,1)}, u32[]{:S(2)}, u32[]{:S(2)}) collective-permute-start(bf16[128,1664]{1,0:T(8,128)(2,1)} %get-tuple-element.96), channel_id=1, source_target_pairs={{0,1},{1,2},{2,3},{3,0},{4,5},{5,6},{6,7},{7,4},{8,9},{9,10},{10,1... | collective-permute-start | bytes 1277960 | tf_op jit(solution)/shard_map/ppermute | solution.py:64
  130.2 28.6 %all-to-all-start = ((bf16[8,256,256]{2,1,0:T(8,128)(2,1)}), bf16[8,256,256]{2,1,0:T(8,128)(2,1)S(1)}, u32[]{:S(2)}, u32[]{:S(2)}) async-start(bf16[8,256,256]{2,1,0:T(8,128)(2,1)} %get-tuple-element.110), calls=%async_computation | async-start | bytes 2097152 | tf_op jit(solution)/shard_map/all_to_all | solution.py:980
  157.1 8.0 %collective-permute-start.9 = (bf16[128,1024]{1,0:T(8,128)(2,1)}, bf16[128,1024]{1,0:T(8,128)(2,1)S(1)}, u32[]{:S(2)}, u32[]{:S(2)}) collective-permute-start(bf16[128,1024]{1,0:T(8,128)(2,1)} %get-tuple-element.101.refs_0_), channel_id=1, source_target_pairs={{0,3},{1,0},{2,1},{3,2},{4,7},{5,4},{6,5},{7,6},{8,11},{9,8},{10,9... | collective-permute-start | bytes 786440 | tf_op jit(solution)/shard_map/ppermute | solution.py:64
  158.9 17.8 %copy-start = (bf16[8,256,256]{2,1,0:T(8,128)(2,1)}, bf16[8,256,256]{2,1,0:T(8,128)(2,1)S(1)}, u32[]{:S(2)}) copy-start(bf16[8,256,256]{2,1,0:T(8,128)(2,1)S(1)} %all-to-all-done.got) | copy-start | bytes 3145732
  165.1 4.8 %copy-start.16 = (bf16[128,1024]{1,0:T(8,128)(2,1)}, bf16[128,1024]{1,0:T(8,128)(2,1)S(1)}, u32[]{:S(2)}) copy-start(bf16[128,1024]{1,0:T(8,128)(2,1)S(1)} %collective-permute-done.9.refs_0_) | copy-start | bytes 786436
  165.1 15.5 %collective-permute-start.10 = (bf16[21,32,128]{2,1,0:T(8,128)(2,1)}, bf16[21,32,128]{2,1,0:T(8,128)(2,1)S(1)}, u32[]{:S(2)}, u32[]{:S(2)}) collective-permute-start(bf16[21,32,128]{2,1,0:T(8,128)(2,1)} %shard_map.291.refs_3_), channel_id=1, source_target_pairs={{0,1},{1,2},{2,3},{3,0},{4,5},{5,6},{6,7},{7,4},{8,9},{9,10},{10,1... | collective-permute-start | bytes 516104 | tf_op jit(solution)/shard_map/ppermute | solution.py:59
  165.1 15.5 %collective-permute-start.11 = (bf16[21,32,128]{2,1,0:T(8,128)(2,1)}, bf16[21,32,128]{2,1,0:T(8,128)(2,1)S(1)}, u32[]{:S(2)}, u32[]{:S(2)}) collective-permute-start(bf16[21,32,128]{2,1,0:T(8,128)(2,1)} %shard_map.291.refs_3_), channel_id=1, source_target_pairs={{0,2},{1,3},{2,0},{3,1},{4,6},{5,7},{6,4},{7,5},{8,10},{9,11},{10,... | collective-permute-start | bytes 516104 | tf_op jit(solution)/shard_map/ppermute | solution.py:59
  169.8 10.7 %collective-permute-start.12 = (bf16[21,32,128]{2,1,0:T(8,128)(2,1)}, bf16[21,32,128]{2,1,0:T(8,128)(2,1)}, u32[]{:S(2)}, u32[]{:S(2)}) collective-permute-start(bf16[21,32,128]{2,1,0:T(8,128)(2,1)} %shard_map.291.refs_3_), channel_id=1, source_target_pairs={{0,3},{1,0},{2,1},{3,2},{4,7},{5,4},{6,5},{7,6},{8,11},{9,8},{10,9... | collective-permute-start | bytes 516104 | tf_op jit(solution)/shard_map/ppermute | solution.py:59
  170.8 9.7 %copy-start.9 = (bf16[128,1024]{1,0:T(8,128)(2,1)S(1)}, bf16[128,1024]{1,0:T(8,128)(2,1)}, u32[]{:S(2)}) copy-start(bf16[128,1024]{1,0:T(8,128)(2,1)} %get-tuple-element.119.refs_1_) | copy-start | bytes 786436
  170.8 11.1 %copy-start.8 = (bf16[128,1024]{1,0:T(8,128)(2,1)S(1)}, bf16[128,1024]{1,0:T(8,128)(2,1)}, u32[]{:S(2)}) copy-start(bf16[128,1024]{1,0:T(8,128)(2,1)} %get-tuple-element.120.refs_2_) | copy-start | bytes 786436
  180.5 5.3 %copy-start.10 = (bf16[21,32,128]{2,1,0:T(8,128)(2,1)}, bf16[21,32,128]{2,1,0:T(8,128)(2,1)S(1)}, u32[]{:S(2)}) copy-start(bf16[21,32,128]{2,1,0:T(8,128)(2,1)S(1)} %collective-permute-done.10.refs_0_) | copy-start | bytes 516100
  180.5 5.3 %copy-start.11 = (bf16[21,32,128]{2,1,0:T(8,128)(2,1)}, bf16[21,32,128]{2,1,0:T(8,128)(2,1)S(1)}, u32[]{:S(2)}) copy-start(bf16[21,32,128]{2,1,0:T(8,128)(2,1)S(1)} %collective-permute-done.11.refs_1_) | copy-start | bytes 516100
  180.5 16.1 %collective-permute-start.13 = (bf16[128,1024]{1,0:T(8,128)(2,1)S(1)}, bf16[128,1024]{1,0:T(8,128)(2,1)S(1)}, u32[]{:S(2)}, u32[]{:S(2)}) collective-permute-start(bf16[128,1024]{1,0:T(8,128)(2,1)S(1)} %copy-done.9), channel_id=1, source_target_pairs={{0,2},{1,3},{2,0},{3,1},{4,6},{5,7},{6,4},{7,5},{8,10},{9,11},{10,... | collective-permute-start | bytes 786440 | tf_op jit(solution)/shard_map/ppermute | solution.py:64
  181.9 14.8 %collective-permute-start.14 = (bf16[128,1024]{1,0:T(8,128)(2,1)S(1)}, bf16[128,1024]{1,0:T(8,128)(2,1)S(1)}, u32[]{:S(2)}, u32[]{:S(2)}) collective-permute-start(bf16[128,1024]{1,0:T(8,128)(2,1)S(1)} %copy-done.8), channel_id=1, source_target_pairs={{0,1},{1,2},{2,3},{3,0},{4,5},{5,6},{6,7},{7,4},{8,9},{9,10},{10,1... | collective-permute-start | bytes 786440 | tf_op jit(solution)/shard_map/ppermute | solution.py:64
  190.0 13.6 %all-to-all-start.1 = ((bf16[8,96,256]{2,1,0:T(8,128)(2,1)}), bf16[8,96,256]{2,1,0:T(8,128)(2,1)S(1)}, u32[]{:S(2)}, u32[]{:S(2)}) async-start(bf16[8,96,256]{2,1,0:T(8,128)(2,1)} %shard_map.294), calls=%async_computation.1 | async-start | bytes 786432 | tf_op jit(solution)/shard_map/all_to_all | solution.py:998
  196.7 0.8 copy-start.18
  (4 other events, 3.0 us)

commit v5 on v4

--- a/solution.py
+++ b/solution.py
@@ -55,7 +55,9 @@
     return lax.optimization_barrier((value, *others))[0]
 
 
-def rotations(block, size):
+def rotations(block, size, count=None, first=1):
+    if count is not None:
+        return [lax.ppermute(block, "ctx", rotation(size, first + j)) for j in range(count)]
     return [lax.ppermute(block, "ctx", rotation(size, j)) for j in range(1, size)] + [block]
 
 
@@ -948,7 +950,7 @@
             all_of += some_of
         now = after(scalars, q[0])
         if cots is None:
-            cots = rotations(after(cot_own, q[0]), ctx_size)
+            cots = rotations(after(cot_own, q[0]), ctx_size, half)
     q, k, v, normed, lora_in = [a[1:] + a[:1] for a in (q, k, v, normed, lora_in)]
     tables = (
         gate_up_weight,
@@ -963,6 +965,8 @@
         scalars, inputs, q, k, v, bias, projection_weight, proj_in_t, adapter_projection_output,
         gain_ffn,
     )
+    cots += rotations(after(cot_own, normed_first), ctx_size, ctx_size - 1 - half, half + 1)
+    cots.append(cot_own)
     *rows_first, wide, narrow = experts(
         scalars, dp_size, cots[:half], normed_first, router_t, tables, None
     )

time: 208 us -> 211 us (1.014)
  waiting for transfers between devices: 25 us -> 31.2 us
  starting transfers between devices: 33.3 us -> 29.2 us
    ppermute x6, waiting for transfers between devices: 12.1 us -> 17.1 us  [send_back(): lax.ppermute(b, 'ctx', rotation(size, -1 - j))]
    ppermute x0 -> x3, starting transfers between devices: none -> 4.69 us  [rotations(): lax.ppermute(block, 'ctx', rotation(size, first + j))]
    ppermute x6 -> x3, starting transfers between devices: 9.32 us -> 4.74 us  [rotations(): lax.ppermute(block, 'ctx', rotation(size, j))]
    ppermute x6, starting transfers between devices: 13.1 us -> 9.47 us  [send_back(): lax.ppermute(b, 'ctx', rotation(size, -1 - j))]
    unnamed x38 -> x40, local copies, waits for them, and re-layouts: 3.23 us -> 4.79 us
  transfers between devices with their start and end apart: 17 -> 17, of which waited for: 5 -> 6; matrix products, arithmetic and copies ran while one was open for 5% -> 5% of each run, Pallas kernels for 63% -> 62%
where the time goes in v5:
time: 211 us
  Pallas kernels  133 us (63%)
  waiting for transfers between devices  31.2 us (15%)
  starting transfers between devices  29.2 us (14%)
  local copies, waits for them, and re-layouts  10.5 us (5%)
  other arithmetic  4.38 us (2%)
  between operations  2.18 us (1%)
    pallas_call x12, Pallas kernels, call(): pl.pallas_call(kernel, grid_spec=pltpu.PrefetchScalarGridSpec(num_scalar_...  133 us
    ppermute x6, waiting for transfers between devices, send_back(): lax.ppermute(b, 'ctx', rotation(size, -1 - j))  17.1 us
    ppermute x1, waiting for transfers between devices, shards(): step(after(inputs[0], cosine, sine, bias, bias_t, router_t, scalars, cot_...  9.71 us
    ppermute x6, starting transfers between devices, send_back(): lax.ppermute(b, 'ctx', rotation(size, -1 - j))  9.47 us
    unnamed x40, local copies, waits for them, and re-layouts  4.79 us
    ppermute x3, starting transfers between devices, rotations(): lax.ppermute(block, 'ctx', rotation(size, j))  4.74 us
    ppermute x3, starting transfers between devices, rotations(): lax.ppermute(block, 'ctx', rotation(size, first + j))  4.69 us
  transfers between devices with their start and end apart: 17, of which 6 were waited for; matrix products, arithmetic and copies ran while one was open for 5% of the time, Pallas kernels for 62%

profile of v5, /device:TPU:0, one launch (start us, length us, event | category | flops | bytes accessed | tf_op | source)
XLA Modules:
  0.0 210.7 jit_solution(2471500124593447198)
XLA Ops:
  0.7 3.1 %collective-permute-start = (bf16[128,1536]{1,0:T(8,128)(2,1)}, bf16[128,1536]{1,0:T(8,128)(2,1)S(1)}, u32[]{:S(2)}, u32[]{:S(2)}) collective-permute-start(bf16[128,1536]{1,0:T(8,128)(2,1)} %bitcast.30), channel_id=1, source_target_pairs={{0,1},{1,2},{2,3},{3,0},{4,5},{5,6},{6,7},{7,4},{8,9},{9,10},{10,1... | collective-permute-start | bytes 1179656 | tf_op jit(solution)/shard_map/ppermute | solution.py:936
  5.2 0.8 copy.38
  7.3 1.0 fusion.1
  8.9 1.7 pad.4.refs_3_.refs_13_
  10.5 1.3 pad_maximum_fusion.1
  11.9 3.2 %collective-permute-done.refs_1_.refs_0_ = bf16[128,1536]{1,0:T(8,128)(2,1)S(1)} collective-permute-done((bf16[128,1536]{1,0:T(8,128)(2,1)}, bf16[128,1536]{1,0:T(8,128)(2,1)S(1)}, u32[]{:S(2)}, u32[]{:S(2)}) %collective-permute-start) | collective-permute-done | bytes 393248 | tf_op jit(solution)/shard_map/ppermute | solution.py:936
  15.1 1.3 copy.40.refs_16_
  17.6 9.7 %collective-permute-done.1.refs_2_.refs_1_ = bf16[128,1536]{1,0:T(8,128)(2,1)} collective-permute-done((bf16[128,1536]{1,0:T(8,128)(2,1)S(1)}, bf16[128,1536]{1,0:T(8,128)(2,1)}, u32[]{:S(2)}, u32[]{:S(2)}) %collective-permute-start.1) | collective-permute-done | bytes 393248 | tf_op jit(solution)/shard_map/ppermute | solution.py:937
  27.3 12.3 %shard_map.285 = (bf16[128,1536]{1,0:T(8,128)(2,1)}, bf16[128,1536]{1,0:T(8,128)(2,1)}, bf16[128,1536]{1,0:T(8,128)(2,1)}, bf16[128,1024]{1,0:T(8,128)(2,1)}, bf...) custom-call(s32[3]{0:T(128)} %pad_add_fusion.scalars, ...), custom_call_target="tpu_custom_call" | custom-call | flops 10000000000 | tf_op jit(solution)/shard_map/pallas_call | solution.py:104
  39.8 4.2 %collective-permute-start.2 = (bf16[128,1664]{1,0:T(8,128)(2,1)S(1)}, bf16[128,1664]{1,0:T(8,128)(2,1)S(1)}, u32[]{:S(2)}, u32[]{:S(2)}) collective-permute-start(bf16[128,1664]{1,0:T(8,128)(2,1)S(1)} %pad_maximum_fusion.refs_1_.refs_17_), channel_id=1, source_target_pairs={{0,1},{1,2},{2,3},{3,0},{4,5},{5,6},{6,7},{7,4},{8,9},{9,10},{10,1... | collective-permute-start | bytes 1277960 | tf_op jit(solution)/shard_map/ppermute | solution.py:60
  44.0 8.7 %shard_map.286 = (bf16[128,1536]{1,0:T(8,128)(2,1)}, bf16[128,1024]{1,0:T(8,128)(2,1)}, bf16[128,1024]{1,0:T(8,128)(2,1)}, bf16[128,1536]{1,0:T(8,128)(2,1)}, bf16[128,48]{1,0:T(8,128)(2,1)}) custom-call(s32[3]{0:T(128)} %pad_add_fusion.scalars, bf16[128,1536]{1,0:T(8,128)(2,1)} %collective-permute-done.4.refs_0_.refs_2_, ...), custom_call_target="tpu_custom_call" | custom-call | flops 10000000000 | tf_op jit(solution)/shard_map/pallas_call | solution.py:104
  52.8 19.8 %shard_map.287 = (bf16[256,1536]{1,0:T(8,128)(2,1)}, bf16[256,1536]{1,0:T(8,128)(2,1)}, bf16[512,1536]{1,0:T(8,128)(2,1)}, bf16[128,16]{1,0:T(8,128)(2,1)}, f32[128,1536]{1,0:T(8,128)}, /*index=5*/f32[128,1]{1,0:T(8,128)}) custom-call(s32[3]{0:T(128)} %pad_add_fusion.scalars, bf16[128,1536]{1,0:T(8,128)(2,1)} %copy-done.6, ...), custom_call_target="tpu_custom_call" | custom-call | tf_op jit(solution)/shard_map/pallas_call | solution.py:104
  73.7 24.7 %shard_map.288 = (bf16[128,1664]{1,0:T(8,128)(2,1)}, bf16[128,1664]{1,0:T(8,128)(2,1)}, f32[240,1536]{1,0:T(8,128)}, f32[5,48,512]{2,1,0:T(8,128)}) custom-call(s32[3]{0:T(128)} %pad_add_fusion.scalars, bf16[128,1664]{1,0:T(8,128)(2,1)} %copy-done.4, bf16[128,1664]{1,0:T(8,128)(2,1)} %copy-done.3, bf16[256,1536]{1,0:T(8,128)(2,1)} %get-tuple-element.90.refs_2_, ...), custom_call_target="tpu_custom_call" | custom-call | tf_op jit(solution)/shard_map/pallas_call | solution.py:104
  98.4 1.5 collective-permute-start.5
  99.9 2.0 collective-permute-start.6
  102.6 25.3 %shard_map.289 = (bf16[128,1664]{1,0:T(8,128)(2,1)}, bf16[128,1664]{1,0:T(8,128)(2,1)}, bf16[8,256,256]{2,1,0:T(8,128)(2,1)}, f32[128,128]{1,0:T(8,128)}) custom-call(s32[3]{0:T(128)} %pad_add_fusion.scalars, bf16[128,1664]{1,0:T(8,128)(2,1)} %copy-done.5, bf16[128,1664]{1,0:T(8,128)(2,1)} %copy-done.1, bf16[256,1536]{1,0:T(8,128)(2,1)} %get-tuple-element.94.refs_2_, ...), custom_call_target="tpu_custom_call" | custom-call | tf_op jit(solution)/shard_map/pallas_call | solution.py:104
  128.9 3.8 %all-to-all-start = ((bf16[8,256,256]{2,1,0:T(8,128)(2,1)}), bf16[8,256,256]{2,1,0:T(8,128)(2,1)S(1)}, u32[]{:S(2)}, u32[]{:S(2)}) async-start(bf16[8,256,256]{2,1,0:T(8,128)(2,1)} %get-tuple-element.112), calls=%async_computation | async-start | bytes 2097152 | tf_op jit(solution)/shard_map/all_to_all | solution.py:984
  132.7 7.0 %collective-permute-done.8.refs_2_ = bf16[128,1664]{1,0:T(8,128)(2,1)S(1)} collective-permute-done((bf16[128,1664]{1,0:T(8,128)(2,1)}, bf16[128,1664]{1,0:T(8,128)(2,1)S(1)}, u32[]{:S(2)}, u32[]{:S(2)}) %collective-permute-start.8) | collective-permute-done | bytes 426016 | tf_op jit(solution)/shard_map/ppermute | solution.py:66
  140.4 16.0 %shard_map.290 = (f32[128,1536]{1,0:T(8,128)}, bf16[128,1536]{1,0:T(8,128)(2,1)}, bf16[128,16]{1,0:T(8,128)(2,1)}, bf16[128,1536]{1,0:T(8,128)(2,1)}, bf16[128,1...) custom-call(s32[3]{0:T(128)} %pad_add_fusion.scalars, ...), custom_call_target="tpu_custom_call" | custom-call | flops 20000000000 | tf_op jit(solution)/shard_map/pallas_call | solution.py:104
  156.3 1.8 collective-permute-start.9
  158.1 3.7 %shard_map.291.refs_3_ = bf16[21,32,128]{2,1,0:T(8,128)(2,1)} custom-call(s32[3]{0:T(128)} %pad_add_fusion.scalars, bf16[128,1024]{1,0:T(8,128)(2,1)} %get-tuple-element.103.refs_0_, bf16[128,1024]{1,0:T(8,128)(2,1)} %get-tuple-element.121.refs_1_, bf16[128,1024]{1,0:T(8,128)(2,1)} %get-tuple-element.122.refs_2_, ...), custom_call_target="tpu_custom_call" | custom-call | tf_op jit(solution)/shard_map/pallas_call | solution.py:104
  161.9 1.5 collective-permute-done.9.refs_0_
  163.4 4.2 %collective-permute-start.12 = (bf16[21,32,128]{2,1,0:T(8,128)(2,1)}, bf16[21,32,128]{2,1,0:T(8,128)(2,1)S(1)}, u32[]{:S(2)}, u32[]{:S(2)}) collective-permute-start(bf16[21,32,128]{2,1,0:T(8,128)(2,1)} %shard_map.291.refs_3_), channel_id=1, source_target_pairs={{0,3},{1,0},{2,1},{3,2},{4,7},{5,4},{6,5},{7,6},{8,11},{9,8},{10,9... | collective-permute-start | bytes 516104 | tf_op jit(solution)/shard_map/ppermute | solution.py:61
  168.9 5.8 %shard_map.292.refs_5_ = f32[128,1536]{1,0:T(8,128)} custom-call(s32[3]{0:T(128)} %pad_add_fusion.scalars, bf16[128,1536]{1,0:T(8,128)(2,1)} %get-tuple-element.129.refs_8_.gq.refs_4_, bf16[1536,1536]{1,0:T(8,128)(2,1)} %query_w.1), custom_call_target="tpu_custom_call" | custom-call | tf_op jit(solution)/shard_map/pallas_call | solution.py:104
  174.7 3.9 %shard_map.293 = (f32[8,5,32,192]{3,2,1,0:T(8,128)}, f32[8,5,2,16,64]{4,3,2,1,0:T(8,128)}, f32[8,5,16,64]{3,2,1,0:T(8,128)}, f32[8,5,16,192]{3,2,1,0:T(8,128)}) custom-call(s32[11]{0:T(128)} %pad_add_fusion.1.scalars, bf16[8,256,256]{2,1,0:T(8,128)(2,1)} %copy-done), custom_call_target="tpu_custom_call" | custom-call | tf_op jit(solution)/shard_map/pallas_call | solution.py:104
  178.6 1.2 collective-permute-done.11.refs_1_
  179.8 4.1 %collective-permute-start.13 = (bf16[128,1024]{1,0:T(8,128)(2,1)S(1)}, bf16[128,1024]{1,0:T(8,128)(2,1)S(1)}, u32[]{:S(2)}, u32[]{:S(2)}) collective-permute-start(bf16[128,1024]{1,0:T(8,128)(2,1)S(1)} %copy-done.9), channel_id=1, source_target_pairs={{0,2},{1,3},{2,0},{3,1},{4,6},{5,7},{6,4},{7,5},{8,10},{9,11},{10,... | collective-permute-start | bytes 786440 | tf_op jit(solution)/shard_map/ppermute | solution.py:66
  183.9 4.3 %shard_map.294 = bf16[8,96,256]{2,1,0:T(8,128)(2,1)} custom-call(s32[3]{0:T(128)} %pad_add_fusion.scalars, bf16[21,32,128]{2,1,0:T(8,128)(2,1)} %collective-permute-done.10.refs_0_, bf16[21,32,128]{2,1,0:T(8,128)(2,1)} %copy-done.11, bf16[21,32,128]{2,1,0:T(8,128)(2,1)} %copy-done.10, bf16[21,32,128]{2,1,0:T(8,128)(2,1)} %shard_map.291.refs_3_, ...), custom_call_target="tpu_custom_call" | custom-call | tf_op jit(solution)/shard_map/pallas_call | solution.py:104
  188.1 3.5 %all-to-all-start.1 = ((bf16[8,96,256]{2,1,0:T(8,128)(2,1)}), bf16[8,96,256]{2,1,0:T(8,128)(2,1)S(1)}, u32[]{:S(2)}, u32[]{:S(2)}) async-start(bf16[8,96,256]{2,1,0:T(8,128)(2,1)} %shard_map.294), calls=%async_computation.1 | async-start | bytes 786432 | tf_op jit(solution)/shard_map/all_to_all | solution.py:1002
  191.6 8.6 %collective-permute-done.13.refs_1_ = bf16[128,1024]{1,0:T(8,128)(2,1)S(1)} collective-permute-done((bf16[128,1024]{1,0:T(8,128)(2,1)S(1)}, bf16[128,1024]{1,0:T(8,128)(2,1)S(1)}, u32[]{:S(2)}, u32[]{:S(2)}) %collective-permute-start.13) | collective-permute-done | bytes 262176 | tf_op jit(solution)/shard_map/ppermute | solution.py:66
  201.1 6.1 %shard_map.295 = f32[128,1536]{1,0:T(8,128)} custom-call(s32[3]{0:T(128)} %pad_add_fusion.scalars, bf16[128,1024]{1,0:T(8,128)(2,1)} %copy-done.17, bf16[128,1024]{1,0:T(8,128)(2,1)} %copy-done.18, bf16[128,1024]{1,0:T(8,128)(2,1)} %copy-done.19, bf16[128,1024]{1,0:T(8,128)(2,1)} %get-tuple-element.107.refs_3_, ...), custom_call_target="tpu_custom_call" | custom-call | flops 20000000000 | tf_op jit(solution)/shard_map/pallas_call | solution.py:104
  208.0 2.7 %shard_map.296 = (f32[8,48,192]{2,1,0:T(8,128)}, f32[8,16,192]{2,1,0:T(8,128)}, f32[8,2,16,64]{3,2,1,0:T(8,128)}, f32[8,16,192]{2,1,0:T(8,128)}, f32[8,16,192]{2,1,0:T(8,128)}) custom-call(s32[11]{0:T(128)} %pad_add_fusion.1.scalars, bf16[8,96,256]{2,1,0:T(8,128)(2,1)} %copy-done.2), custom_call_target="tpu_custom_call" | custom-call | tf_op jit(solution)/shard_map/pallas_call | solution.py:104
  (73 shorter events, 10.0 us)
Async XLA Ops:
  0.6 11.2 %copy-start.7 = (bf16[1,128,1536]{2,1,0:T(8,128)(2,1)S(1)}, bf16[1,128,1536]{2,1,0:T(8,128)(2,1)}, u32[]{:S(2)}) copy-start(bf16[1,128,1536]{2,1,0:T(8,128)(2,1)} %param.43) | copy-start | bytes 1179652
  0.7 14.4 %collective-permute-start = (bf16[128,1536]{1,0:T(8,128)(2,1)}, bf16[128,1536]{1,0:T(8,128)(2,1)S(1)}, u32[]{:S(2)}, u32[]{:S(2)}) collective-permute-start(bf16[128,1536]{1,0:T(8,128)(2,1)} %bitcast.30), channel_id=1, source_target_pairs={{0,1},{1,2},{2,3},{3,0},{4,5},{5,6},{6,7},{7,4},{8,9},{9,10},{10,1... | collective-permute-start | bytes 1179656 | tf_op jit(solution)/shard_map/ppermute | solution.py:936
  6.5 9.9 %copy-start.12 = (f32[1536]{0:T(1024)S(1)}, f32[1536]{0:T(1024)}, u32[]{:S(2)}) copy-start(f32[1536]{0:T(1024)} %param.26) | copy-start | bytes 18436
  6.5 10.5 %copy-start.13 = (f32[1536]{0:T(1024)S(1)}, f32[1536]{0:T(1024)}, u32[]{:S(2)}) copy-start(f32[1536]{0:T(1024)} %param.27) | copy-start | bytes 18436
  11.9 60.7 %copy-start.1 = (bf16[128,1664]{1,0:T(8,128)(2,1)}, bf16[128,1664]{1,0:T(8,128)(2,1)S(1)}, u32[]{:S(2)}) copy-start(bf16[128,1664]{1,0:T(8,128)(2,1)S(1)} %pad_maximum_fusion.refs_1_.refs_17_) | copy-start | bytes 1277956
  15.1 12.2 %copy-start.6 = (bf16[128,1536]{1,0:T(8,128)(2,1)}, bf16[128,1536]{1,0:T(8,128)(2,1)S(1)}, u32[]{:S(2)}) copy-start(bf16[128,1536]{1,0:T(8,128)(2,1)S(1)} %collective-permute-done.refs_1_.refs_0_) | copy-start | bytes 1179652
  15.1 12.2 %collective-permute-start.1 = (bf16[128,1536]{1,0:T(8,128)(2,1)S(1)}, bf16[128,1536]{1,0:T(8,128)(2,1)}, u32[]{:S(2)}, u32[]{:S(2)}) collective-permute-start(bf16[128,1536]{1,0:T(8,128)(2,1)S(1)} %collective-permute-done.refs_1_.refs_0_), channel_id=1, source_target_pairs={{0,1},{1,2},{2,3},{3,0},{4,5},{5,6},{6,7},{7,4},{8,9},{9,10},{10,1... | collective-permute-start | bytes 1179656 | tf_op jit(solution)/shard_map/ppermute | solution.py:937
  27.3 16.7 %collective-permute-start.4 = (bf16[128,1536]{1,0:T(8,128)(2,1)}, bf16[128,1536]{1,0:T(8,128)(2,1)}, u32[]{:S(2)}, u32[]{:S(2)}) collective-permute-start(bf16[128,1536]{1,0:T(8,128)(2,1)} %collective-permute-done.1.refs_2_.refs_1_), channel_id=1, source_target_pairs={{0,1},{1,2},{2,3},{3,0},{4,5},{5,6},{6,7},{7,4},{8,9},{9,10},{10,1... | collective-permute-start | bytes 1179656 | tf_op jit(solution)/shard_map/ppermute | solution.py:939
  39.6 33.2 %collective-permute-start.3 = (bf16[128,1664]{1,0:T(8,128)(2,1)S(1)}, bf16[128,1664]{1,0:T(8,128)(2,1)S(1)}, u32[]{:S(2)}, u32[]{:S(2)}) collective-permute-start(bf16[128,1664]{1,0:T(8,128)(2,1)S(1)} %pad_maximum_fusion.refs_1_.refs_17_), channel_id=1, source_target_pairs={{0,2},{1,3},{2,0},{3,1},{4,6},{5,7},{6,4},{7,5},{8,10},{9,11},{10,... | collective-permute-start | bytes 1277960 | tf_op jit(solution)/shard_map/ppermute | solution.py:60
  39.8 33.0 %collective-permute-start.2 = (bf16[128,1664]{1,0:T(8,128)(2,1)S(1)}, bf16[128,1664]{1,0:T(8,128)(2,1)S(1)}, u32[]{:S(2)}, u32[]{:S(2)}) collective-permute-start(bf16[128,1664]{1,0:T(8,128)(2,1)S(1)} %pad_maximum_fusion.refs_1_.refs_17_), channel_id=1, source_target_pairs={{0,1},{1,2},{2,3},{3,0},{4,5},{5,6},{6,7},{7,4},{8,9},{9,10},{10,1... | collective-permute-start | bytes 1277960 | tf_op jit(solution)/shard_map/ppermute | solution.py:60
  72.5 29.4 %collective-permute-start.7 = (bf16[128,1664]{1,0:T(8,128)(2,1)S(1)}, bf16[128,1664]{1,0:T(8,128)(2,1)S(1)}, u32[]{:S(2)}, u32[]{:S(2)}) collective-permute-start(bf16[128,1664]{1,0:T(8,128)(2,1)S(1)} %pad_maximum_fusion.refs_1_.refs_17_), channel_id=1, source_target_pairs={{0,3},{1,0},{2,1},{3,2},{4,7},{5,4},{6,5},{7,6},{8,11},{9,8},{10,9... | collective-permute-start | bytes 1277960 | tf_op jit(solution)/shard_map/ppermute | solution.py:60
  72.8 0.8 copy-start.3
  72.8 0.9 copy-start.4
  98.4 29.6 %collective-permute-start.5 = (bf16[128,1664]{1,0:T(8,128)(2,1)}, bf16[128,1664]{1,0:T(8,128)(2,1)S(1)}, u32[]{:S(2)}, u32[]{:S(2)}) collective-permute-start(bf16[128,1664]{1,0:T(8,128)(2,1)} %get-tuple-element.91), channel_id=1, source_target_pairs={{0,3},{1,0},{2,1},{3,2},{4,7},{5,4},{6,5},{7,6},{8,11},{9,8},{10,9... | collective-permute-start | bytes 1277960 | tf_op jit(solution)/shard_map/ppermute | solution.py:66
  99.9 28.1 %collective-permute-start.6 = (bf16[128,1664]{1,0:T(8,128)(2,1)}, bf16[128,1664]{1,0:T(8,128)(2,1)S(1)}, u32[]{:S(2)}, u32[]{:S(2)}) collective-permute-start(bf16[128,1664]{1,0:T(8,128)(2,1)} %get-tuple-element.92), channel_id=1, source_target_pairs={{0,2},{1,3},{2,0},{3,1},{4,6},{5,7},{6,4},{7,5},{8,10},{9,11},{10,... | collective-permute-start | bytes 1277960 | tf_op jit(solution)/shard_map/ppermute | solution.py:66
  128.0 0.9 copy-start.15
  128.0 11.6 %collective-permute-start.8 = (bf16[128,1664]{1,0:T(8,128)(2,1)}, bf16[128,1664]{1,0:T(8,128)(2,1)S(1)}, u32[]{:S(2)}, u32[]{:S(2)}) collective-permute-start(bf16[128,1664]{1,0:T(8,128)(2,1)} %get-tuple-element.98), channel_id=1, source_target_pairs={{0,1},{1,2},{2,3},{3,0},{4,5},{5,6},{6,7},{7,4},{8,9},{9,10},{10,1... | collective-permute-start | bytes 1277960 | tf_op jit(solution)/shard_map/ppermute | solution.py:66
  128.9 29.3 %all-to-all-start = ((bf16[8,256,256]{2,1,0:T(8,128)(2,1)}), bf16[8,256,256]{2,1,0:T(8,128)(2,1)S(1)}, u32[]{:S(2)}, u32[]{:S(2)}) async-start(bf16[8,256,256]{2,1,0:T(8,128)(2,1)} %get-tuple-element.112), calls=%async_computation | async-start | bytes 2097152 | tf_op jit(solution)/shard_map/all_to_all | solution.py:984
  156.3 7.0 %collective-permute-start.9 = (bf16[128,1024]{1,0:T(8,128)(2,1)}, bf16[128,1024]{1,0:T(8,128)(2,1)S(1)}, u32[]{:S(2)}, u32[]{:S(2)}) collective-permute-start(bf16[128,1024]{1,0:T(8,128)(2,1)} %get-tuple-element.103.refs_0_), channel_id=1, source_target_pairs={{0,3},{1,0},{2,1},{3,2},{4,7},{5,4},{6,5},{7,6},{8,11},{9,8},{10,9... | collective-permute-start | bytes 786440 | tf_op jit(solution)/shard_map/ppermute | solution.py:66
  158.1 16.6 %copy-start = (bf16[8,256,256]{2,1,0:T(8,128)(2,1)}, bf16[8,256,256]{2,1,0:T(8,128)(2,1)S(1)}, u32[]{:S(2)}) copy-start(bf16[8,256,256]{2,1,0:T(8,128)(2,1)S(1)} %all-to-all-done.got) | copy-start | bytes 3145732
  163.4 4.2 %copy-start.17 = (bf16[128,1024]{1,0:T(8,128)(2,1)}, bf16[128,1024]{1,0:T(8,128)(2,1)S(1)}, u32[]{:S(2)}) copy-start(bf16[128,1024]{1,0:T(8,128)(2,1)S(1)} %collective-permute-done.9.refs_0_) | copy-start | bytes 786436
  163.4 15.2 %collective-permute-start.12 = (bf16[21,32,128]{2,1,0:T(8,128)(2,1)}, bf16[21,32,128]{2,1,0:T(8,128)(2,1)S(1)}, u32[]{:S(2)}, u32[]{:S(2)}) collective-permute-start(bf16[21,32,128]{2,1,0:T(8,128)(2,1)} %shard_map.291.refs_3_), channel_id=1, source_target_pairs={{0,3},{1,0},{2,1},{3,2},{4,7},{5,4},{6,5},{7,6},{8,11},{9,8},{10,9... | collective-permute-start | bytes 516104 | tf_op jit(solution)/shard_map/ppermute | solution.py:61
  167.5 12.2 %collective-permute-start.11 = (bf16[21,32,128]{2,1,0:T(8,128)(2,1)}, bf16[21,32,128]{2,1,0:T(8,128)(2,1)S(1)}, u32[]{:S(2)}, u32[]{:S(2)}) collective-permute-start(bf16[21,32,128]{2,1,0:T(8,128)(2,1)} %shard_map.291.refs_3_), channel_id=1, source_target_pairs={{0,2},{1,3},{2,0},{3,1},{4,6},{5,7},{6,4},{7,5},{8,10},{9,11},{10,... | collective-permute-start | bytes 516104 | tf_op jit(solution)/shard_map/ppermute | solution.py:61
  167.5 12.2 %collective-permute-start.10 = (bf16[21,32,128]{2,1,0:T(8,128)(2,1)}, bf16[21,32,128]{2,1,0:T(8,128)(2,1)}, u32[]{:S(2)}, u32[]{:S(2)}) collective-permute-start(bf16[21,32,128]{2,1,0:T(8,128)(2,1)} %shard_map.291.refs_3_), channel_id=1, source_target_pairs={{0,1},{1,2},{2,3},{3,0},{4,5},{5,6},{6,7},{7,4},{8,9},{9,10},{10,1... | collective-permute-start | bytes 516104 | tf_op jit(solution)/shard_map/ppermute | solution.py:61
  168.9 10.8 %copy-start.9 = (bf16[128,1024]{1,0:T(8,128)(2,1)S(1)}, bf16[128,1024]{1,0:T(8,128)(2,1)}, u32[]{:S(2)}) copy-start(bf16[128,1024]{1,0:T(8,128)(2,1)} %get-tuple-element.121.refs_1_) | copy-start | bytes 786436
  168.9 14.9 %copy-start.8 = (bf16[128,1024]{1,0:T(8,128)(2,1)S(1)}, bf16[128,1024]{1,0:T(8,128)(2,1)}, u32[]{:S(2)}) copy-start(bf16[128,1024]{1,0:T(8,128)(2,1)} %get-tuple-element.122.refs_2_) | copy-start | bytes 786436
  178.6 5.3 %copy-start.10 = (bf16[21,32,128]{2,1,0:T(8,128)(2,1)}, bf16[21,32,128]{2,1,0:T(8,128)(2,1)S(1)}, u32[]{:S(2)}) copy-start(bf16[21,32,128]{2,1,0:T(8,128)(2,1)S(1)} %collective-permute-done.12.refs_2_) | copy-start | bytes 516100
  179.7 4.1 %copy-start.11 = (bf16[21,32,128]{2,1,0:T(8,128)(2,1)}, bf16[21,32,128]{2,1,0:T(8,128)(2,1)S(1)}, u32[]{:S(2)}) copy-start(bf16[21,32,128]{2,1,0:T(8,128)(2,1)S(1)} %collective-permute-done.11.refs_1_) | copy-start | bytes 516100
  179.8 20.5 %collective-permute-start.13 = (bf16[128,1024]{1,0:T(8,128)(2,1)S(1)}, bf16[128,1024]{1,0:T(8,128)(2,1)S(1)}, u32[]{:S(2)}, u32[]{:S(2)}) collective-permute-start(bf16[128,1024]{1,0:T(8,128)(2,1)S(1)} %copy-done.9), channel_id=1, source_target_pairs={{0,2},{1,3},{2,0},{3,1},{4,6},{5,7},{6,4},{7,5},{8,10},{9,11},{10,... | collective-permute-start | bytes 786440 | tf_op jit(solution)/shard_map/ppermute | solution.py:66
  183.9 16.4 %collective-permute-start.14 = (bf16[128,1024]{1,0:T(8,128)(2,1)S(1)}, bf16[128,1024]{1,0:T(8,128)(2,1)S(1)}, u32[]{:S(2)}, u32[]{:S(2)}) collective-permute-start(bf16[128,1024]{1,0:T(8,128)(2,1)S(1)} %copy-done.8), channel_id=1, source_target_pairs={{0,1},{1,2},{2,3},{3,0},{4,5},{5,6},{6,7},{7,4},{8,9},{9,10},{10,1... | collective-permute-start | bytes 786440 | tf_op jit(solution)/shard_map/ppermute | solution.py:66
  188.1 19.1 %all-to-all-start.1 = ((bf16[8,96,256]{2,1,0:T(8,128)(2,1)}), bf16[8,96,256]{2,1,0:T(8,128)(2,1)S(1)}, u32[]{:S(2)}, u32[]{:S(2)}) async-start(bf16[8,96,256]{2,1,0:T(8,128)(2,1)} %shard_map.294), calls=%async_computation.1 | async-start | bytes 786432 | tf_op jit(solution)/shard_map/all_to_all | solution.py:1002
  200.3 0.8 copy-start.19
  (5 other events, 3.7 us)
